TPU v7x, 128 devices: a whole 4x4x4 slice. The times are simulated.
128 devices in a mesh: dp: 8 (over x, y_hi), seq: 16 (over z, y_lo, core).
Axes of the slice: x: 4, y: 4 (y_hi: 2, y_lo: 2; y = y_hi * 2 + y_lo), z: 4, core: 2. Of those that a mesh axis runs over, the one named last changes fastest.
Arguments:
- queries: bfloat16 [8, 4096, 2048], P('dp', 'seq'), may hold values from -32 to 32, as said below
- key_rows: bfloat16 [8, 4096, 2048], P('dp', 'seq'), may hold values from -32 to 32, as said below
- value_rows: bfloat16 [8, 4096, 2048], P('dp', 'seq'), may hold values from -6 to 6
- cotangent: bfloat16 [8, 4096, 1536], P('dp', 'seq'), may hold values from -6 to 6
- attn_gate: float32 [8, 1536], P('dp'), may hold values from -4 to 4
- lengths: int32 [8], P('dp'), may hold values from 1024 to 4096, as said below
- w_out: bfloat16 [2048, 1536], P('seq'), may hold values from -0.125 to 0.125
- row_moment: float32 [2048], P('seq'), may hold values from 1 to 30
- col_moment: float32 [1536], P('dp'), may hold values from 1 to 30
Outputs:
- grad_queries: bfloat16 [8, 4096, 2048], P('dp', 'seq')
- grad_keys: bfloat16 [8, 4096, 2048], P('dp', 'seq')
- grad_values: bfloat16 [8, 4096, 2048], P('dp', 'seq')
- grad_gate: float32 [8, 1536], P('dp')
- grad_weight: float32 [2048, 1536], P('seq', 'dp')
- row_new: float32 [2048], P('seq')
- col_new: float32 [1536], P('dp')
Inputs may be any that keep to these rules, and one draw needn't show every extreme that they name: `lengths`: token slots at or beyond a sample's length are padding; some sample fills all 4096 slots. `queries`: query features. `key_rows`: key features.
All inputs are finite; a program needn't handle non-finite values.
Results may differ from a plain program's by a relative error of at most 0.019.
Values may be sent and summed in bfloat16 or wider, within the bound.
No kernel may reach another device: no remote copies, remote signals or barrier semaphores. Data moves between devices by JAX's collectives and lax.ppermute only.
A program may use at most 128 MiB of HBM per device.

v0:
```python
import math

import jax
import jax.numpy as jnp
from jax import lax
from jax.sharding import PartitionSpec as P

HEAD_DIM = 128


epsilon = 1e-30


def head_pass(query_rows, key_part, value_part, grad_rows, valid_len):
    seq_total = query_rows.shape[0]
    head_width = query_rows.shape[1]
    block_rows = min(512, seq_total)
    block_count = seq_total // block_rows
    score_scale = 1.0 / math.sqrt(HEAD_DIM)
    live_keys = jnp.arange(seq_total) < valid_len

    def one_block(step_index, carry):
        grad_q, grad_k, grad_v, attended = carry
        first = step_index * block_rows
        rows_q = lax.dynamic_slice_in_dim(query_rows, first, block_rows, 0)
        rows_g = lax.dynamic_slice_in_dim(grad_rows, first, block_rows, 0)
        live_rows = first + jnp.arange(block_rows) < valid_len
        scores = (
            jnp.einsum("qd,kd->qk", rows_q, key_part, preferred_element_type=jnp.float32)
            * score_scale
        )
        scores = jnp.where(live_keys[None, :], scores, -1e30)
        row_top = jnp.max(scores, axis=1, keepdims=True)
        exponent = jnp.exp(scores - row_top)
        probs = exponent / jnp.sum(exponent, axis=1, keepdims=True)
        probs = jnp.where(live_rows[:, None], probs, jnp.zeros_like(probs))
        probs_low = probs.astype(jnp.bfloat16)
        out_rows = jnp.dot(probs_low, value_part, preferred_element_type=jnp.float32).astype(
            jnp.bfloat16
        )
        delta = jnp.sum(
            rows_g.astype(jnp.float32) * out_rows.astype(jnp.float32), axis=1, keepdims=True
        )
        dprob = jnp.einsum("qd,kd->qk", rows_g, value_part, preferred_element_type=jnp.float32)
        dscore = (probs * (dprob - delta) * score_scale).astype(jnp.bfloat16)
        dq_rows = jnp.dot(dscore, key_part, preferred_element_type=jnp.float32).astype(jnp.bfloat16)
        grad_k = grad_k + jnp.einsum(
            "qk,qd->kd", dscore, rows_q, preferred_element_type=jnp.float32
        )
        grad_v = grad_v + jnp.einsum(
            "qk,qd->kd", probs_low, rows_g, preferred_element_type=jnp.float32
        )
        grad_q = lax.dynamic_update_slice_in_dim(grad_q, dq_rows, first, 0)
        attended = lax.dynamic_update_slice_in_dim(attended, out_rows, first, 0)
        return (grad_q, grad_k, grad_v, attended)

    start_state = (
        jnp.zeros((seq_total, head_width), jnp.bfloat16),
        jnp.zeros((seq_total, head_width), jnp.float32),
        jnp.zeros((seq_total, head_width), jnp.float32),
        jnp.zeros((seq_total, head_width), jnp.bfloat16),
    )
    grad_q, grad_k, grad_v, attended = lax.fori_loop(0, block_count, one_block, start_state)
    return (grad_q, grad_k.astype(jnp.bfloat16), grad_v.astype(jnp.bfloat16), attended)


def moments(grad_block, row_moment, col_moment, inner_dim, width_dim):
    squares = grad_block * grad_block + epsilon
    row_total = lax.psum(jnp.sum(squares, axis=1), "dp")
    col_total = lax.psum(jnp.sum(squares, axis=0), "seq")
    row_new = 0.8 * row_moment + 0.2 * (row_total / width_dim)
    col_new = 0.8 * col_moment + 0.2 * (col_total / inner_dim)
    return (row_new, col_new)


def shards(
    queries, key_rows, value_rows, cotangent, attn_gate, lengths, w_out, row_moment, col_moment
):
    tok_rows = queries.shape[1]
    inner_dim = queries.shape[2]
    width_dim = cotangent.shape[2]
    head_total = inner_dim // HEAD_DIM
    valid_len = lengths[0]
    shape_four = (1, tok_rows, head_total, HEAD_DIM)
    out_shape = (1, tok_rows, inner_dim)
    scaled = (attn_gate[0][None, :] * cotangent[0].astype(jnp.float32)).astype(jnp.bfloat16)
    full_weight = lax.all_gather(w_out, "seq", axis=0, tiled=True)
    out_grad = jnp.einsum(
        "td,rd->tr", scaled, full_weight, preferred_element_type=jnp.float32
    ).astype(jnp.bfloat16)
    head_q, head_k, head_v, head_g = (
        lax.all_to_all(queries.reshape(shape_four), "seq", split_axis=2, concat_axis=1, tiled=True),
        lax.all_to_all(
            key_rows.reshape(shape_four), "seq", split_axis=2, concat_axis=1, tiled=True
        ),
        lax.all_to_all(
            value_rows.reshape(shape_four), "seq", split_axis=2, concat_axis=1, tiled=True
        ),
        lax.all_to_all(
            out_grad.reshape(shape_four), "seq", split_axis=2, concat_axis=1, tiled=True
        ),
    )
    results = [
        head_pass(head_q[0, :, 0], head_k[0, :, 0], head_v[0, :, 0], head_g[0, :, 0], valid_len)
    ]
    stacked = [
        jnp.stack([result[member] for result in results], axis=1)[None] for member in range(4)
    ]
    back_q, back_k, back_v, back_out = (
        lax.all_to_all(stacked[0], "seq", split_axis=1, concat_axis=2, tiled=True),
        lax.all_to_all(stacked[1], "seq", split_axis=1, concat_axis=2, tiled=True),
        lax.all_to_all(stacked[2], "seq", split_axis=1, concat_axis=2, tiled=True),
        lax.all_to_all(stacked[3], "seq", split_axis=1, concat_axis=2, tiled=True),
    )
    attended = back_out.reshape(tok_rows, inner_dim)
    mixed = jnp.dot(attended, full_weight, preferred_element_type=jnp.float32)
    gate_part = jnp.sum(cotangent[0].astype(jnp.float32) * mixed, axis=0)[None, :]
    row_part = lax.psum_scatter(
        jnp.einsum("tr,td->rd", attended, scaled, preferred_element_type=jnp.float32).astype(
            jnp.bfloat16
        ),
        "seq",
        scatter_dimension=0,
        tiled=True,
    )
    grad_weight = lax.psum_scatter(row_part, "dp", scatter_dimension=1, tiled=True).astype(
        jnp.float32
    )
    grad_gate = lax.psum(gate_part, "seq")
    row_new, col_new = moments(grad_weight, row_moment, col_moment, inner_dim, width_dim)
    return (
        back_q.reshape(out_shape),
        back_k.reshape(out_shape),
        back_v.reshape(out_shape),
        grad_gate,
        grad_weight,
        row_new,
        col_new,
    )


def solution(mesh):
    placed = (
        P("dp", "seq", None),
        P("dp", "seq", None),
        P("dp", "seq", None),
        P("dp", "seq", None),
        P("dp", None),
        P("dp"),
        P("seq", None),
        P("seq"),
        P("dp"),
    )
    return jax.shard_map(
        shards,
        mesh=mesh,
        in_specs=placed,
        out_specs=(
            P("dp", "seq", None),
            P("dp", "seq", None),
            P("dp", "seq", None),
            P("dp", None),
            P("seq", "dp"),
            P("seq"),
            P("dp"),
        ),
        check_vma=False,
    )
```

profile of v0, /device:TPU:0, one launch (start us, length us, event | category | flops | bytes accessed | tf_op | source)
XLA Modules:
  0.0 707.2 jit_solution(13070510084518225628)
XLA Ops:
  10.7 6.5 all-to-all-start.3
  19.1 23.1 %all-to-all-done.3 = bf16[1,256,16,128]{3,1,0,2:T(8,128)(2,1)S(1)} async-done(((bf16[1,256,16,128]{3,1,0,2:T(8,128)(2,1)}), bf16[1,256,16,128]{3,1,0,2:T(8,128)(2,1)S(1)}, u32[]{:S(2)}, u32[]{:S(2)}) %all-to-all-start.3) | async-done | bytes 1048608 | tf_op jit(solution)/shard_map/all_to_all | solution.py:96
  48.7 23.4 %all-to-all-done = bf16[1,256,16,128]{3,1,0,2:T(8,128)(2,1)S(1)} async-done(((bf16[1,256,16,128]{3,1,0,2:T(8,128)(2,1)}), bf16[1,256,16,128]{3,1,0,2:T(8,128)(2,1)S(1)}, u32[]{:S(2)}, u32[]{:S(2)}) %all-to-all-start) | async-done | bytes 1048608 | tf_op jit(solution)/shard_map/all_to_all | solution.py:92
  83.7 9.6 %all-to-all-done.1 = bf16[1,256,16,128]{3,1,0,2:T(8,128)(2,1)S(1)} async-done(((bf16[1,256,16,128]{3,1,0,2:T(8,128)(2,1)}), bf16[1,256,16,128]{3,1,0,2:T(8,128)(2,1)S(1)}, u32[]{:S(2)}, u32[]{:S(2)}) %all-to-all-start.1) | async-done | bytes 1048608 | tf_op jit(solution)/shard_map/all_to_all | solution.py:93
  97.9 16.4 %all-to-all-done.2 = bf16[1,256,16,128]{3,1,0,2:T(8,128)(2,1)} async-done(((bf16[1,256,16,128]{3,1,0,2:T(8,128)(2,1)}), bf16[1,256,16,128]{3,1,0,2:T(8,128)(2,1)}, u32[]{:S(2)}, u32[]{:S(2)}) %all-to-all-start.2) | async-done | bytes 1048608 | tf_op jit(solution)/shard_map/all_to_all | solution.py:99
  116.4 271.2 %while.22 = (s32[]{:T(128)}, bf16[4096,128]{1,0:T(8,128)(2,1)}, f32[4096,128]{1,0:T(8,128)}, f32[4096,128]{1,0:T(8,128)S(1)}, bf16[4096,128]{0,1:T(8,128)(2,1)},...) while((s32[]{:T(128)}, bf16[4096,128]{1,0:T(8,128)(2,1)}, ...), condition=%wide.region_4.5_spmd.clone.clone.clone, body=%wide.region_0.4_spmd.clone.clone.clone.sunk | while | flops 3261468160 | bytes 148536640 | solution.py:63
  128.6 5.1 multiply_reduce_fusion.2
  161.9 5.1 multiply_reduce_fusion.2
  170.9 5.6 convolution_add_fusion.4
  195.9 5.1 multiply_reduce_fusion.2
  204.9 5.6 convolution_add_fusion.4
  238.9 5.6 convolution_add_fusion.4
  263.8 5.1 multiply_reduce_fusion.2
  272.9 5.6 convolution_add_fusion.4
  306.9 5.6 convolution_add_fusion.4
  331.8 5.1 multiply_reduce_fusion.2
  340.9 5.6 convolution_add_fusion.4
  365.8 5.1 multiply_reduce_fusion.2
  374.8 5.6 convolution_add_fusion.4
  387.7 5.5 copy.86
  393.7 23.8 %reduce.4 = bf16[4096,128]{1,0:T(8,128)(2,1)S(1)} reduce(bf16[4096,1,1,128]{3,2,1,0:T(2,128)(2,1)} %bitcast.118, bf16[]{:T(256)} %broadcast.78), dimensions={1,2}, to_apply=%bitcast.66.reduce_sub_computation | reduce | bytes 2097154
  418.6 20.1 %all_to_all.120 = bf16[16,2,16384]{2,1,0:T(2,128)(2,1)S(1)} all-to-all(bf16[16,2,16384]{2,1,0:T(2,128)(2,1)} %reshape.76), channel_id=1, replica_groups=mesh['dp'=8,'seq'=16] {'seq'}, dimensions={0} | all-to-all | bytes 2097152 | tf_op jit(solution)/shard_map/all_to_all | solution.py:113
  446.4 5.6 convolution_convert_fusion.1
  454.8 16.7 %copy.105 = bf16[1,4096,1,128]{3,2,0,1:T(2,128)(2,1)S(1)} copy(bf16[1,4096,1,128]{3,1,2,0:T(8,128)(2,1)S(1)} %get-tuple-element.417) | data formatting | bytes 2097152 | tf_op jit(solution)/shard_map/broadcast_in_dim;stack | solution.py:107
  471.5 23.4 %reduce.3 = bf16[4096,128]{1,0:T(8,128)(2,1)} reduce(bf16[4096,1,1,128]{3,2,1,0:T(2,128)(2,1)S(1)} %bitcast.120, bf16[]{:T(256)} %broadcast.78), dimensions={1,2}, to_apply=%bitcast.89.reduce_sub_computation | reduce | bytes 2097154
  504.7 23.4 %reduce.2 = bf16[4096,128]{1,0:T(8,128)(2,1)} reduce(bf16[4096,1,1,128]{3,2,1,0:T(2,128)(2,1)S(1)} %bitcast.121, bf16[]{:T(256)} %broadcast.78), dimensions={1,2}, to_apply=%bitcast.90.reduce_sub_computation | reduce | bytes 2097154
  530.3 5.8 all-to-all-start.5
  539.2 23.4 %reduce.1 = bf16[4096,128]{1,0:T(8,128)(2,1)} reduce(bf16[4096,1,1,128]{3,2,1,0:T(2,128)(2,1)S(1)} %bitcast.119, bf16[]{:T(256)} %broadcast.78), dimensions={1,2}, to_apply=%bitcast.91.reduce_sub_computation | reduce | bytes 2097154
  564.8 5.7 all-to-all-start.4
  596.7 51.1 %reduce-scatter.7.cloned.1.call-done = bf16[192,128]{1,0:T(8,128)(2,1)} async-done(((bf16[1536,128]{1,0:T(8,128)(2,1)}), bf16[192,128]{1,0:T(8,128)(2,1)}) %reduce-scatter.7.cloned.1.call-update) | async-done | bytes 49168
  649.5 21.6 %psum.22 = f32[128]{0:T(128)S(1)} all-reduce(f32[128]{0:T(128)S(1)} %get-tuple-element.390), channel_id=1, replica_groups=mesh['dp'=8,'seq'=16] {'dp'}, use_global_device_ids=true, to_apply=%region_10.11 | all-reduce | flops 128 | bytes 1024 | tf_op jit(solution)/shard_map/psum | solution.py:69
  671.1 28.2 %all-reduce = (f32[1,1536]{1,0:T(1,128)}, f32[192]{0:T(256)S(1)}) all-reduce(f32[1,1536]{1,0:T(1,128)S(1)} %broadcast_in_dim.60, f32[192]{0:T(256)S(1)} %get-tuple-element.389), channel_id=1, replica_groups=mesh['dp'=8,'seq'=16] {'seq'}, use_global_device_ids=true, to_apply=%region_6.7 | all-reduce | flops 1728 | bytes 13824 | tf_op jit(solution)/shard_map/psum | solution.py:129
  (241 shorter events, 289.5 us)
Async XLA Ops:
  7.2 10.1 %copy-start.5 = (bf16[1,256,2048]{2,1,0:T(8,128)(2,1)S(1)}, bf16[1,256,2048]{2,1,0:T(8,128)(2,1)}, u32[]{:S(2)}) copy-start(bf16[1,256,2048]{2,1,0:T(8,128)(2,1)} %param.11) | copy-start | bytes 3145732
  7.2 69.6 %all-gather.2.cloned.1.call-start = ((), (), s32[]{:S(2)}) async-start(), calls=%async_computation.10 | async-start | bytes 6684672 | tf_op jit(solution)/shard_map/all_gather | solution.py:87
  10.7 31.5 %all-to-all-start.3 = ((bf16[1,256,16,128]{3,1,0,2:T(8,128)(2,1)}), bf16[1,256,16,128]{3,1,0,2:T(8,128)(2,1)S(1)}, u32[]{:S(2)}, u32[]{:S(2)}) async-start(bf16[1,256,16,128]{3,1,0,2:T(8,128)(2,1)} %copy.76), calls=%async_computation.3 | async-start | bytes 2097152 | tf_op jit(solution)/shard_map/all_to_all | solution.py:96
  19.1 57.6 %copy-start.8 = (f32[1,1536]{1,0:T(1,128)S(1)}, f32[1,1536]{1,0:T(1,128)}, u32[]{:S(2)}) copy-start(f32[1,1536]{1,0:T(1,128)} %param.15) | copy-start | bytes 18436
  42.2 29.9 %all-to-all-start = ((bf16[1,256,16,128]{3,1,0,2:T(8,128)(2,1)}), bf16[1,256,16,128]{3,1,0,2:T(8,128)(2,1)S(1)}, u32[]{:S(2)}, u32[]{:S(2)}) async-start(bf16[1,256,16,128]{3,1,0,2:T(8,128)(2,1)} %copy.71), calls=%async_computation | async-start | bytes 2097152 | tf_op jit(solution)/shard_map/all_to_all | solution.py:92
  73.1 20.2 %all-to-all-start.1 = ((bf16[1,256,16,128]{3,1,0,2:T(8,128)(2,1)}), bf16[1,256,16,128]{3,1,0,2:T(8,128)(2,1)S(1)}, u32[]{:S(2)}, u32[]{:S(2)}) async-start(bf16[1,256,16,128]{3,1,0,2:T(8,128)(2,1)} %copy.73), calls=%async_computation.1 | async-start | bytes 2097152 | tf_op jit(solution)/shard_map/all_to_all | solution.py:93
  93.3 21.0 %all-to-all-start.2 = ((bf16[1,256,16,128]{3,1,0,2:T(8,128)(2,1)}), bf16[1,256,16,128]{3,1,0,2:T(8,128)(2,1)}, u32[]{:S(2)}, u32[]{:S(2)}) async-start(bf16[1,256,16,128]{3,1,0,2:T(8,128)(2,1)} %copy.74), calls=%async_computation.2 | async-start | bytes 2097152 | tf_op jit(solution)/shard_map/all_to_all | solution.py:99
  97.7 473.2 %reduce-scatter.5.cloned.1.call-start = ((), (), s32[]{:S(2)}) async-start(), calls=%async_computation.11 | async-start | bytes 6684672 | tf_op jit(solution)/shard_map/reduce_scatter | solution.py:118
  137.6 9.1 %slice-start = ((s8[8388608]{0:T(1024)(128)(4,1)}), s8[4194304]{0:T(1024)(128)(4,1)S(1)}, s32[]{:S(2)}) async-start(s8[8388608]{0:T(1024)(128)(4,1)} %bitcast.108), calls=%async_computation.13 | async-start | bytes 8388608 | tf_op jit(solution)/shard_map/while
  137.6 9.1 %slice-start.1 = ((s8[8388608]{0:T(1024)(128)(4,1)}), s8[4194304]{0:T(1024)(128)(4,1)S(1)}, s32[]{:S(2)}) async-start(s8[8388608]{0:T(1024)(128)(4,1)} %bitcast.108), calls=%async_computation.14 | async-start | bytes 8388608 | tf_op jit(solution)/shard_map/while
  170.9 9.8 %slice-start = ((s8[8388608]{0:T(1024)(128)(4,1)}), s8[4194304]{0:T(1024)(128)(4,1)S(1)}, s32[]{:S(2)}) async-start(s8[8388608]{0:T(1024)(128)(4,1)} %bitcast.108), calls=%async_computation.13 | async-start | bytes 8388608 | tf_op jit(solution)/shard_map/while
  170.9 9.8 %slice-start.1 = ((s8[8388608]{0:T(1024)(128)(4,1)}), s8[4194304]{0:T(1024)(128)(4,1)S(1)}, s32[]{:S(2)}) async-start(s8[8388608]{0:T(1024)(128)(4,1)} %bitcast.108), calls=%async_computation.14 | async-start | bytes 8388608 | tf_op jit(solution)/shard_map/while
  204.9 9.8 %slice-start = ((s8[8388608]{0:T(1024)(128)(4,1)}), s8[4194304]{0:T(1024)(128)(4,1)S(1)}, s32[]{:S(2)}) async-start(s8[8388608]{0:T(1024)(128)(4,1)} %bitcast.108), calls=%async_computation.13 | async-start | bytes 8388608 | tf_op jit(solution)/shard_map/while
  204.9 9.8 %slice-start.1 = ((s8[8388608]{0:T(1024)(128)(4,1)}), s8[4194304]{0:T(1024)(128)(4,1)S(1)}, s32[]{:S(2)}) async-start(s8[8388608]{0:T(1024)(128)(4,1)} %bitcast.108), calls=%async_computation.14 | async-start | bytes 8388608 | tf_op jit(solution)/shard_map/while
  238.9 9.8 %slice-start = ((s8[8388608]{0:T(1024)(128)(4,1)}), s8[4194304]{0:T(1024)(128)(4,1)S(1)}, s32[]{:S(2)}) async-start(s8[8388608]{0:T(1024)(128)(4,1)} %bitcast.108), calls=%async_computation.13 | async-start | bytes 8388608 | tf_op jit(solution)/shard_map/while
  238.9 9.8 %slice-start.1 = ((s8[8388608]{0:T(1024)(128)(4,1)}), s8[4194304]{0:T(1024)(128)(4,1)S(1)}, s32[]{:S(2)}) async-start(s8[8388608]{0:T(1024)(128)(4,1)} %bitcast.108), calls=%async_computation.14 | async-start | bytes 8388608 | tf_op jit(solution)/shard_map/while
  272.9 9.8 %slice-start = ((s8[8388608]{0:T(1024)(128)(4,1)}), s8[4194304]{0:T(1024)(128)(4,1)S(1)}, s32[]{:S(2)}) async-start(s8[8388608]{0:T(1024)(128)(4,1)} %bitcast.108), calls=%async_computation.13 | async-start | bytes 8388608 | tf_op jit(solution)/shard_map/while
  272.9 9.8 %slice-start.1 = ((s8[8388608]{0:T(1024)(128)(4,1)}), s8[4194304]{0:T(1024)(128)(4,1)S(1)}, s32[]{:S(2)}) async-start(s8[8388608]{0:T(1024)(128)(4,1)} %bitcast.108), calls=%async_computation.14 | async-start | bytes 8388608 | tf_op jit(solution)/shard_map/while
  306.9 9.8 %slice-start = ((s8[8388608]{0:T(1024)(128)(4,1)}), s8[4194304]{0:T(1024)(128)(4,1)S(1)}, s32[]{:S(2)}) async-start(s8[8388608]{0:T(1024)(128)(4,1)} %bitcast.108), calls=%async_computation.13 | async-start | bytes 8388608 | tf_op jit(solution)/shard_map/while
  306.9 9.8 %slice-start.1 = ((s8[8388608]{0:T(1024)(128)(4,1)}), s8[4194304]{0:T(1024)(128)(4,1)S(1)}, s32[]{:S(2)}) async-start(s8[8388608]{0:T(1024)(128)(4,1)} %bitcast.108), calls=%async_computation.14 | async-start | bytes 8388608 | tf_op jit(solution)/shard_map/while
  340.9 9.8 %slice-start = ((s8[8388608]{0:T(1024)(128)(4,1)}), s8[4194304]{0:T(1024)(128)(4,1)S(1)}, s32[]{:S(2)}) async-start(s8[8388608]{0:T(1024)(128)(4,1)} %bitcast.108), calls=%async_computation.13 | async-start | bytes 8388608 | tf_op jit(solution)/shard_map/while
  340.9 9.8 %slice-start.1 = ((s8[8388608]{0:T(1024)(128)(4,1)}), s8[4194304]{0:T(1024)(128)(4,1)S(1)}, s32[]{:S(2)}) async-start(s8[8388608]{0:T(1024)(128)(4,1)} %bitcast.108), calls=%async_computation.14 | async-start | bytes 8388608 | tf_op jit(solution)/shard_map/while
  374.8 9.8 %slice-start = ((s8[8388608]{0:T(1024)(128)(4,1)}), s8[4194304]{0:T(1024)(128)(4,1)S(1)}, s32[]{:S(2)}) async-start(s8[8388608]{0:T(1024)(128)(4,1)} %bitcast.108), calls=%async_computation.13 | async-start | bytes 8388608 | tf_op jit(solution)/shard_map/while
  374.8 9.8 %slice-start.1 = ((s8[8388608]{0:T(1024)(128)(4,1)}), s8[4194304]{0:T(1024)(128)(4,1)S(1)}, s32[]{:S(2)}) async-start(s8[8388608]{0:T(1024)(128)(4,1)} %bitcast.108), calls=%async_computation.14 | async-start | bytes 8388608 | tf_op jit(solution)/shard_map/while
  438.7 7.6 %copy-start.7 = (f32[1536]{0:T(1024)S(1)}, f32[1536]{0:T(1024)}, u32[]{:S(2)}) copy-start(f32[1536]{0:T(1024)} %copy-done.6) | copy-start | bytes 18436
  497.0 33.2 %all-to-all-start.6 = ((bf16[16,2,16384]{2,1,0:T(2,128)(2,1)}), bf16[16,2,16384]{2,1,0:T(2,128)(2,1)}, u32[]{:S(2)}, u32[]{:S(2)}) async-start(bf16[16,2,16384]{2,1,0:T(2,128)(2,1)} %reshape.82), calls=%async_computation.6 | async-start | bytes 2097152 | tf_op jit(solution)/shard_map/all_to_all | solution.py:112
  530.3 34.6 %all-to-all-start.5 = ((bf16[16,2,16384]{2,1,0:T(2,128)(2,1)}), bf16[16,2,16384]{2,1,0:T(2,128)(2,1)}, u32[]{:S(2)}, u32[]{:S(2)}) async-start(bf16[16,2,16384]{2,1,0:T(2,128)(2,1)} %reshape.80), calls=%async_computation.5 | async-start | bytes 2097152 | tf_op jit(solution)/shard_map/all_to_all | solution.py:111
  562.6 10.1 %copy-start.4 = (bf16[1,256,1536]{2,1,0:T(8,128)(2,1)S(1)}, bf16[1,256,1536]{2,1,0:T(8,128)(2,1)}, u32[]{:S(2)}) copy-start(bf16[1,256,1536]{2,1,0:T(8,128)(2,1)} %param.14) | copy-start | bytes 2359300
  564.8 25.4 %all-to-all-start.4 = ((bf16[16,2,16384]{2,1,0:T(2,128)(2,1)}), bf16[16,2,16384]{2,1,0:T(2,128)(2,1)}, u32[]{:S(2)}, u32[]{:S(2)}) async-start(bf16[16,2,16384]{2,1,0:T(2,128)(2,1)} %reshape.78), calls=%async_computation.4 | async-start | bytes 2097152 | tf_op jit(solution)/shard_map/all_to_all | solution.py:110
  570.5 77.2 %reduce-scatter.7.cloned.1.call-start = ((), (), s32[]{:S(2)}) async-start(), calls=%async_computation.12 | async-start | bytes 442368
  594.6 104.8 %copy-start.9 = (f32[192]{0:T(256)S(1)}, f32[192]{0:T(256)}, u32[]{:S(2)}) copy-start(f32[192]{0:T(256)} %param.19) | copy-start | bytes 2308
  594.6 105.3 %copy-start.10 = (f32[128]{0:T(128)S(1)}, f32[128]{0:T(128)}, u32[]{:S(2)}) copy-start(f32[128]{0:T(128)} %param.18) | copy-start | bytes 1540
  (19 other events, 96.8 us)
Sparse Core Ops, SparseCore 0:
  9.7 64.2 all-gather.1
  452.1 88.4 reduce-scatter.4
  575.0 72.7 reduce-scatter.6
where the time goes:
time: 714 us; the launch traced here: 707 us
  matrix products  200 us (28%)
  other arithmetic  164 us (23%)
  waiting for transfers between devices  124 us (17%)
  local copies, waits for them, and re-layouts  99 us (14%)
  blocking collectives  69.9 us (10%)
  starting transfers between devices  34.7 us (5%)
  between operations  14.3 us (2%)
    unnamed x7, other arithmetic  94 us
    unnamed x4, waiting for transfers between devices  51.8 us
    dot_general x8, matrix products, one_block(): jnp.einsum('qk,qd->kd', dscore, rows_q, preferred_element_type=jnp.float32)  44.4 us
    unnamed x41, local copies, waits for them, and re-layouts  40.7 us
    dot_general x8, matrix products, one_block(): jnp.dot(probs_low, value_part, preferred_element_type=jnp.float32)  40.4 us
    select_n x8, other arithmetic, one_block(): probs = jnp.where(live_rows[:, None], probs, jnp.zeros_like(probs))  38.5 us
    dot_general x8, matrix products, one_block(): jnp.dot(dscore, key_part, preferred_element_type=jnp.float32)  32.8 us
    another operation x4, local copies, waits for them, and re-layouts, shards(): jnp.stack([result[member] for result in results], axis=1)[None]  28.5 us
  transfers between devices with their start and end apart: 10, of which 5 were waited for; matrix products, arithmetic and copies ran while one was open for 20% of the time, Pallas kernels for 0%

commit v1 on v0

v1 whole, which is shorter than its diff:
```python
import jax
import jax.numpy as jnp
from jax import lax
from jax.experimental import pallas as pl
from jax.experimental.pallas import tpu as pltpu
from jax.sharding import PartitionSpec as P

HEAD_DIM = 128
SCALE = 1.0 / HEAD_DIM**0.5
LOG2E = 1.4426950408889634
EPSILON = 1e-30
BLOCK = 512
BF16 = jnp.bfloat16
F32 = jnp.float32
PARAMS = pltpu.CompilerParams(vmem_limit_bytes=56 * 2**20)


def contract(left, right, left_dim, right_dim):
    return lax.dot_general(
        left, right, (((left_dim,), (right_dim,)), ((), ())), preferred_element_type=F32
    )


def split_columns(sources):
    tokens, inner = sources[0].shape
    heads = inner // HEAD_DIM
    count = len(sources)

    def body(*refs):
        out, sems = refs[count], refs[count + 1]
        copies = []
        for which in range(count):
            for head in range(heads):
                copies.append(
                    pltpu.make_async_copy(
                        refs[which].at[:, pl.ds(head * HEAD_DIM, HEAD_DIM)],
                        out.at[head, pl.ds(which * tokens, tokens), :],
                        sems.at[which * heads + head],
                    )
                )
        for copy in copies:
            copy.start()
        for copy in copies:
            copy.wait()

    return pl.pallas_call(
        body,
        in_specs=[pl.BlockSpec(memory_space=pl.ANY)] * count,
        out_specs=pl.BlockSpec(memory_space=pl.ANY),
        out_shape=jax.ShapeDtypeStruct((heads, count * tokens, HEAD_DIM), BF16),
        scratch_shapes=[pltpu.SemaphoreType.DMA((count * heads,))],
        name="split_columns",
    )(*sources)


def join_columns(stacked, count):
    heads, rows, _ = stacked.shape
    tokens = rows // count

    def body(*refs):
        source, outs, sems = refs[0], refs[1 : 1 + count], refs[1 + count]
        copies = []
        for which in range(count):
            for head in range(heads):
                copies.append(
                    pltpu.make_async_copy(
                        source.at[head, pl.ds(which * tokens, tokens), :],
                        outs[which].at[:, pl.ds(head * HEAD_DIM, HEAD_DIM)],
                        sems.at[which * heads + head],
                    )
                )
        for copy in copies:
            copy.start()
        for copy in copies:
            copy.wait()

    return pl.pallas_call(
        body,
        in_specs=[pl.BlockSpec(memory_space=pl.ANY)],
        out_specs=[pl.BlockSpec(memory_space=pl.ANY)] * count,
        out_shape=[jax.ShapeDtypeStruct((tokens, heads * HEAD_DIM), BF16)] * count,
        scratch_shapes=[pltpu.SemaphoreType.DMA((count * heads,))],
        name="join_columns",
    )(stacked)


def forward(valid_len, packed):
    parts, rows, _ = packed.shape
    tokens = rows // 3
    total = parts * tokens
    span = BLOCK // tokens

    def body(len_ref, q_ref, k_ref, v_ref, e_ref, att_ref, qt_ref, inv_ref, kt_ref, va_ref, ka, vt):
        step = pl.program_id(0)
        length = len_ref[0]

        @pl.when(step == 0)
        def _():
            key_rows = k_ref[...].reshape(total, HEAD_DIM)
            value_rows = v_ref[...].reshape(total, HEAD_DIM)
            row = lax.broadcasted_iota(jnp.int32, (total, HEAD_DIM), 0)
            col = lax.broadcasted_iota(jnp.int32, (total, HEAD_DIM), 1)
            ka[:, :HEAD_DIM] = key_rows
            ka[:, HEAD_DIM:] = jnp.where((row >= length) & (col == 0), -1e30, 0.0).astype(BF16)
            vt[:HEAD_DIM, :] = value_rows.T
            vt[HEAD_DIM:, :] = jnp.ones((16, total), BF16)
            kt_ref[...] = key_rows.T
            va_ref[:, :HEAD_DIM] = value_rows
            va_ref[:, HEAD_DIM:] = jnp.where(col < 2, 1.0, 0.0).astype(BF16)

        query = q_ref[...].reshape(BLOCK, HEAD_DIM).T
        qt_ref[...] = query
        row = lax.broadcasted_iota(jnp.int32, (HEAD_DIM, BLOCK), 0)
        extra = jnp.where(row == 0, 1.0, 0.0).astype(BF16)
        scores = contract(ka[...], jnp.concatenate([query, extra], axis=0), 1, 0)
        top = jnp.max(scores, axis=0, keepdims=True)
        slot = step * BLOCK + lax.broadcasted_iota(jnp.int32, (1, BLOCK), 1)
        live = slot < length
        top = jnp.where(live, top * (SCALE * LOG2E), 1e30)
        low = jnp.exp2(scores * (SCALE * LOG2E) - top).astype(BF16)
        e_ref[...] = low
        summed = contract(vt[...], low, 1, 0)
        inverse = jnp.where(live, 1.0 / summed[HEAD_DIM : HEAD_DIM + 1], 0.0)
        att_ref[...] = (summed[:HEAD_DIM] * inverse).astype(BF16)
        inv_ref[...] = jnp.broadcast_to(inverse, (8, BLOCK))

    whole = lambda i, n: (0, 0)
    column = lambda i, n: (0, i)
    return pl.pallas_call(
        body,
        grid_spec=pltpu.PrefetchScalarGridSpec(
            num_scalar_prefetch=1,
            grid=(total // BLOCK,),
            in_specs=[
                pl.BlockSpec((span, tokens, HEAD_DIM), lambda i, n: (i, 0, 0)),
                pl.BlockSpec((parts, tokens, HEAD_DIM), lambda i, n: (0, 1, 0)),
                pl.BlockSpec((parts, tokens, HEAD_DIM), lambda i, n: (0, 2, 0)),
            ],
            out_specs=[
                pl.BlockSpec((total, BLOCK), column),
                pl.BlockSpec((HEAD_DIM, BLOCK), column),
                pl.BlockSpec((HEAD_DIM, BLOCK), column),
                pl.BlockSpec((8, BLOCK), column),
                pl.BlockSpec((HEAD_DIM, total), whole),
                pl.BlockSpec((total, 2 * HEAD_DIM), whole),
            ],
            scratch_shapes=[
                pltpu.VMEM((total, 2 * HEAD_DIM), BF16),
                pltpu.VMEM((HEAD_DIM + 16, total), BF16),
            ],
        ),
        out_shape=[
            jax.ShapeDtypeStruct((total, total), BF16),
            jax.ShapeDtypeStruct((HEAD_DIM, total), BF16),
            jax.ShapeDtypeStruct((HEAD_DIM, total), BF16),
            jax.ShapeDtypeStruct((8, total), F32),
            jax.ShapeDtypeStruct((HEAD_DIM, total), BF16),
            jax.ShapeDtypeStruct((total, 2 * HEAD_DIM), BF16),
        ],
        compiler_params=PARAMS,
        cost_estimate=pl.CostEstimate(
            flops=6 * total * total * HEAD_DIM,
            bytes_accessed=2 * total * total,
            transcendentals=total * total,
        ),
        name="forward",
    )(valid_len, packed, packed, packed)


def project(cotangent, gated, attended, inverse):
    total, width = cotangent.shape
    block = 1024

    def body(c_ref, w_ref, o_ref, inv_ref, g_ref, d_ref, a_ref):
        step = pl.program_id(0)
        rows = c_ref[...]
        grad = contract(w_ref[...], rows, 1, 1).astype(BF16).astype(F32)
        low = (grad * inv_ref[0:1]).astype(BF16)
        g_ref[...] = low
        out = o_ref[...]
        delta = jnp.sum(low.astype(F32) * out.astype(F32), axis=0, keepdims=True)
        d_ref[...] = jnp.broadcast_to(delta, (8, block))
        outer = contract(out, rows, 1, 0)

        @pl.when(step == 0)
        def _():
            a_ref[...] = outer

        @pl.when(step > 0)
        def _():
            a_ref[...] += outer

    column = lambda i: (0, i)
    whole = lambda i: (0, 0)
    return pl.pallas_call(
        body,
        grid=(total // block,),
        in_specs=[
            pl.BlockSpec((block, width), lambda i: (i, 0)),
            pl.BlockSpec((HEAD_DIM, width), whole),
            pl.BlockSpec((HEAD_DIM, block), column),
            pl.BlockSpec((8, block), column),
        ],
        out_specs=[
            pl.BlockSpec((HEAD_DIM, block), column),
            pl.BlockSpec((8, block), column),
            pl.BlockSpec((HEAD_DIM, width), whole),
        ],
        out_shape=[
            jax.ShapeDtypeStruct((HEAD_DIM, total), BF16),
            jax.ShapeDtypeStruct((8, total), F32),
            jax.ShapeDtypeStruct((HEAD_DIM, width), F32),
        ],
        compiler_params=PARAMS,
        cost_estimate=pl.CostEstimate(
            flops=4 * total * width * HEAD_DIM,
            bytes_accessed=2 * total * width,
            transcendentals=0,
        ),
        name="project",
    )(cotangent, gated, attended, inverse)


def backward(low, grad, delta, query, key, value, parts):
    total = low.shape[0]
    tokens = total // parts
    span = BLOCK // tokens
    last = total // BLOCK - 1

    def body(e_ref, g_ref, d_ref, q_ref, k_ref, v_ref, o_ref, dk, dv):
        step = pl.program_id(0)
        minus = -d_ref[0:1]
        high = minus.astype(BF16).astype(F32)
        row = lax.broadcasted_iota(jnp.int32, (HEAD_DIM, BLOCK), 0)
        extra = jnp.where(row == 0, high, jnp.where(row == 1, minus - high, 0.0)).astype(BF16)
        grad_block = g_ref[...]
        dprob = contract(v_ref[...], jnp.concatenate([grad_block, extra], axis=0), 1, 0)
        probs = e_ref[...]
        dscore = (probs.astype(F32) * dprob).astype(BF16)
        dq = contract(k_ref[...], dscore, 1, 0) * SCALE
        o_ref[pl.ds(step * span, span), 0:tokens, :] = (
            dq.T.astype(BF16).reshape(span, tokens, HEAD_DIM)
        )
        dv_step = contract(probs, grad_block, 1, 1)
        dk_step = contract(dscore, q_ref[...], 1, 1)

        @pl.when(step == 0)
        def _():
            dk[...] = dk_step
            dv[...] = dv_step

        @pl.when((step > 0) & (step < last))
        def _():
            dk[...] += dk_step
            dv[...] += dv_step

        @pl.when(step == last)
        def _():
            o_ref[:, tokens : 2 * tokens, :] = (
                ((dk[...] + dk_step) * SCALE).astype(BF16).reshape(parts, tokens, HEAD_DIM)
            )
            o_ref[:, 2 * tokens :, :] = (
                (dv[...] + dv_step).astype(BF16).reshape(parts, tokens, HEAD_DIM)
            )

    column = lambda i: (0, i)
    whole = lambda i: (0, 0)
    return pl.pallas_call(
        body,
        grid=(last + 1,),
        in_specs=[
            pl.BlockSpec((total, BLOCK), column),
            pl.BlockSpec((HEAD_DIM, BLOCK), column),
            pl.BlockSpec((8, BLOCK), column),
            pl.BlockSpec((HEAD_DIM, BLOCK), column),
            pl.BlockSpec((HEAD_DIM, total), whole),
            pl.BlockSpec((total, 2 * HEAD_DIM), whole),
        ],
        out_specs=pl.BlockSpec((parts, 3 * tokens, HEAD_DIM), lambda i: (0, 0, 0)),
        out_shape=jax.ShapeDtypeStruct((parts, 3 * tokens, HEAD_DIM), BF16),
        scratch_shapes=[pltpu.VMEM((total, HEAD_DIM), F32), pltpu.VMEM((total, HEAD_DIM), F32)],
        compiler_params=PARAMS,
        cost_estimate=pl.CostEstimate(
            flops=10 * total * total * HEAD_DIM,
            bytes_accessed=2 * total * total,
            transcendentals=0,
        ),
        name="backward",
    )(low, grad, delta, query, key, value)


def total_over(values, axis, size):
    spread = jnp.broadcast_to(values[None], (size,) + values.shape)
    return jnp.sum(lax.all_to_all(spread, axis, 0, 0, tiled=True), axis=0)


def shards(
    queries, key_rows, value_rows, cotangent, attn_gate, lengths, w_out, row_moment, col_moment
):
    seq_size = lax.axis_size("seq")
    dp_size = lax.axis_size("dp")
    inner_dim = queries.shape[2]
    width_dim = cotangent.shape[2]
    tokens = queries.shape[1]
    gate = attn_gate[0][None, :]
    every = lax.all_gather(cotangent[0], "seq", axis=0, tiled=True)
    packed = split_columns([queries[0], key_rows[0], value_rows[0]])
    packed = lax.all_to_all(packed, "seq", 0, 0, tiled=True)
    weight = w_out.astype(F32)
    gated = (weight * gate).astype(BF16)
    low, attended, query, inverse, key, value = forward(lengths, packed)
    grad, delta, outer = project(every, gated, attended, inverse)

    partial = (outer * gate).astype(BF16).reshape(HEAD_DIM, dp_size, width_dim // dp_size)
    partial = lax.all_to_all(partial.transpose(1, 0, 2), "dp", 0, 0, tiled=True)
    grad_weight = jnp.sum(partial.astype(F32), axis=0)
    squares = grad_weight * grad_weight + EPSILON
    gate_part = jnp.sum(weight * outer, axis=0)
    row_total = total_over(jnp.sum(squares, axis=1), "dp", dp_size)
    joined = total_over(
        jnp.concatenate([jnp.sum(squares, axis=0), gate_part]), "seq", seq_size
    )
    col_total, grad_gate = joined[: width_dim // dp_size], joined[width_dim // dp_size :]
    row_new = 0.8 * row_moment + 0.2 * (row_total / width_dim)
    col_new = 0.8 * col_moment + 0.2 * (col_total / inner_dim)

    back = backward(low, grad, delta, query, key, value, seq_size)
    back = lax.all_to_all(back, "seq", 0, 0, tiled=True)
    grad_q, grad_k, grad_v = join_columns(back, 3)
    return (
        grad_q[None],
        grad_k[None],
        grad_v[None],
        grad_gate[None],
        grad_weight,
        row_new,
        col_new,
    )


def solution(mesh):
    tokens = P("dp", "seq", None)
    return jax.shard_map(
        shards,
        mesh=mesh,
        in_specs=(
            tokens,
            tokens,
            tokens,
            tokens,
            P("dp", None),
            P("dp"),
            P("seq", None),
            P("seq"),
            P("dp"),
        ),
        out_specs=(
            tokens,
            tokens,
            tokens,
            P("dp", None),
            P("seq", "dp"),
            P("seq"),
            P("dp"),
        ),
        check_vma=False,
    )
```

time: 714 us -> 422 us (0.59)
  Pallas kernels: 0 us -> 278 us
  matrix products: 200 us -> 0 us
  other arithmetic: 164 us -> 3.53 us
  local copies, waits for them, and re-layouts: 99 us -> 5.53 us
  blocking collectives: 69.9 us -> 16.2 us
  waiting for transfers between devices: 124 us -> 83 us
  starting transfers between devices: 34.7 us -> 19.2 us
    pallas_call x0 -> x5, Pallas kernels: none -> 278 us  [the longest x1 96.8 us: split_columns(): pl.pallas_call(body, in_specs=[pl.BlockSpec(memory_space=pl.ANY)] * count...]
    dot_general x51 -> x0, matrix products: 200 us -> none  [the longest x8 44.4 us: one_block(): jnp.einsum('qk,qd->kd', dscore, rows_q, preferred_element_type=jnp.float32)]
    unnamed x7 -> x1, other arithmetic: 94 us -> 0.02 us
    unnamed x4 -> x1, waiting for transfers between devices: 51.8 us -> 0.68 us
    psum x2 -> x0, blocking collectives: 49.8 us -> none  [the longest x1 28.2 us: shards(): grad_gate = lax.psum(gate_part, 'seq')]
    select_n x8 -> x0, other arithmetic: 38.5 us -> none  [one_block(): probs = jnp.where(live_rows[:, None], probs, jnp.zeros_like(probs))]
    unnamed x41 -> x14, local copies, waits for them, and re-layouts: 40.7 us -> 3.33 us
    another operation x6 -> x0, local copies, waits for them, and re-layouts: 30.7 us -> none  [the longest x4 28.5 us: shards(): jnp.stack([result[member] for result in results], axis=1)[None]]
  transfers between devices with their start and end apart: 10 -> 5, of which waited for: 5 -> 3; matrix products, arithmetic and copies ran while one was open for 20% -> 1% of each run, Pallas kernels for 0% -> 41%
where the time goes in v1:
time: 422 us; the launch traced here: 421 us
  Pallas kernels  278 us (66%)
  waiting for transfers between devices  83 us (20%)
  starting transfers between devices  19.2 us (5%)
  blocking collectives  16.2 us (4%)
  between operations  14.8 us (4%)
  local copies, waits for them, and re-layouts  5.53 us (1%)
    pallas_call x1, Pallas kernels, split_columns(): pl.pallas_call(body, in_specs=[pl.BlockSpec(memory_space=pl.ANY)] * count...  96.8 us
    pallas_call x1, Pallas kernels, join_columns(): pl.pallas_call(body, in_specs=[pl.BlockSpec(memory_space=pl.ANY)], out_sp...  96.8 us
    pallas_call x1, Pallas kernels, backward(): pl.pallas_call(body, grid=(last + 1,), in_specs=[pl.BlockSpec((total, BLO...  40.5 us
    all_to_all x1, waiting for transfers between devices, shards(): packed = lax.all_to_all(packed, 'seq', 0, 0, tiled=True)  37.6 us
    all_to_all x1, waiting for transfers between devices, shards(): back = lax.all_to_all(back, 'seq', 0, 0, tiled=True)  37.2 us
    pallas_call x1, Pallas kernels, forward(): pl.pallas_call(body, grid_spec=pltpu.PrefetchScalarGridSpec(num_scalar_pr...  33.9 us
    all_to_all x1, blocking collectives, shards(): partial = lax.all_to_all(partial.transpose(1, 0, 2), 'dp', 0, 0, tiled=True)  16.2 us
    pallas_call x1, Pallas kernels, project(): pl.pallas_call(body, grid=(total // block,), in_specs=[pl.BlockSpec((bloc...  10.3 us
  transfers between devices with their start and end apart: 5, of which 3 were waited for; matrix products, arithmetic and copies ran while one was open for 1% of the time, Pallas kernels for 41%

profile of v1, /device:TPU:0, one launch (start us, length us, event | category | flops | bytes accessed | tf_op | source)
XLA Modules:
  0.0 420.6 jit_solution(657785381274477377)
XLA Ops:
  7.2 0.0 all-gather.3.cloned.1.call-start
  7.2 0.7 all-gather.3.cloned.1.call-update
  7.9 96.8 %split_columns.1 = bf16[16,768,128]{2,1,0:T(8,128)(2,1)} custom-call(bf16[256,2048]{1,0:T(8,128)(2,1)} %bitcast.13, bf16[256,2048]{1,0:T(8,128)(2,1)} %bitcast.14, bf16[256,2048]{1,0:T(8,128)(2,1)} %bitcast.15), custom_call_target="tpu_custom_call" | custom-call | tf_op jit(solution)/shard_map/split_columns/pallas_call | solution.py:46
  104.8 6.7 %all-to-all-start = ((bf16[16,768,128]{2,1,0:T(8,128)(2,1)}), bf16[16,768,128]{2,1,0:T(8,128)(2,1)S(1)}, u32[]{:S(2)}, u32[]{:S(2)}) async-start(bf16[16,768,128]{2,1,0:T(8,128)(2,1)} %split_columns.1), calls=%async_computation | async-start | bytes 6291456 | tf_op jit(solution)/shard_map/all_to_all | solution.py:308
  112.1 0.8 fusion.w_ref
  112.9 37.6 %all-to-all-done.q_ref.k_ref.v_ref = bf16[16,768,128]{2,1,0:T(8,128)(2,1)S(1)} async-done(((bf16[16,768,128]{2,1,0:T(8,128)(2,1)}), bf16[16,768,128]{2,1,0:T(8,128)(2,1)S(1)}, u32[]{:S(2)}, u32[]{:S(2)}) %all-to-all-start) | async-done | bytes 3145760 | tf_op jit(solution)/shard_map/all_to_all | solution.py:308
  150.5 1.6 copy-done.1
  152.2 33.9 %forward.1 = (bf16[4096,4096]{1,0:T(8,128)(2,1)}, bf16[128,4096]{1,0:T(8,128)(2,1)}, bf16[128,4096]{1,0:T(8,128)(2,1)}, f32[8,4096]{1,0:T(8,128)}, bf16[128,4096]{1,0:T(8,128)(2,1)}, /*index=5*/bf16[4096,256]{1,0:T(8,128)(2,1)}) custom-call(s32[1]{0:T(128)S(6)} %copy.24.len_ref, bf16[16,768,128]{2,1,0:T(8,128)(2,1)} %copy-done.1, ...), custom_call_target="tpu_custom_call" | custom-call | flops 12884901888 | bytes 33554432 | tf_op jit(solution)/shard_map/forward/pallas_call | solution.py:129
  186.1 0.0 all-gather.3.cloned.1.call-done
  186.1 10.3 %project.1 = (bf16[128,4096]{1,0:T(8,128)(2,1)}, f32[8,4096]{1,0:T(8,128)}, f32[128,1536]{1,0:T(8,128)}) custom-call(bf16[4096,1536]{1,0:T(8,128)(2,1)} %bitcast.11, bf16[128,1536]{1,0:T(8,128)(2,1)} %fusion.w_ref, bf16[128,4096]{1,0:T(8,128)(2,1)} %get-tuple-element.20.o_ref, f32[8,4096]{1,0:T(8,128)} %get-tuple-element.21.inv_ref), custom_call_target="tpu_custom_call" | custom-call | flops 3221225472 | bytes 12582912 | tf_op jit(solution)/shard_map/project/pallas_call | solution.py:195
  196.4 1.3 multiply_convert_fusion
  197.7 0.2 copy.18
  197.9 16.2 %all_to_all.27 = bf16[8,128,192]{1,2,0:T(8,128)(2,1)S(1)} all-to-all(bf16[8,128,192]{1,2,0:T(8,128)(2,1)S(1)} %bitcast.12), channel_id=1, replica_groups=mesh['dp'=8,'seq'=16] {'dp'}, dimensions={0} | all-to-all | bytes 786432 | tf_op jit(solution)/shard_map/all_to_all | solution.py:315
  214.2 0.1 convert_reduce_fusion
  214.2 0.0 copy-start.3
  214.2 0.1 fusion.2
  214.3 0.6 broadcast_in_dim.29
  214.9 3.3 all-to-all-start.4
  218.3 0.1 pad_maximum_fusion
  218.3 7.4 %all-to-all-done.4 = f32[8,1,128]{2,1,0:T(1,128)S(1)} async-done(((f32[8,1,128]{2,1,0:T(1,128)}), f32[8,1,128]{2,1,0:T(1,128)S(1)}, u32[]{:S(2)}, u32[]{:S(2)}) %all-to-all-start.4) | async-done | bytes 4128 | tf_op jit(solution)/shard_map/all_to_all | solution.py:294
  225.8 0.7 broadcast_in_dim.27
  226.5 3.7 all-to-all-start.3
  230.2 40.5 %backward.1 = bf16[16,768,128]{2,1,0:T(8,128)(2,1)} custom-call(bf16[4096,4096]{1,0:T(8,128)(2,1)} %get-tuple-element.19.e_ref, bf16[128,4096]{1,0:T(8,128)(2,1)} %get-tuple-element.22.g_ref, f32[8,4096]{1,0:T(8,128)} %get-tuple-element.23.d_ref, bf16[128,4096]{1,0:T(8,128)(2,1)} %get-tuple-element.24.q_ref, bf16[128,4096]{1,0:T(8,128)(2,1)} %get-tuple-element.25.k_ref, ...), custom_call_target="tpu_custom_call" | custom-call | flops 21474836480 | bytes 33554432 | tf_op jit(solution)/shard_map/backward/pallas_call | solution.py:268
  270.7 5.5 %all-to-all-start.1 = ((bf16[16,768,128]{2,1,0:T(8,128)(2,1)}), bf16[16,768,128]{2,1,0:T(8,128)(2,1)S(1)}, u32[]{:S(2)}, u32[]{:S(2)}) async-start(bf16[16,768,128]{2,1,0:T(8,128)(2,1)} %backward.1), calls=%async_computation.1 | async-start | bytes 6291456 | tf_op jit(solution)/shard_map/all_to_all | solution.py:328
  276.2 0.5 multiply_add_fusion.1
  276.7 0.1 reduce_sum.57
  276.8 0.1 slice.8
  276.9 0.6 broadcast_in_dim.28
  277.5 0.6 fusion.4
  278.0 37.2 %all-to-all-done.1.refs_0_ = bf16[16,768,128]{2,1,0:T(8,128)(2,1)S(1)} async-done(((bf16[16,768,128]{2,1,0:T(8,128)(2,1)}), bf16[16,768,128]{2,1,0:T(8,128)(2,1)S(1)}, u32[]{:S(2)}, u32[]{:S(2)}) %all-to-all-start.1) | async-done | bytes 3145760 | tf_op jit(solution)/shard_map/all_to_all | solution.py:328
  315.3 1.6 copy-done
  316.9 96.8 %join_columns.1 = (bf16[256,2048]{1,0:T(8,128)(2,1)}, bf16[256,2048]{1,0:T(8,128)(2,1)}, bf16[256,2048]{1,0:T(8,128)(2,1)}) custom-call(bf16[16,768,128]{2,1,0:T(8,128)(2,1)} %copy-done), custom_call_target="tpu_custom_call" | custom-call | tf_op jit(solution)/shard_map/join_columns/pallas_call | solution.py:77
  (14 shorter events, 0.1 us)
Async XLA Ops:
  7.2 178.9 %all-gather.3.cloned.1.call-start = ((), (), s32[]{:S(2)}) async-start(), calls=%async_computation.5 | async-start | bytes 13369344 | tf_op jit(solution)/shard_map/all_gather | solution.py:306
  104.7 7.3 %copy-start.4 = (f32[1,1536]{1,0:T(1,128)S(1)}, f32[1,1536]{1,0:T(1,128)}, u32[]{:S(2)}) copy-start(f32[1,1536]{1,0:T(1,128)} %param.13) | copy-start | bytes 18436
  104.7 7.4 %copy-start.2 = (bf16[128,1536]{1,0:T(8,128)(2,1)S(1)}, bf16[128,1536]{1,0:T(8,128)(2,1)}, u32[]{:S(2)}) copy-start(bf16[128,1536]{1,0:T(8,128)(2,1)} %param.15) | copy-start | bytes 1179652
  104.8 45.8 %all-to-all-start = ((bf16[16,768,128]{2,1,0:T(8,128)(2,1)}), bf16[16,768,128]{2,1,0:T(8,128)(2,1)S(1)}, u32[]{:S(2)}, u32[]{:S(2)}) async-start(bf16[16,768,128]{2,1,0:T(8,128)(2,1)} %split_columns.1), calls=%async_computation | async-start | bytes 6291456 | tf_op jit(solution)/shard_map/all_to_all | solution.py:308
  150.5 1.7 copy-start.1
  214.2 56.4 %copy-start.3 = (f32[128,192]{0,1:T(8,128)}, f32[128,192]{0,1:T(8,128)S(1)}, u32[]{:S(2)}) copy-start(f32[128,192]{0,1:T(8,128)S(1)} %convert_reduce_fusion) | copy-start | bytes 294916
  214.9 10.8 %all-to-all-start.4 = ((f32[8,1,128]{2,1,0:T(1,128)}), f32[8,1,128]{2,1,0:T(1,128)S(1)}, u32[]{:S(2)}, u32[]{:S(2)}) async-start(f32[8,1,128]{2,1,0:T(1,128)} %broadcast_in_dim.29), calls=%async_computation.4 | async-start | bytes 8192 | tf_op jit(solution)/shard_map/all_to_all | solution.py:294
  226.5 44.2 %all-to-all-start.3 = ((f32[16,1,1728]{2,1,0:T(1,128)}), f32[16,1,1728]{2,1,0:T(1,128)S(1)}, u32[]{:S(2)}, u32[]{:S(2)}) async-start(f32[16,1,1728]{2,1,0:T(1,128)} %broadcast_in_dim.27), calls=%async_computation.3 | async-start | bytes 229376 | tf_op jit(solution)/shard_map/all_to_all | solution.py:294
  270.7 5.5 %copy-start.6 = (f32[128]{0:T(128)S(1)}, f32[128]{0:T(128)}, u32[]{:S(2)}) copy-start(f32[128]{0:T(128)} %param.16) | copy-start | bytes 1540
  270.7 6.8 %copy-start.5 = (f32[192]{0:T(256)S(1)}, f32[192]{0:T(256)}, u32[]{:S(2)}) copy-start(f32[192]{0:T(256)} %param.17) | copy-start | bytes 2308
  270.7 44.6 %all-to-all-start.1 = ((bf16[16,768,128]{2,1,0:T(8,128)(2,1)}), bf16[16,768,128]{2,1,0:T(8,128)(2,1)S(1)}, u32[]{:S(2)}, u32[]{:S(2)}) async-start(bf16[16,768,128]{2,1,0:T(8,128)(2,1)} %backward.1), calls=%async_computation.1 | async-start | bytes 6291456 | tf_op jit(solution)/shard_map/all_to_all | solution.py:328
  315.3 1.7 copy-start
Sparse Core Ops, SparseCore 0:
  9.7 118.7 all-gather.2

commit v2 on v1

--- a/solution.py
+++ b/solution.py
@@ -25,68 +25,46 @@
     tokens, inner = sources[0].shape
     heads = inner // HEAD_DIM
     count = len(sources)
+    block = tokens // 4
 
     def body(*refs):
-        out, sems = refs[count], refs[count + 1]
-        copies = []
+        out = refs[count]
         for which in range(count):
             for head in range(heads):
-                copies.append(
-                    pltpu.make_async_copy(
-                        refs[which].at[:, pl.ds(head * HEAD_DIM, HEAD_DIM)],
-                        out.at[head, pl.ds(which * tokens, tokens), :],
-                        sems.at[which * heads + head],
-                    )
-                )
-        for copy in copies:
-            copy.start()
-        for copy in copies:
-            copy.wait()
-
-    return pl.pallas_call(
-        body,
-        in_specs=[pl.BlockSpec(memory_space=pl.ANY)] * count,
-        out_specs=pl.BlockSpec(memory_space=pl.ANY),
-        out_shape=jax.ShapeDtypeStruct((heads, count * tokens, HEAD_DIM), BF16),
-        scratch_shapes=[pltpu.SemaphoreType.DMA((count * heads,))],
+                out[head, which] = refs[which][:, head * HEAD_DIM : (head + 1) * HEAD_DIM]
+
+    return pl.pallas_call(
+        body,
+        grid=(tokens // block,),
+        in_specs=[pl.BlockSpec((block, inner), lambda i: (i, 0))] * count,
+        out_specs=pl.BlockSpec((heads, count, block, HEAD_DIM), lambda i: (0, 0, i, 0)),
+        out_shape=jax.ShapeDtypeStruct((heads, count, tokens, HEAD_DIM), BF16),
         name="split_columns",
     )(*sources)
 
 
-def join_columns(stacked, count):
-    heads, rows, _ = stacked.shape
-    tokens = rows // count
+def join_columns(stacked):
+    heads, count, tokens, _ = stacked.shape
+    inner = heads * HEAD_DIM
+    block = tokens // 4
 
     def body(*refs):
-        source, outs, sems = refs[0], refs[1 : 1 + count], refs[1 + count]
-        copies = []
         for which in range(count):
             for head in range(heads):
-                copies.append(
-                    pltpu.make_async_copy(
-                        source.at[head, pl.ds(which * tokens, tokens), :],
-                        outs[which].at[:, pl.ds(head * HEAD_DIM, HEAD_DIM)],
-                        sems.at[which * heads + head],
-                    )
-                )
-        for copy in copies:
-            copy.start()
-        for copy in copies:
-            copy.wait()
-
-    return pl.pallas_call(
-        body,
-        in_specs=[pl.BlockSpec(memory_space=pl.ANY)],
-        out_specs=[pl.BlockSpec(memory_space=pl.ANY)] * count,
-        out_shape=[jax.ShapeDtypeStruct((tokens, heads * HEAD_DIM), BF16)] * count,
-        scratch_shapes=[pltpu.SemaphoreType.DMA((count * heads,))],
+                refs[1 + which][:, head * HEAD_DIM : (head + 1) * HEAD_DIM] = refs[0][head, which]
+
+    return pl.pallas_call(
+        body,
+        grid=(tokens // block,),
+        in_specs=[pl.BlockSpec((heads, count, block, HEAD_DIM), lambda i: (0, 0, i, 0))],
+        out_specs=[pl.BlockSpec((block, inner), lambda i: (i, 0))] * count,
+        out_shape=[jax.ShapeDtypeStruct((tokens, inner), BF16)] * count,
         name="join_columns",
     )(stacked)
 
 
 def forward(valid_len, packed):
-    parts, rows, _ = packed.shape
-    tokens = rows // 3
+    parts, _, tokens, _ = packed.shape
     total = parts * tokens
     span = BLOCK // tokens
 
@@ -132,9 +110,9 @@
             num_scalar_prefetch=1,
             grid=(total // BLOCK,),
             in_specs=[
-                pl.BlockSpec((span, tokens, HEAD_DIM), lambda i, n: (i, 0, 0)),
-                pl.BlockSpec((parts, tokens, HEAD_DIM), lambda i, n: (0, 1, 0)),
-                pl.BlockSpec((parts, tokens, HEAD_DIM), lambda i, n: (0, 2, 0)),
+                pl.BlockSpec((span, None, tokens, HEAD_DIM), lambda i, n: (i, 0, 0, 0)),
+                pl.BlockSpec((parts, None, tokens, HEAD_DIM), lambda i, n: (0, 1, 0, 0)),
+                pl.BlockSpec((parts, None, tokens, HEAD_DIM), lambda i, n: (0, 2, 0, 0)),
             ],
             out_specs=[
                 pl.BlockSpec((total, BLOCK), column),
@@ -238,7 +216,7 @@
         probs = e_ref[...]
         dscore = (probs.astype(F32) * dprob).astype(BF16)
         dq = contract(k_ref[...], dscore, 1, 0) * SCALE
-        o_ref[pl.ds(step * span, span), 0:tokens, :] = (
+        o_ref[pl.ds(step * span, span), 0] = (
             dq.T.astype(BF16).reshape(span, tokens, HEAD_DIM)
         )
         dv_step = contract(probs, grad_block, 1, 1)
@@ -256,10 +234,10 @@
 
         @pl.when(step == last)
         def _():
-            o_ref[:, tokens : 2 * tokens, :] = (
+            o_ref[:, 1] = (
                 ((dk[...] + dk_step) * SCALE).astype(BF16).reshape(parts, tokens, HEAD_DIM)
             )
-            o_ref[:, 2 * tokens :, :] = (
+            o_ref[:, 2] = (
                 (dv[...] + dv_step).astype(BF16).reshape(parts, tokens, HEAD_DIM)
             )
 
@@ -276,8 +254,8 @@
             pl.BlockSpec((HEAD_DIM, total), whole),
             pl.BlockSpec((total, 2 * HEAD_DIM), whole),
         ],
-        out_specs=pl.BlockSpec((parts, 3 * tokens, HEAD_DIM), lambda i: (0, 0, 0)),
-        out_shape=jax.ShapeDtypeStruct((parts, 3 * tokens, HEAD_DIM), BF16),
+        out_specs=pl.BlockSpec((parts, 3, tokens, HEAD_DIM), lambda i: (0, 0, 0, 0)),
+        out_shape=jax.ShapeDtypeStruct((parts, 3, tokens, HEAD_DIM), BF16),
         scratch_shapes=[pltpu.VMEM((total, HEAD_DIM), F32), pltpu.VMEM((total, HEAD_DIM), F32)],
         compiler_params=PARAMS,
         cost_estimate=pl.CostEstimate(
@@ -313,6 +291,8 @@
 
     partial = (outer * gate).astype(BF16).reshape(HEAD_DIM, dp_size, width_dim // dp_size)
     partial = lax.all_to_all(partial.transpose(1, 0, 2), "dp", 0, 0, tiled=True)
+    back = backward(low, grad, delta, query, key, value, seq_size)
+    back, partial = lax.optimization_barrier((back, partial))
     grad_weight = jnp.sum(partial.astype(F32), axis=0)
     squares = grad_weight * grad_weight + EPSILON
     gate_part = jnp.sum(weight * outer, axis=0)
@@ -323,10 +303,8 @@
     col_total, grad_gate = joined[: width_dim // dp_size], joined[width_dim // dp_size :]
     row_new = 0.8 * row_moment + 0.2 * (row_total / width_dim)
     col_new = 0.8 * col_moment + 0.2 * (col_total / inner_dim)
-
-    back = backward(low, grad, delta, query, key, value, seq_size)
     back = lax.all_to_all(back, "seq", 0, 0, tiled=True)
-    grad_q, grad_k, grad_v = join_columns(back, 3)
+    grad_q, grad_k, grad_v = join_columns(back)
     return (
         grad_q[None],
         grad_k[None],

time: 422 us -> 264 us (0.63)
  Pallas kernels: 278 us -> 93.5 us
  waiting for transfers between devices: 83 us -> 111 us
  blocking collectives: 16.2 us -> 9.09 us
  starting transfers between devices: 19.2 us -> 24.6 us
    pallas_call x2, Pallas kernels: 194 us -> 8.74 us  [the longest x1 4.37 us: join_columns(): pl.pallas_call(body, grid=(tokens // block,), in_specs=[pl.BlockSpec((hea...]
    all_to_all x1, waiting for transfers between devices: 37.6 us -> 65.8 us  [shards(): packed = lax.all_to_all(packed, 'seq', 0, 0, tiled=True)]
    all_to_all x1, blocking collectives: 16.2 us -> 9.09 us  [total_over(): return jnp.sum(lax.all_to_all(spread, axis, 0, 0, tiled=True), axis=0)]
    all_to_all x0 -> x1, starting transfers between devices: none -> 6.85 us  [shards(): partial = lax.all_to_all(partial.transpose(1, 0, 2), 'dp', 0, 0, tiled=True)]
  transfers between devices with their start and end apart: 5 -> 5, of which waited for: 3 -> 3; matrix products, arithmetic and copies ran while one was open for 1% -> 1% of each run, Pallas kernels for 41% -> 30%
where the time goes in v2:
time: 264 us; the launch traced here: 262 us
  waiting for transfers between devices  111 us (42%)
  Pallas kernels  93.5 us (35%)
  starting transfers between devices  24.6 us (9%)
  between operations  14.8 us (6%)
  blocking collectives  9.09 us (3%)
  local copies, waits for them, and re-layouts  5.57 us (2%)
  other arithmetic  3.53 us (1%)
    all_to_all x1, waiting for transfers between devices, shards(): packed = lax.all_to_all(packed, 'seq', 0, 0, tiled=True)  65.8 us
    pallas_call x1, Pallas kernels, backward(): pl.pallas_call(body, grid=(last + 1,), in_specs=[pl.BlockSpec((total, BLO...  40.5 us
    all_to_all x1, waiting for transfers between devices, shards(): back = lax.all_to_all(back, 'seq', 0, 0, tiled=True)  37.2 us
    pallas_call x1, Pallas kernels, forward(): pl.pallas_call(body, grid_spec=pltpu.PrefetchScalarGridSpec(num_scalar_pr...  33.9 us
    pallas_call x1, Pallas kernels, project(): pl.pallas_call(body, grid=(total // block,), in_specs=[pl.BlockSpec((bloc...  10.3 us
    all_to_all x1, blocking collectives, total_over(): return jnp.sum(lax.all_to_all(spread, axis, 0, 0, tiled=True), axis=0)  9.09 us
    all_to_all x1, waiting for transfers between devices, total_over(): return jnp.sum(lax.all_to_all(spread, axis, 0, 0, tiled=True), axis=0)  7.5 us
    all_to_all x1, starting transfers between devices, total_over(): return jnp.sum(lax.all_to_all(spread, axis, 0, 0, tiled=True), axis=0)  7.2 us
  transfers between devices with their start and end apart: 5, of which 3 were waited for; matrix products, arithmetic and copies ran while one was open for 1% of the time, Pallas kernels for 30%

profile of v2, /device:TPU:0, one launch (start us, length us, event | category | flops | bytes accessed | tf_op | source)
XLA Modules:
  0.0 262.3 jit_solution(12877019490361257813)
XLA Ops:
  7.2 0.0 all-gather.3.cloned.1.call-start
  7.2 0.7 all-gather.3.cloned.1.call-update
  7.9 4.4 %split_columns.1 = bf16[16,3,256,128]{3,2,1,0:T(8,128)(2,1)} custom-call(bf16[256,2048]{1,0:T(8,128)(2,1)} %bitcast.12, bf16[256,2048]{1,0:T(8,128)(2,1)} %bitcast.13, bf16[256,2048]{1,0:T(8,128)(2,1)} %bitcast.14), custom_call_target="tpu_custom_call" | custom-call | tf_op jit(solution)/shard_map/split_columns/pallas_call | solution.py:36
  12.3 6.6 %all-to-all-start = ((bf16[16,3,256,128]{3,2,1,0:T(8,128)(2,1)}), bf16[16,3,256,128]{3,2,1,0:T(8,128)(2,1)S(1)}, u32[]{:S(2)}, u32[]{:S(2)}) async-start(bf16[16,3,256,128]{3,2,1,0:T(8,128)(2,1)} %split_columns.1), calls=%async_computation | async-start | bytes 6291456 | tf_op jit(solution)/shard_map/all_to_all | solution.py:286
  19.6 0.8 fusion.w_ref
  20.4 65.8 %all-to-all-done.q_ref.k_ref.v_ref = bf16[16,3,256,128]{3,2,1,0:T(8,128)(2,1)S(1)} async-done(((bf16[16,3,256,128]{3,2,1,0:T(8,128)(2,1)}), bf16[16,3,256,128]{3,2,1,0:T(8,128)(2,1)S(1)}, u32[]{:S(2)}, u32[]{:S(2)}) %all-to-all-start) | async-done | bytes 3145760 | tf_op jit(solution)/shard_map/all_to_all | solution.py:286
  86.3 1.6 copy-done.1
  87.9 33.9 %forward.1 = (bf16[4096,4096]{1,0:T(8,128)(2,1)}, bf16[128,4096]{1,0:T(8,128)(2,1)}, bf16[128,4096]{1,0:T(8,128)(2,1)}, f32[8,4096]{1,0:T(8,128)}, bf16[128,4096]{1,0:T(8,128)(2,1)}, /*index=5*/bf16[4096,256]{1,0:T(8,128)(2,1)}) custom-call(s32[1]{0:T(128)S(6)} %copy.24.len_ref, bf16[16,3,256,128]{3,2,1,0:T(8,128)(2,1)} %copy-done.1, ...), custom_call_target="tpu_custom_call" | custom-call | flops 12884901888 | bytes 33554432 | tf_op jit(solution)/shard_map/forward/pallas_call | solution.py:107
  121.8 0.0 all-gather.3.cloned.1.call-done
  121.9 10.3 %project.1 = (bf16[128,4096]{1,0:T(8,128)(2,1)}, f32[8,4096]{1,0:T(8,128)}, f32[128,1536]{1,0:T(8,128)}) custom-call(bf16[4096,1536]{1,0:T(8,128)(2,1)} %bitcast.11, bf16[128,1536]{1,0:T(8,128)(2,1)} %fusion.w_ref, bf16[128,4096]{1,0:T(8,128)(2,1)} %get-tuple-element.22.o_ref, f32[8,4096]{1,0:T(8,128)} %get-tuple-element.23.inv_ref), custom_call_target="tpu_custom_call" | custom-call | flops 3221225472 | bytes 12582912 | tf_op jit(solution)/shard_map/project/pallas_call | solution.py:173
  132.2 1.3 fusion.1
  133.5 0.9 copy.18
  134.4 6.9 %all-to-all-start.1 = ((bf16[8,128,192]{1,2,0:T(8,128)(2,1)}), bf16[8,128,192]{1,2,0:T(8,128)(2,1)S(1)}, u32[]{:S(2)}, u32[]{:S(2)}) async-start(bf16[8,128,192]{1,2,0:T(8,128)(2,1)} %bitcast.5), calls=%async_computation.1 | async-start | bytes 786432 | tf_op jit(solution)/shard_map/all_to_all | solution.py:293
  141.2 40.5 %backward.1 = bf16[16,3,256,128]{3,2,1,0:T(8,128)(2,1)} custom-call(bf16[4096,4096]{1,0:T(8,128)(2,1)} %get-tuple-element.21.e_ref, bf16[128,4096]{1,0:T(8,128)(2,1)} %get-tuple-element.24.g_ref, f32[8,4096]{1,0:T(8,128)} %get-tuple-element.25.d_ref, bf16[128,4096]{1,0:T(8,128)(2,1)} %get-tuple-element.26.q_ref, bf16[128,4096]{1,0:T(8,128)(2,1)} %get-tuple-element.27.k_ref, ...), custom_call_target="tpu_custom_call" | custom-call | flops 21474836480 | bytes 33554432 | tf_op jit(solution)/shard_map/backward/pallas_call | solution.py:246
  181.7 0.1 convert_reduce_fusion
  181.8 0.0 copy-start.3
  181.8 0.1 fusion.2
  181.9 0.6 broadcast_in_dim.29
  182.5 7.2 %all-to-all-start.4 = ((f32[8,1,128]{2,1,0:T(1,128)}), f32[8,1,128]{2,1,0:T(1,128)S(1)}, u32[]{:S(2)}, u32[]{:S(2)}) async-start(f32[8,1,128]{2,1,0:T(1,128)} %broadcast_in_dim.29), calls=%async_computation.4 | async-start | bytes 8192 | tf_op jit(solution)/shard_map/all_to_all | solution.py:272
  189.7 0.1 pad_maximum_fusion
  189.8 7.5 %all-to-all-done.4 = f32[8,1,128]{2,1,0:T(1,128)S(1)} async-done(((f32[8,1,128]{2,1,0:T(1,128)}), f32[8,1,128]{2,1,0:T(1,128)S(1)}, u32[]{:S(2)}, u32[]{:S(2)}) %all-to-all-start.4) | async-done | bytes 4128 | tf_op jit(solution)/shard_map/all_to_all | solution.py:272
  197.3 0.1 broadcast_in_dim.27
  197.3 9.1 %all_to_all.27 = f32[16,1,1728]{2,1,0:T(1,128)S(1)} all-to-all(f32[16,1,1728]{2,1,0:T(1,128)S(1)} %broadcast_in_dim.27), channel_id=1, replica_groups=mesh['dp'=8,'seq'=16] {'seq'}, dimensions={0} | all-to-all | bytes 221184 | tf_op jit(solution)/shard_map/all_to_all | solution.py:272
  206.4 3.9 %all-to-all-start.2 = ((bf16[16,3,256,128]{3,2,1,0:T(8,128)(2,1)}), bf16[16,3,256,128]{3,2,1,0:T(8,128)(2,1)S(1)}, u32[]{:S(2)}, u32[]{:S(2)}) async-start(bf16[16,3,256,128]{3,2,1,0:T(8,128)(2,1)} %backward.1), calls=%async_computation.2 | async-start | bytes 6291456 | tf_op jit(solution)/shard_map/all_to_all | solution.py:306
  210.4 0.5 multiply_add_fusion.1
  210.9 0.1 reduce_sum.57
  210.9 0.1 slice.8
  211.0 0.6 broadcast_in_dim.28
  211.6 0.6 fusion.4
  212.2 37.2 %all-to-all-done.2.refs_0_ = bf16[16,3,256,128]{3,2,1,0:T(8,128)(2,1)S(1)} async-done(((bf16[16,3,256,128]{3,2,1,0:T(8,128)(2,1)}), bf16[16,3,256,128]{3,2,1,0:T(8,128)(2,1)S(1)}, u32[]{:S(2)}, u32[]{:S(2)}) %all-to-all-start.2) | async-done | bytes 3145760 | tf_op jit(solution)/shard_map/all_to_all | solution.py:306
  249.4 1.6 copy-done
  251.1 4.4 %join_columns.1 = (bf16[256,2048]{1,0:T(8,128)(2,1)}, bf16[256,2048]{1,0:T(8,128)(2,1)}, bf16[256,2048]{1,0:T(8,128)(2,1)}) custom-call(bf16[16,3,256,128]{3,2,1,0:T(8,128)(2,1)} %copy-done), custom_call_target="tpu_custom_call" | custom-call | tf_op jit(solution)/shard_map/join_columns/pallas_call | solution.py:56
  (14 shorter events, 0.1 us)
Async XLA Ops:
  7.2 114.7 %all-gather.3.cloned.1.call-start = ((), (), s32[]{:S(2)}) async-start(), calls=%async_computation.5 | async-start | bytes 13369344 | tf_op jit(solution)/shard_map/all_gather | solution.py:284
  12.3 7.3 %copy-start.4 = (f32[1,1536]{1,0:T(1,128)S(1)}, f32[1,1536]{1,0:T(1,128)}, u32[]{:S(2)}) copy-start(f32[1,1536]{1,0:T(1,128)} %param.13) | copy-start | bytes 18436
  12.3 7.3 %copy-start.2 = (bf16[128,1536]{1,0:T(8,128)(2,1)S(1)}, bf16[128,1536]{1,0:T(8,128)(2,1)}, u32[]{:S(2)}) copy-start(bf16[128,1536]{1,0:T(8,128)(2,1)} %param.15) | copy-start | bytes 1179652
  12.3 74.0 %all-to-all-start = ((bf16[16,3,256,128]{3,2,1,0:T(8,128)(2,1)}), bf16[16,3,256,128]{3,2,1,0:T(8,128)(2,1)S(1)}, u32[]{:S(2)}, u32[]{:S(2)}) async-start(bf16[16,3,256,128]{3,2,1,0:T(8,128)(2,1)} %split_columns.1), calls=%async_computation | async-start | bytes 6291456 | tf_op jit(solution)/shard_map/all_to_all | solution.py:286
  86.3 1.7 copy-start.1
  134.4 47.3 %all-to-all-start.1 = ((bf16[8,128,192]{1,2,0:T(8,128)(2,1)}), bf16[8,128,192]{1,2,0:T(8,128)(2,1)S(1)}, u32[]{:S(2)}, u32[]{:S(2)}) async-start(bf16[8,128,192]{1,2,0:T(8,128)(2,1)} %bitcast.5), calls=%async_computation.1 | async-start | bytes 786432 | tf_op jit(solution)/shard_map/all_to_all | solution.py:293
  181.8 24.7 %copy-start.3 = (f32[128,192]{0,1:T(8,128)}, f32[128,192]{0,1:T(8,128)S(1)}, u32[]{:S(2)}) copy-start(f32[128,192]{0,1:T(8,128)S(1)} %convert_reduce_fusion) | copy-start | bytes 294916
  182.5 14.8 %all-to-all-start.4 = ((f32[8,1,128]{2,1,0:T(1,128)}), f32[8,1,128]{2,1,0:T(1,128)S(1)}, u32[]{:S(2)}, u32[]{:S(2)}) async-start(f32[8,1,128]{2,1,0:T(1,128)} %broadcast_in_dim.29), calls=%async_computation.4 | async-start | bytes 8192 | tf_op jit(solution)/shard_map/all_to_all | solution.py:272
  206.4 3.9 %copy-start.6 = (f32[128]{0:T(128)S(1)}, f32[128]{0:T(128)}, u32[]{:S(2)}) copy-start(f32[128]{0:T(128)} %param.16) | copy-start | bytes 1540
  206.4 5.2 %copy-start.5 = (f32[192]{0:T(256)S(1)}, f32[192]{0:T(256)}, u32[]{:S(2)}) copy-start(f32[192]{0:T(256)} %param.17) | copy-start | bytes 2308
  206.4 43.0 %all-to-all-start.2 = ((bf16[16,3,256,128]{3,2,1,0:T(8,128)(2,1)}), bf16[16,3,256,128]{3,2,1,0:T(8,128)(2,1)S(1)}, u32[]{:S(2)}, u32[]{:S(2)}) async-start(bf16[16,3,256,128]{3,2,1,0:T(8,128)(2,1)} %backward.1), calls=%async_computation.2 | async-start | bytes 6291456 | tf_op jit(solution)/shard_map/all_to_all | solution.py:306
  249.4 1.7 copy-start
Sparse Core Ops, SparseCore 0:
  9.7 108.1 all-gather.2

commit v3 on v2

v3 whole, which is shorter than its diff:
```python
import jax
import jax.numpy as jnp
from jax import lax
from jax.experimental import pallas as pl
from jax.experimental.pallas import tpu as pltpu
from jax.sharding import PartitionSpec as P

HEAD_DIM = 128
SCALE = 1.0 / HEAD_DIM**0.5
LOG2E = 1.4426950408889634
EPSILON = 1e-30
BLOCK = 512
HALVES = 2
BF16 = jnp.bfloat16
F32 = jnp.float32
PARAMS = pltpu.CompilerParams(vmem_limit_bytes=56 * 2**20)


def contract(left, right, left_dim, right_dim):
    return lax.dot_general(
        left, right, (((left_dim,), (right_dim,)), ((), ())), preferred_element_type=F32
    )


def split_columns(sources):
    tokens, inner = sources[0].shape
    heads = inner // HEAD_DIM
    count = len(sources)
    block = tokens // 4

    def body(*refs):
        out = refs[count]
        for which in range(count):
            for head in range(heads):
                out[head, which] = refs[which][:, head * HEAD_DIM : (head + 1) * HEAD_DIM]

    return pl.pallas_call(
        body,
        grid=(tokens // block,),
        in_specs=[pl.BlockSpec((block, inner), lambda i: (i, 0))] * count,
        out_specs=pl.BlockSpec((heads, count, block, HEAD_DIM), lambda i: (0, 0, i, 0)),
        out_shape=jax.ShapeDtypeStruct((heads, count, tokens, HEAD_DIM), BF16),
        name="split_columns",
    )(*sources)


def join_columns(stacked):
    heads, count, tokens, _ = stacked.shape
    inner = heads * HEAD_DIM
    block = tokens // 4

    def body(*refs):
        rows = pl.ds(pl.program_id(0) * block, block)
        for which in range(count):
            for head in range(heads):
                refs[1 + which][:, head * HEAD_DIM : (head + 1) * HEAD_DIM] = refs[0][
                    head, which, rows, :
                ]

    return pl.pallas_call(
        body,
        grid=(tokens // block,),
        in_specs=[pl.BlockSpec(memory_space=pltpu.VMEM)],
        out_specs=[pl.BlockSpec((block, inner), lambda i: (i, 0))] * count,
        out_shape=[jax.ShapeDtypeStruct((tokens, inner), BF16)] * count,
        name="join_columns",
    )(stacked)


def forward(valid_len, packed):
    parts, _, tokens, _ = packed.shape
    total = parts * tokens
    half = tokens // HALVES
    span = BLOCK // half
    steps = total // BLOCK
    chunk = 512

    def body(
        len_ref, p_ref, e_ref, att_ref, qt_ref, inv_ref, kt_ref, va_ref, ka, vt, held, tops
    ):
        step = pl.program_id(0)
        length = len_ref[0]

        @pl.when(step == 0)
        def _():
            key_rows = p_ref[:, 1].reshape(total, HEAD_DIM)
            value_rows = p_ref[:, 2].reshape(total, HEAD_DIM)
            row = lax.broadcasted_iota(jnp.int32, (total, HEAD_DIM), 0)
            col = lax.broadcasted_iota(jnp.int32, (total, HEAD_DIM), 1)
            ka[:, :HEAD_DIM] = key_rows
            ka[:, HEAD_DIM:] = jnp.where((row >= length) & (col == 0), -1e30, 0.0).astype(BF16)
            vt[:HEAD_DIM, :] = value_rows.T
            vt[HEAD_DIM:, :] = jnp.ones((16, total), BF16)
            kt_ref[...] = key_rows.T
            va_ref[:, :HEAD_DIM] = value_rows
            va_ref[:, HEAD_DIM:] = jnp.where(col < 2, 1.0, 0.0).astype(BF16)

        def live(block):
            lane = lax.broadcasted_iota(jnp.int32, (1, BLOCK), 1)
            per_half = parts // span
            part = (block % per_half) * span + lane // half
            return part * tokens + (block // per_half) * half + lane % half < length

        def work(score_next, weigh_last):
            if score_next:
                per_half = parts // span
                query = p_ref[
                    pl.ds(step % per_half * span, span), 0, pl.ds(step // per_half * half, half), :
                ]
                query = query.reshape(BLOCK, HEAD_DIM).T
                qt_ref[...] = query
                row = lax.broadcasted_iota(jnp.int32, (HEAD_DIM, BLOCK), 0)
                extra = jnp.where(row == 0, 1.0, 0.0).astype(BF16)
                widened = jnp.concatenate([query, extra], axis=0)
                top = jnp.full((8, BLOCK), -3e38, F32)
            if weigh_last:
                shift = tops[0:1]
                summed = jnp.zeros((HEAD_DIM + 16, BLOCK), F32)
            for first in range(0, total, chunk):
                rows = slice(first, first + chunk)
                if weigh_last:
                    low = jnp.exp2(held[rows, :] * (SCALE * LOG2E) - shift).astype(BF16)
                    e_ref[rows, :] = low
                if score_next:
                    scores = contract(ka[rows, :], widened, 1, 0)
                    held[rows, :] = scores
                    top = jnp.maximum(top, jnp.max(scores.reshape(chunk // 8, 8, BLOCK), axis=0))
                if weigh_last:
                    summed = summed + contract(vt[:, rows], low, 1, 0)
            if weigh_last:
                inverse = jnp.where(live(step - 1), 1.0 / summed[HEAD_DIM : HEAD_DIM + 1], 0.0)
                att_ref[...] = (summed[:HEAD_DIM] * inverse).astype(BF16)
                inv_ref[...] = jnp.broadcast_to(inverse, (8, BLOCK))
            if score_next:
                top = jnp.max(top, axis=0, keepdims=True) * (SCALE * LOG2E)
                tops[...] = jnp.broadcast_to(jnp.where(live(step), top, 1e30), (8, BLOCK))

        pl.when(step == 0)(lambda: work(True, False))
        pl.when((step > 0) & (step < steps))(lambda: work(True, True))
        pl.when(step == steps)(lambda: work(False, True))

    whole = lambda i, n: (0, 0)
    scored = lambda i, n: (0, jnp.minimum(i, steps - 1))
    weighed = lambda i, n: (0, jnp.maximum(i - 1, 0))
    return pl.pallas_call(
        body,
        grid_spec=pltpu.PrefetchScalarGridSpec(
            num_scalar_prefetch=1,
            grid=(steps + 1,),
            in_specs=[
                pl.BlockSpec(memory_space=pltpu.VMEM),
            ],
            out_specs=[
                pl.BlockSpec((total, BLOCK), weighed),
                pl.BlockSpec((HEAD_DIM, BLOCK), weighed),
                pl.BlockSpec((HEAD_DIM, BLOCK), scored),
                pl.BlockSpec((8, BLOCK), weighed),
                pl.BlockSpec((HEAD_DIM, total), whole),
                pl.BlockSpec((total, 2 * HEAD_DIM), whole),
            ],
            scratch_shapes=[
                pltpu.VMEM((total, 2 * HEAD_DIM), BF16),
                pltpu.VMEM((HEAD_DIM + 16, total), BF16),
                pltpu.VMEM((total, BLOCK), F32),
                pltpu.VMEM((8, BLOCK), F32),
            ],
        ),
        out_shape=[
            jax.ShapeDtypeStruct((total, total), BF16),
            jax.ShapeDtypeStruct((HEAD_DIM, total), BF16),
            jax.ShapeDtypeStruct((HEAD_DIM, total), BF16),
            jax.ShapeDtypeStruct((8, total), F32),
            jax.ShapeDtypeStruct((HEAD_DIM, total), BF16),
            jax.ShapeDtypeStruct((total, 2 * HEAD_DIM), BF16),
        ],
        compiler_params=PARAMS,
        cost_estimate=pl.CostEstimate(
            flops=6 * total * total * HEAD_DIM,
            bytes_accessed=2 * total * total,
            transcendentals=total * total,
        ),
        name="forward",
    )(valid_len, packed)


def project(which, cotangent, gated, attended, inverse):
    count, width = cotangent.shape
    block = 1024
    steps = count // block

    def body(c_ref, w_ref, o_ref, inv_ref, g_ref, d_ref, a_ref):
        step = pl.program_id(0)
        rows = c_ref[...]
        grad = contract(w_ref[...], rows, 1, 1).astype(BF16).astype(F32)
        low = (grad * inv_ref[0:1]).astype(BF16)
        g_ref[...] = low
        out = o_ref[...]
        delta = jnp.sum(low.astype(F32) * out.astype(F32), axis=0, keepdims=True)
        d_ref[...] = jnp.broadcast_to(delta, (8, block))
        outer = contract(out, rows, 1, 0)

        @pl.when(step == 0)
        def _():
            a_ref[...] = outer

        @pl.when(step > 0)
        def _():
            a_ref[...] += outer

    column = lambda i: (0, i)
    shifted = lambda i: (0, i + which * steps)
    whole = lambda i: (0, 0)
    return pl.pallas_call(
        body,
        grid=(steps,),
        in_specs=[
            pl.BlockSpec((block, width), lambda i: (i, 0)),
            pl.BlockSpec((HEAD_DIM, width), whole),
            pl.BlockSpec((HEAD_DIM, block), shifted),
            pl.BlockSpec((8, block), shifted),
        ],
        out_specs=[
            pl.BlockSpec((HEAD_DIM, block), column),
            pl.BlockSpec((8, block), column),
            pl.BlockSpec((HEAD_DIM, width), whole),
        ],
        out_shape=[
            jax.ShapeDtypeStruct((HEAD_DIM, count), BF16),
            jax.ShapeDtypeStruct((8, count), F32),
            jax.ShapeDtypeStruct((HEAD_DIM, width), F32),
        ],
        compiler_params=PARAMS,
        cost_estimate=pl.CostEstimate(
            flops=4 * count * width * HEAD_DIM,
            bytes_accessed=2 * count * width,
            transcendentals=0,
        ),
        name="project",
    )(cotangent, gated, attended, inverse)


def backward(which, low, grad, delta, query, key, value, parts, earlier):
    total = low.shape[0]
    tokens = total // parts
    half = tokens // HALVES
    span = BLOCK // half
    steps = grad.shape[1] // BLOCK
    chunk = 1024
    final = which == HALVES - 1
    n_in = 6 + len(earlier)

    def body(*refs):
        e_ref, g_ref, d_ref, q_ref, k_ref, v_ref = refs[:6]
        before = refs[6:n_in]
        if final:
            o_ref, dk, dv = refs[n_in:]
        else:
            dq_ref, dk, dv = refs[n_in:]
        step = pl.program_id(0)

        @pl.when(step == 0)
        def _():
            if before:
                dk[...] = before[-2][...]
                dv[...] = before[-1][...]
            else:
                dk[...] = jnp.zeros_like(dk)
                dv[...] = jnp.zeros_like(dv)

        minus = -d_ref[0:1]
        high = minus.astype(BF16).astype(F32)
        row = lax.broadcasted_iota(jnp.int32, (HEAD_DIM, BLOCK), 0)
        extra = jnp.where(row == 0, high, jnp.where(row == 1, minus - high, 0.0)).astype(BF16)
        grad_block = g_ref[...]
        widened = jnp.concatenate([grad_block, extra], axis=0)
        grad_rows = grad_block.T
        query_rows = q_ref[...].T
        dq = jnp.zeros((HEAD_DIM, BLOCK), F32)
        for first in range(0, total, chunk):
            rows = slice(first, first + chunk)
            dprob = contract(v_ref[rows, :], widened, 1, 0)
            probs = e_ref[rows, :]
            dscore = (probs.astype(F32) * dprob).astype(BF16)
            dq = dq + contract(k_ref[:, rows], dscore, 1, 0)
            dv[rows, :] += contract(probs, grad_rows, 1, 0)
            dk[rows, :] += contract(dscore, query_rows, 1, 0)
        dq = (dq * SCALE).T.astype(BF16).reshape(span, half, HEAD_DIM)
        at = pl.ds(step * span, span)
        if final:
            o_ref[at, 0, which * half : (which + 1) * half, :] = dq

            @pl.when(step == steps - 1)
            def _():
                for index in range(which):
                    o_ref[:, 0, index * half : (index + 1) * half, :] = before[index][...]
                o_ref[:, 1] = (dk[...] * SCALE).astype(BF16).reshape(parts, tokens, HEAD_DIM)
                o_ref[:, 2] = dv[...].astype(BF16).reshape(parts, tokens, HEAD_DIM)

        else:
            dq_ref[at] = dq

    column = lambda i: (0, i)
    shifted = lambda i: (0, i + which * steps)
    whole = lambda i: (0, 0)
    sums = jax.ShapeDtypeStruct((total, HEAD_DIM), F32)
    if final:
        out_specs = pl.BlockSpec((parts, 3, tokens, HEAD_DIM), lambda i: (0, 0, 0, 0))
        out_shape = jax.ShapeDtypeStruct((parts, 3, tokens, HEAD_DIM), BF16)
        scratch = [pltpu.VMEM((total, HEAD_DIM), F32)] * 2
    else:
        out_specs = [
            pl.BlockSpec((parts, half, HEAD_DIM), lambda i: (0, 0, 0)),
            pl.BlockSpec((total, HEAD_DIM), whole),
            pl.BlockSpec((total, HEAD_DIM), whole),
        ]
        out_shape = [jax.ShapeDtypeStruct((parts, half, HEAD_DIM), BF16), sums, sums]
        scratch = []
    return pl.pallas_call(
        body,
        grid=(steps,),
        in_specs=[
            pl.BlockSpec((total, BLOCK), shifted),
            pl.BlockSpec((HEAD_DIM, BLOCK), column),
            pl.BlockSpec((8, BLOCK), column),
            pl.BlockSpec((HEAD_DIM, BLOCK), shifted),
            pl.BlockSpec((HEAD_DIM, total), whole),
            pl.BlockSpec((total, 2 * HEAD_DIM), whole),
        ]
        + [
            pl.BlockSpec(memory_space=pltpu.VMEM) for _ in earlier
        ],
        out_specs=out_specs,
        out_shape=out_shape,
        scratch_shapes=scratch,
        compiler_params=PARAMS,
        cost_estimate=pl.CostEstimate(
            flops=10 * total * total * HEAD_DIM // HALVES,
            bytes_accessed=2 * total * total // HALVES,
            transcendentals=0,
        ),
        name="backward",
    )(low, grad, delta, query, key, value, *earlier)


def swap(values, axis, size, bit):
    return lax.ppermute(values, axis, [(i, i ^ bit) for i in range(size)])


def total_over(values, axis, size):
    bit = 1
    while bit < size:
        values = values + swap(values, axis, size, bit)
        bit *= 2
    return values


def scatter_over(values, axis, size):
    bit = size // 2
    while bit:
        upper = lax.axis_index(axis) // bit % 2
        keep = lax.dynamic_slice_in_dim(values, upper * bit, bit, 0)
        give = lax.dynamic_slice_in_dim(values, (1 - upper) * bit, bit, 0)
        values = keep + swap(give, axis, size, bit)
        bit //= 2
    return values[0]


def shards(
    queries, key_rows, value_rows, cotangent, attn_gate, lengths, w_out, row_moment, col_moment
):
    seq_size = lax.axis_size("seq")
    dp_size = lax.axis_size("dp")
    inner_dim = queries.shape[2]
    width_dim = cotangent.shape[2]
    columns = width_dim // dp_size
    half = queries.shape[1] // HALVES
    gate = attn_gate[0][None, :]
    every = [
        lax.all_gather(cotangent[0, i * half : (i + 1) * half], "seq", axis=0, tiled=True)
        for i in range(HALVES)
    ]
    packed = split_columns([queries[0], key_rows[0], value_rows[0]])
    packed = lax.all_to_all(packed, "seq", 0, 0, tiled=True)
    weight = w_out.astype(F32)
    gated = (weight * gate).astype(BF16)
    low, attended, query, inverse, key, value = forward(lengths, packed)

    earlier, sums, outer = [], [], 0.0
    for which in range(HALVES):
        grad, delta, part = project(which, every[which], gated, attended, inverse)
        outer = outer + part
        back = backward(
            which, low, grad, delta, query, key, value, seq_size, earlier + sums
        )
        if which < HALVES - 1:
            earlier.append(back[0])
            sums = list(back[1:])
    back = lax.all_to_all(back, "seq", 0, 0, tiled=True)

    partial = (outer * gate).reshape(HEAD_DIM, dp_size, columns).transpose(1, 0, 2)
    grad_weight = scatter_over(partial, "dp", dp_size)
    squares = grad_weight * grad_weight + EPSILON
    gate_part = jnp.sum(weight * outer, axis=0)
    row_total = total_over(jnp.sum(squares, axis=1), "dp", dp_size)
    joined = jnp.concatenate([jnp.sum(squares, axis=0), gate_part])
    joined = total_over(joined, "seq", seq_size)
    row_new = 0.8 * row_moment + 0.2 * (row_total / width_dim)
    col_new = 0.8 * col_moment + 0.2 * (joined[:columns] / inner_dim)
    grad_q, grad_k, grad_v = join_columns(back)
    return (
        grad_q[None],
        grad_k[None],
        grad_v[None],
        joined[columns:][None],
        grad_weight,
        row_new,
        col_new,
    )


def solution(mesh):
    tokens = P("dp", "seq", None)
    return jax.shard_map(
        shards,
        mesh=mesh,
        in_specs=(
            tokens,
            tokens,
            tokens,
            tokens,
            P("dp", None),
            P("dp"),
            P("seq", None),
            P("seq"),
            P("dp"),
        ),
        out_specs=(
            tokens,
            tokens,
            tokens,
            P("dp", None),
            P("seq", "dp"),
            P("seq"),
            P("dp"),
        ),
        check_vma=False,
    )
```

time: 264 us -> 273 us (1.034)
  blocking collectives: 9.09 us -> 0 us
  waiting for transfers between devices: 111 us -> 119 us
  other arithmetic: 3.53 us -> 8.79 us
  local copies, waits for them, and re-layouts: 5.57 us -> 10.7 us
  starting transfers between devices: 24.6 us -> 28.6 us
  Pallas kernels: 93.5 us -> 90.3 us
    all_to_all x1, waiting for transfers between devices: 37.2 us -> 0.01 us  [shards(): back = lax.all_to_all(back, 'seq', 0, 0, tiled=True)]
    ppermute x0 -> x10, waiting for transfers between devices: none -> 36 us  [swap(): return lax.ppermute(values, axis, [(i, i ^ bit) for i in range(size)])]
    all_gather x1 -> x2, waiting for transfers between devices: 0.01 us -> 17.3 us  [shards(): lax.all_gather(cotangent[0, i * half:(i + 1) * half], 'seq', axis=0, tile...]
    ppermute x0 -> x10, starting transfers between devices: none -> 16.9 us  [swap(): return lax.ppermute(values, axis, [(i, i ^ bit) for i in range(size)])]
    all_to_all x2 -> x0, starting transfers between devices: 14.1 us -> none  [the longest x1 7.2 us: total_over(): return jnp.sum(lax.all_to_all(spread, axis, 0, 0, tiled=True), axis=0)]
    pallas_call x1, Pallas kernels: 33.9 us -> 23.3 us  [forward(): pl.pallas_call(body, grid_spec=pltpu.PrefetchScalarGridSpec(num_scalar_pr...]
    all_to_all x1 -> x0, blocking collectives: 9.09 us -> none  [total_over(): return jnp.sum(lax.all_to_all(spread, axis, 0, 0, tiled=True), axis=0)]
    all_to_all x2 -> x0, waiting for transfers between devices: 7.5 us -> none  [the longest x1 7.5 us: total_over(): return jnp.sum(lax.all_to_all(spread, axis, 0, 0, tiled=True), axis=0)]
  transfers between devices with their start and end apart: 5 -> 14, of which waited for: 3 -> 10; matrix products, arithmetic and copies ran while one was open for 1% -> 5% of each run, Pallas kernels for 30% -> 13%
where the time goes in v3:
time: 273 us; the launch traced here: 272 us
  waiting for transfers between devices  119 us (44%)
  Pallas kernels  90.3 us (33%)
  starting transfers between devices  28.6 us (10%)
  between operations  14.8 us (5%)
  local copies, waits for them, and re-layouts  10.7 us (4%)
  other arithmetic  8.79 us (3%)
    all_to_all x1, waiting for transfers between devices, shards(): packed = lax.all_to_all(packed, 'seq', 0, 0, tiled=True)  65.1 us
    pallas_call x2, Pallas kernels, backward(): pl.pallas_call(body, grid=(steps,), in_specs=[pl.BlockSpec((total, BLOCK)...  45.5 us
    ppermute x10, waiting for transfers between devices, swap(): return lax.ppermute(values, axis, [(i, i ^ bit) for i in range(size)])  36 us
    pallas_call x1, Pallas kernels, forward(): pl.pallas_call(body, grid_spec=pltpu.PrefetchScalarGridSpec(num_scalar_pr...  23.3 us
    all_gather x2, waiting for transfers between devices, shards(): lax.all_gather(cotangent[0, i * half:(i + 1) * half], 'seq', axis=0, tile...  17.3 us
    ppermute x10, starting transfers between devices, swap(): return lax.ppermute(values, axis, [(i, i ^ bit) for i in range(size)])  16.9 us
    pallas_call x2, Pallas kernels, project(): pl.pallas_call(body, grid=(steps,), in_specs=[pl.BlockSpec((block, width)...  13 us
    all_to_all x1, starting transfers between devices, shards(): packed = lax.all_to_all(packed, 'seq', 0, 0, tiled=True)  6.65 us
  transfers between devices with their start and end apart: 14, of which 10 were waited for; matrix products, arithmetic and copies ran while one was open for 5% of the time, Pallas kernels for 13%

profile of v3, /device:TPU:0, one launch (start us, length us, event | category | flops | bytes accessed | tf_op | source)
XLA Modules:
  0.0 272.4 jit_solution(15569323882988429537)
XLA Ops:
  7.2 2.1 fusion.5
  10.1 4.4 %split_columns.1 = bf16[16,3,256,128]{3,2,1,0:T(8,128)(2,1)} custom-call(bf16[256,2048]{1,0:T(8,128)(2,1)} %bitcast.20, bf16[256,2048]{1,0:T(8,128)(2,1)} %bitcast.21, bf16[256,2048]{1,0:T(8,128)(2,1)} %bitcast.22), custom_call_target="tpu_custom_call" | custom-call | tf_op jit(solution)/shard_map/split_columns/pallas_call | solution.py:37
  14.4 6.6 %all-to-all-start = ((bf16[16,3,256,128]{3,2,1,0:T(8,128)(2,1)}), bf16[16,3,256,128]{3,2,1,0:T(8,128)(2,1)S(1)}, u32[]{:S(2)}, u32[]{:S(2)}) async-start(bf16[16,3,256,128]{3,2,1,0:T(8,128)(2,1)} %split_columns.1), calls=%async_computation | async-start | bytes 6291456 | tf_op jit(solution)/shard_map/all_to_all | solution.py:383
  22.6 65.1 %all-to-all-done.p_ref = bf16[16,3,256,128]{3,2,1,0:T(8,128)(2,1)S(1)} async-done(((bf16[16,3,256,128]{3,2,1,0:T(8,128)(2,1)}), bf16[16,3,256,128]{3,2,1,0:T(8,128)(2,1)S(1)}, u32[]{:S(2)}, u32[]{:S(2)}) %all-to-all-start) | async-done | bytes 3145760 | tf_op jit(solution)/shard_map/all_to_all | solution.py:383
  87.7 1.6 copy-done.1
  89.3 23.3 %forward.1 = (bf16[4096,4096]{1,0:T(8,128)(2,1)}, bf16[128,4096]{1,0:T(8,128)(2,1)}, bf16[128,4096]{1,0:T(8,128)(2,1)}, f32[8,4096]{1,0:T(8,128)}, bf16[128,4096]{1,0:T(8,128)(2,1)}, /*index=5*/bf16[4096,256]{1,0:T(8,128)(2,1)}) custom-call(s32[1]{0:T(128)S(6)} %copy.19.len_ref, bf16[16,3,256,128]{3,2,1,0:T(8,128)(2,1)} %copy-done.1), custom_call_target="tpu_custom_call" | custom-call | flops 12884901888 | bytes 33554432 | tf_op jit(solution)/shard_map/forward/pallas_call | solution.py:145
  112.7 6.5 %project.2 = (bf16[128,2048]{1,0:T(8,128)(2,1)}, f32[8,2048]{1,0:T(8,128)}, f32[128,1536]{1,0:T(8,128)}) custom-call(bf16[2048,1536]{1,0:T(8,128)(2,1)} %bitcast.16, bf16[128,1536]{1,0:T(8,128)(2,1)} %fusion.w_ref, bf16[128,4096]{1,0:T(8,128)(2,1)} %get-tuple-element.26.o_ref, f32[8,4096]{1,0:T(8,128)} %get-tuple-element.27.inv_ref), custom_call_target="tpu_custom_call" | custom-call | flops 1610612736 | bytes 6291456 | tf_op jit(solution)/shard_map/project/pallas_call | solution.py:213
  119.2 17.3 %all-gather.7.cloned.1.call-done = bf16[1,2048,1536]{2,1,0:T(8,128)(2,1)} async-done(((bf16[1,128,1536]{2,1,0:T(8,128)(2,1)}), bf16[1,2048,1536]{2,1,0:T(8,128)(2,1)}) %all-gather.7.cloned.1.call-update) | async-done | bytes 6291472 | tf_op jit(solution)/shard_map/all_gather | solution.py:379
  136.5 6.4 %project.3 = (bf16[128,2048]{1,0:T(8,128)(2,1)}, f32[8,2048]{1,0:T(8,128)}, f32[128,1536]{1,0:T(8,128)}) custom-call(bf16[2048,1536]{1,0:T(8,128)(2,1)} %bitcast.17, bf16[128,1536]{1,0:T(8,128)(2,1)} %fusion.w_ref, bf16[128,4096]{1,0:T(8,128)(2,1)} %get-tuple-element.26.o_ref, f32[8,4096]{1,0:T(8,128)} %get-tuple-element.27.inv_ref), custom_call_target="tpu_custom_call" | custom-call | flops 1610612736 | bytes 6291456 | tf_op jit(solution)/shard_map/project/pallas_call | solution.py:213
  143.0 22.1 %backward.2 = (bf16[16,128,128]{2,1,0:T(8,128)(2,1)}, f32[4096,128]{1,0:T(8,128)}, f32[4096,128]{1,0:T(8,128)}) custom-call(bf16[4096,4096]{1,0:T(8,128)(2,1)} %get-tuple-element.25.refs_0_, bf16[128,2048]{1,0:T(8,128)(2,1)} %get-tuple-element.33.refs_1_, f32[8,2048]{1,0:T(8,128)} %get-tuple-element.34.refs_2_, bf16[128,4096]{1,0:T(8,128)(2,1)} %get-tuple-element.30.refs_3_, ...), custom_call_target="tpu_custom_call" | custom-call | flops 10737418240 | bytes 16777216 | tf_op jit(solution)/shard_map/backward/pallas_call | solution.py:318
  165.0 23.4 %backward.3 = bf16[16,3,256,128]{3,2,1,0:T(8,128)(2,1)} custom-call(bf16[4096,4096]{1,0:T(8,128)(2,1)} %get-tuple-element.25.refs_0_, bf16[128,2048]{1,0:T(8,128)(2,1)} %get-tuple-element.28.refs_1_, f32[8,2048]{1,0:T(8,128)} %get-tuple-element.29.refs_2_, bf16[128,4096]{1,0:T(8,128)(2,1)} %get-tuple-element.30.refs_3_, ...), custom_call_target="tpu_custom_call" | custom-call | flops 10737418240 | bytes 16777216 | tf_op jit(solution)/shard_map/backward/pallas_call | solution.py:318
  188.4 5.0 %all-to-all-start.1 = ((bf16[16,3,256,128]{3,2,1,0:T(8,128)(2,1)}), bf16[16,3,256,128]{3,2,1,0:T(8,128)(2,1)S(1)}, u32[]{:S(2)}, u32[]{:S(2)}) async-start(bf16[16,3,256,128]{3,2,1,0:T(8,128)(2,1)} %backward.3), calls=%async_computation.1 | async-start | bytes 6291456 | tf_op jit(solution)/shard_map/all_to_all | solution.py:398
  193.5 2.4 broadcast_multiply_fusion
  195.9 2.3 copy.18
  199.2 3.1 %collective-permute-start = (f32[4,128,192]{1,2,0:T(8,128)S(1)}, f32[4,128,192]{1,2,0:T(8,128)}, u32[]{:S(2)}, u32[]{:S(2)}) collective-permute-start(f32[4,128,192]{1,2,0:T(8,128)S(1)} %dynamic-slice_bitcast_fusion), channel_id=1, source_target_pairs={{0,64},{16,80},{32,96},{48,112},{64,0},{80,16},{96,32},{112,48},{1... | collective-permute-start | bytes 1179656 | tf_op jit(solution)/shard_map/ppermute | solution.py:346
  202.3 10.0 %collective-permute-done = f32[4,128,192]{1,2,0:T(8,128)} collective-permute-done((f32[4,128,192]{1,2,0:T(8,128)S(1)}, f32[4,128,192]{1,2,0:T(8,128)}, u32[]{:S(2)}, u32[]{:S(2)}) %collective-permute-start) | collective-permute-done | bytes 393248 | tf_op jit(solution)/shard_map/ppermute | solution.py:346
  212.3 1.2 bitcast_add_fusion
  214.1 1.5 collective-permute-start.1
  215.6 5.2 %collective-permute-done.1 = f32[2,128,192]{1,2,0:T(8,128)} collective-permute-done((f32[2,128,192]{1,2,0:T(8,128)}, f32[2,128,192]{1,2,0:T(8,128)}, u32[]{:S(2)}, u32[]{:S(2)}) %collective-permute-start.1) | collective-permute-done | bytes 196640 | tf_op jit(solution)/shard_map/ppermute | solution.py:346
  222.4 2.8 %collective-permute-start.2 = (f32[1,128,192]{1,2,0:T(8,128)S(1)}, f32[1,128,192]{1,2,0:T(8,128)S(1)}, u32[]{:S(2)}, u32[]{:S(2)}) collective-permute-start(f32[1,128,192]{1,2,0:T(8,128)S(1)} %constant_dynamic-slice_fusion), channel_id=1, source_target_pairs={{0,16},{16,0},{32,48},{48,32},{64,80},{80,64},{96,112},{112,96},{1... | collective-permute-start | bytes 294920 | tf_op jit(solution)/shard_map/ppermute | solution.py:346
  225.2 9.6 %collective-permute-done.2 = f32[1,128,192]{1,2,0:T(8,128)S(1)} collective-permute-done((f32[1,128,192]{1,2,0:T(8,128)S(1)}, f32[1,128,192]{1,2,0:T(8,128)S(1)}, u32[]{:S(2)}, u32[]{:S(2)}) %collective-permute-start.2) | collective-permute-done | bytes 98336 | tf_op jit(solution)/shard_map/ppermute | solution.py:346
  234.8 1.5 fusion.2
  236.5 1.2 collective-permute-done.3
  238.6 2.8 %collective-permute-done.4 = f32[1728]{0:T(1024)S(1)} collective-permute-done((f32[1728]{0:T(1024)S(1)}, f32[1728]{0:T(1024)S(1)}, u32[]{:S(2)}, u32[]{:S(2)}) %collective-permute-start.4) | collective-permute-done | bytes 6944 | tf_op jit(solution)/shard_map/ppermute | solution.py:346
  242.7 4.1 %collective-permute-done.7 = f32[128]{0:T(128)S(1)} collective-permute-done((f32[128]{0:T(128)S(1)}, f32[128]{0:T(128)S(1)}, u32[]{:S(2)}, u32[]{:S(2)}) %collective-permute-start.7) | collective-permute-done | bytes 544 | tf_op jit(solution)/shard_map/ppermute | solution.py:346
  246.8 1.4 collective-permute-start.8
  248.3 2.1 collective-permute-done.8
  250.4 3.0 %collective-permute-start.9 = (f32[128]{0:T(128)S(1)}, f32[128]{0:T(128)S(1)}, u32[]{:S(2)}, u32[]{:S(2)}) collective-permute-start(f32[128]{0:T(128)S(1)} %add.97), channel_id=1, source_target_pairs={{0,64},{16,80},{32,96},{48,112},{64,0},{80,16},{96,32},{112,48},{1... | collective-permute-start | bytes 1544 | tf_op jit(solution)/shard_map/ppermute | solution.py:346
  253.4 2.9 %collective-permute-start.6 = (f32[1728]{0:T(1024)S(1)}, f32[1728]{0:T(1024)S(1)}, u32[]{:S(2)}, u32[]{:S(2)}) collective-permute-start(f32[1728]{0:T(1024)S(1)} %add.94), channel_id=1, source_target_pairs={{0,8},{1,9},{2,10},{3,11},{4,12},{5,13},{6,14},{7,15},{8,0},{9,1},... | collective-permute-start | bytes 20744 | tf_op jit(solution)/shard_map/ppermute | solution.py:346
  256.3 1.2 multiply_add_fusion.1
  259.8 1.6 copy-done
  261.4 4.2 %join_columns.1 = (bf16[256,2048]{1,0:T(8,128)(2,1)}, bf16[256,2048]{1,0:T(8,128)(2,1)}, bf16[256,2048]{1,0:T(8,128)(2,1)}) custom-call(bf16[16,3,256,128]{3,2,1,0:T(8,128)(2,1)} %copy-done), custom_call_target="tpu_custom_call" | custom-call | tf_op jit(solution)/shard_map/join_columns/pallas_call | solution.py:60
  (39 shorter events, 9.7 us)
Async XLA Ops:
  7.2 105.5 %all-gather.5.cloned.1.call-start = ((), (), s32[]{:S(2)}) async-start(), calls=%async_computation.2 | async-start | bytes 6684672 | tf_op jit(solution)/shard_map/all_gather | solution.py:379
  9.3 127.2 %all-gather.7.cloned.1.call-start = ((), (), s32[]{:S(2)}) async-start(), calls=%async_computation.3 | async-start | bytes 6684672 | tf_op jit(solution)/shard_map/all_gather | solution.py:379
  14.4 7.3 %copy-start.4 = (f32[1,1536]{1,0:T(1,128)S(1)}, f32[1,1536]{1,0:T(1,128)}, u32[]{:S(2)}) copy-start(f32[1,1536]{1,0:T(1,128)} %param.13) | copy-start | bytes 18436
  14.4 7.3 %copy-start.2 = (bf16[128,1536]{1,0:T(8,128)(2,1)S(1)}, bf16[128,1536]{1,0:T(8,128)(2,1)}, u32[]{:S(2)}) copy-start(bf16[128,1536]{1,0:T(8,128)(2,1)} %param.15) | copy-start | bytes 1179652
  14.4 73.3 %all-to-all-start = ((bf16[16,3,256,128]{3,2,1,0:T(8,128)(2,1)}), bf16[16,3,256,128]{3,2,1,0:T(8,128)(2,1)S(1)}, u32[]{:S(2)}, u32[]{:S(2)}) async-start(bf16[16,3,256,128]{3,2,1,0:T(8,128)(2,1)} %split_columns.1), calls=%async_computation | async-start | bytes 6291456 | tf_op jit(solution)/shard_map/all_to_all | solution.py:383
  87.7 1.6 copy-start.1
  188.4 71.3 %all-to-all-start.1 = ((bf16[16,3,256,128]{3,2,1,0:T(8,128)(2,1)}), bf16[16,3,256,128]{3,2,1,0:T(8,128)(2,1)S(1)}, u32[]{:S(2)}, u32[]{:S(2)}) async-start(bf16[16,3,256,128]{3,2,1,0:T(8,128)(2,1)} %backward.3), calls=%async_computation.1 | async-start | bytes 6291456 | tf_op jit(solution)/shard_map/all_to_all | solution.py:398
  195.9 63.3 %copy-start.5 = (f32[192]{0:T(256)S(1)}, f32[192]{0:T(256)}, u32[]{:S(2)}) copy-start(f32[192]{0:T(256)} %param.17) | copy-start | bytes 2308
  199.2 13.1 %collective-permute-start = (f32[4,128,192]{1,2,0:T(8,128)S(1)}, f32[4,128,192]{1,2,0:T(8,128)}, u32[]{:S(2)}, u32[]{:S(2)}) collective-permute-start(f32[4,128,192]{1,2,0:T(8,128)S(1)} %dynamic-slice_bitcast_fusion), channel_id=1, source_target_pairs={{0,64},{16,80},{32,96},{48,112},{64,0},{80,16},{96,32},{112,48},{1... | collective-permute-start | bytes 1179656 | tf_op jit(solution)/shard_map/ppermute | solution.py:346
  214.1 6.7 %collective-permute-start.1 = (f32[2,128,192]{1,2,0:T(8,128)}, f32[2,128,192]{1,2,0:T(8,128)}, u32[]{:S(2)}, u32[]{:S(2)}) collective-permute-start(f32[2,128,192]{1,2,0:T(8,128)} %constant_dynamic-slice_fusion.1), channel_id=1, source_target_pairs={{0,32},{16,48},{32,0},{48,16},{64,96},{80,112},{96,64},{112,80},{1... | collective-permute-start | bytes 589832 | tf_op jit(solution)/shard_map/ppermute | solution.py:346
  221.8 0.7 copy-start.3
  222.4 12.4 %collective-permute-start.2 = (f32[1,128,192]{1,2,0:T(8,128)S(1)}, f32[1,128,192]{1,2,0:T(8,128)S(1)}, u32[]{:S(2)}, u32[]{:S(2)}) collective-permute-start(f32[1,128,192]{1,2,0:T(8,128)S(1)} %constant_dynamic-slice_fusion), channel_id=1, source_target_pairs={{0,16},{16,0},{32,48},{48,32},{64,80},{80,64},{96,112},{112,96},{1... | collective-permute-start | bytes 294920 | tf_op jit(solution)/shard_map/ppermute | solution.py:346
  236.5 1.2 collective-permute-start.3
  237.7 3.7 %collective-permute-start.4 = (f32[1728]{0:T(1024)S(1)}, f32[1728]{0:T(1024)S(1)}, u32[]{:S(2)}, u32[]{:S(2)}) collective-permute-start(f32[1728]{0:T(1024)S(1)} %fusion.6), channel_id=1, source_target_pairs={{0,2},{1,3},{2,0},{3,1},{4,6},{5,7},{6,4},{7,5},{8,10},{9,11},{10,... | collective-permute-start | bytes 20744 | tf_op jit(solution)/shard_map/ppermute | solution.py:346
  241.4 12.0 %collective-permute-start.5 = (f32[1728]{0:T(1024)S(1)}, f32[1728]{0:T(1024)S(1)}, u32[]{:S(2)}, u32[]{:S(2)}) collective-permute-start(f32[1728]{0:T(1024)S(1)} %add.93), channel_id=1, source_target_pairs={{0,4},{1,5},{2,6},{3,7},{4,0},{5,1},{6,2},{7,3},{8,12},{9,13},{10,... | collective-permute-start | bytes 20744 | tf_op jit(solution)/shard_map/ppermute | solution.py:346
  241.8 5.0 %collective-permute-start.7 = (f32[128]{0:T(128)S(1)}, f32[128]{0:T(128)S(1)}, u32[]{:S(2)}, u32[]{:S(2)}) collective-permute-start(f32[128]{0:T(128)S(1)} %get-tuple-element.43), channel_id=1, source_target_pairs={{0,16},{16,0},{32,48},{48,32},{64,80},{80,64},{96,112},{112,96},{1... | collective-permute-start | bytes 1544 | tf_op jit(solution)/shard_map/ppermute | solution.py:346
  246.8 3.5 %collective-permute-start.8 = (f32[128]{0:T(128)S(1)}, f32[128]{0:T(128)S(1)}, u32[]{:S(2)}, u32[]{:S(2)}) collective-permute-start(f32[128]{0:T(128)S(1)} %add.96), channel_id=1, source_target_pairs={{0,32},{16,48},{32,0},{48,16},{64,96},{80,112},{96,64},{112,80},{1... | collective-permute-start | bytes 1544 | tf_op jit(solution)/shard_map/ppermute | solution.py:346
  250.4 5.9 %collective-permute-start.9 = (f32[128]{0:T(128)S(1)}, f32[128]{0:T(128)S(1)}, u32[]{:S(2)}, u32[]{:S(2)}) collective-permute-start(f32[128]{0:T(128)S(1)} %add.97), channel_id=1, source_target_pairs={{0,64},{16,80},{32,96},{48,112},{64,0},{80,16},{96,32},{112,48},{1... | collective-permute-start | bytes 1544 | tf_op jit(solution)/shard_map/ppermute | solution.py:346
  253.4 5.2 %collective-permute-start.6 = (f32[1728]{0:T(1024)S(1)}, f32[1728]{0:T(1024)S(1)}, u32[]{:S(2)}, u32[]{:S(2)}) collective-permute-start(f32[1728]{0:T(1024)S(1)} %add.94), channel_id=1, source_target_pairs={{0,8},{1,9},{2,10},{3,11},{4,12},{5,13},{6,14},{7,15},{8,0},{9,1},... | collective-permute-start | bytes 20744 | tf_op jit(solution)/shard_map/ppermute | solution.py:346
  259.8 1.6 copy-start
Sparse Core Ops, SparseCore 0:
  9.7 79.7 all-gather.4
  91.2 45.2 all-gather.6

commit v4 on v3

--- a/solution.py
+++ b/solution.py
@@ -10,10 +10,9 @@
 LOG2E = 1.4426950408889634
 EPSILON = 1e-30
 BLOCK = 512
-HALVES = 2
 BF16 = jnp.bfloat16
 F32 = jnp.float32
-PARAMS = pltpu.CompilerParams(vmem_limit_bytes=56 * 2**20)
+PARAMS = pltpu.CompilerParams(vmem_limit_bytes=40 * 2**20)
 
 
 def contract(left, right, left_dim, right_dim):
@@ -63,6 +62,7 @@
         in_specs=[pl.BlockSpec(memory_space=pltpu.VMEM)],
         out_specs=[pl.BlockSpec((block, inner), lambda i: (i, 0))] * count,
         out_shape=[jax.ShapeDtypeStruct((tokens, inner), BF16)] * count,
+        compiler_params=pltpu.CompilerParams(vmem_limit_bytes=12 * 2**20),
         name="join_columns",
     )(stacked)
 
@@ -70,8 +70,7 @@
 def forward(valid_len, packed):
     parts, _, tokens, _ = packed.shape
     total = parts * tokens
-    half = tokens // HALVES
-    span = BLOCK // half
+    span = BLOCK // tokens
     steps = total // BLOCK
     chunk = 512
 
@@ -96,17 +95,12 @@
             va_ref[:, HEAD_DIM:] = jnp.where(col < 2, 1.0, 0.0).astype(BF16)
 
         def live(block):
-            lane = lax.broadcasted_iota(jnp.int32, (1, BLOCK), 1)
-            per_half = parts // span
-            part = (block % per_half) * span + lane // half
-            return part * tokens + (block // per_half) * half + lane % half < length
+            slot = block * BLOCK + lax.broadcasted_iota(jnp.int32, (1, BLOCK), 1)
+            return slot < length
 
         def work(score_next, weigh_last):
             if score_next:
-                per_half = parts // span
-                query = p_ref[
-                    pl.ds(step % per_half * span, span), 0, pl.ds(step // per_half * half, half), :
-                ]
+                query = p_ref[pl.ds(step * span, span), 0]
                 query = query.reshape(BLOCK, HEAD_DIM).T
                 qt_ref[...] = query
                 row = lax.broadcasted_iota(jnp.int32, (HEAD_DIM, BLOCK), 0)
@@ -183,89 +177,73 @@
     )(valid_len, packed)
 
 
-def project(which, cotangent, gated, attended, inverse):
-    count, width = cotangent.shape
-    block = 1024
-    steps = count // block
-
-    def body(c_ref, w_ref, o_ref, inv_ref, g_ref, d_ref, a_ref):
+def project(places, pieces, gated, attended, inverse):
+    width = gated.shape[1]
+    total = attended.shape[1]
+    count = len(pieces)
+
+    def body(*refs):
+        place_ref, sources = refs[0], refs[1 : 1 + count]
+        w_ref, o_ref, inv_ref, g_ref, d_ref, a_ref = refs[1 + count : 7 + count]
+        buffers, sems = refs[7 + count : 7 + 2 * count], refs[7 + 2 * count]
+        copies = [
+            pltpu.make_async_copy(sources[i], buffers[i], sems.at[i]) for i in range(count)
+        ]
+        for copy in copies:
+            copy.start()
+        outer = jnp.zeros((HEAD_DIM, width), F32)
+        for i in range(count):
+            size = pieces[i][0].shape[0]
+            lanes = pl.ds(pl.multiple_of(place_ref[pieces[i][1]], HEAD_DIM), size)
+            copies[i].wait()
+            rows = buffers[i][...]
+            grad = contract(w_ref[...], rows, 1, 1).astype(BF16).astype(F32)
+            low = (grad * inv_ref[0:1, lanes]).astype(BF16)
+            g_ref[:, lanes] = low
+            out = o_ref[:, lanes]
+            delta = jnp.sum(low.astype(F32) * out.astype(F32), axis=0, keepdims=True)
+            d_ref[:, lanes] = jnp.broadcast_to(delta, (8, size))
+            outer = outer + contract(out, rows, 1, 0)
+        a_ref[...] = outer
+
+    vmem = pl.BlockSpec(memory_space=pltpu.VMEM)
+    return pl.pallas_call(
+        body,
+        in_specs=[pl.BlockSpec(memory_space=pltpu.SMEM)]
+        + [pl.BlockSpec(memory_space=pl.ANY)] * count
+        + [vmem] * 3,
+        out_specs=[vmem] * 3,
+        out_shape=[
+            jax.ShapeDtypeStruct((HEAD_DIM, total), BF16),
+            jax.ShapeDtypeStruct((8, total), F32),
+            jax.ShapeDtypeStruct((HEAD_DIM, width), F32),
+        ],
+        scratch_shapes=[pltpu.VMEM(rows.shape, BF16) for rows, _ in pieces]
+        + [pltpu.SemaphoreType.DMA((count,))],
+        compiler_params=PARAMS,
+        cost_estimate=pl.CostEstimate(
+            flops=4 * total * width * HEAD_DIM,
+            bytes_accessed=2 * total * width,
+            transcendentals=0,
+        ),
+        name="project",
+    )(places, *[rows for rows, _ in pieces], gated, attended, inverse)
+
+
+def backward(low, grad, delta, query, key, value, parts):
+    total = low.shape[0]
+    tokens = total // parts
+    span = BLOCK // tokens
+    steps = total // BLOCK
+    chunk = 1024
+
+    def body(e_ref, g_ref, d_ref, q_ref, k_ref, v_ref, o_ref, dk, dv):
         step = pl.program_id(0)
-        rows = c_ref[...]
-        grad = contract(w_ref[...], rows, 1, 1).astype(BF16).astype(F32)
-        low = (grad * inv_ref[0:1]).astype(BF16)
-        g_ref[...] = low
-        out = o_ref[...]
-        delta = jnp.sum(low.astype(F32) * out.astype(F32), axis=0, keepdims=True)
-        d_ref[...] = jnp.broadcast_to(delta, (8, block))
-        outer = contract(out, rows, 1, 0)
 
         @pl.when(step == 0)
         def _():
-            a_ref[...] = outer
-
-        @pl.when(step > 0)
-        def _():
-            a_ref[...] += outer
-
-    column = lambda i: (0, i)
-    shifted = lambda i: (0, i + which * steps)
-    whole = lambda i: (0, 0)
-    return pl.pallas_call(
-        body,
-        grid=(steps,),
-        in_specs=[
-            pl.BlockSpec((block, width), lambda i: (i, 0)),
-            pl.BlockSpec((HEAD_DIM, width), whole),
-            pl.BlockSpec((HEAD_DIM, block), shifted),
-            pl.BlockSpec((8, block), shifted),
-        ],
-        out_specs=[
-            pl.BlockSpec((HEAD_DIM, block), column),
-            pl.BlockSpec((8, block), column),
-            pl.BlockSpec((HEAD_DIM, width), whole),
-        ],
-        out_shape=[
-            jax.ShapeDtypeStruct((HEAD_DIM, count), BF16),
-            jax.ShapeDtypeStruct((8, count), F32),
-            jax.ShapeDtypeStruct((HEAD_DIM, width), F32),
-        ],
-        compiler_params=PARAMS,
-        cost_estimate=pl.CostEstimate(
-            flops=4 * count * width * HEAD_DIM,
-            bytes_accessed=2 * count * width,
-            transcendentals=0,
-        ),
-        name="project",
-    )(cotangent, gated, attended, inverse)
-
-
-def backward(which, low, grad, delta, query, key, value, parts, earlier):
-    total = low.shape[0]
-    tokens = total // parts
-    half = tokens // HALVES
-    span = BLOCK // half
-    steps = grad.shape[1] // BLOCK
-    chunk = 1024
-    final = which == HALVES - 1
-    n_in = 6 + len(earlier)
-
-    def body(*refs):
-        e_ref, g_ref, d_ref, q_ref, k_ref, v_ref = refs[:6]
-        before = refs[6:n_in]
-        if final:
-            o_ref, dk, dv = refs[n_in:]
-        else:
-            dq_ref, dk, dv = refs[n_in:]
-        step = pl.program_id(0)
-
-        @pl.when(step == 0)
-        def _():
-            if before:
-                dk[...] = before[-2][...]
-                dv[...] = before[-1][...]
-            else:
-                dk[...] = jnp.zeros_like(dk)
-                dv[...] = jnp.zeros_like(dv)
+            dk[...] = jnp.zeros_like(dk)
+            dv[...] = jnp.zeros_like(dv)
 
         minus = -d_ref[0:1]
         high = minus.astype(BF16).astype(F32)
@@ -284,62 +262,38 @@
             dq = dq + contract(k_ref[:, rows], dscore, 1, 0)
             dv[rows, :] += contract(probs, grad_rows, 1, 0)
             dk[rows, :] += contract(dscore, query_rows, 1, 0)
-        dq = (dq * SCALE).T.astype(BF16).reshape(span, half, HEAD_DIM)
-        at = pl.ds(step * span, span)
-        if final:
-            o_ref[at, 0, which * half : (which + 1) * half, :] = dq
-
-            @pl.when(step == steps - 1)
-            def _():
-                for index in range(which):
-                    o_ref[:, 0, index * half : (index + 1) * half, :] = before[index][...]
-                o_ref[:, 1] = (dk[...] * SCALE).astype(BF16).reshape(parts, tokens, HEAD_DIM)
-                o_ref[:, 2] = dv[...].astype(BF16).reshape(parts, tokens, HEAD_DIM)
-
-        else:
-            dq_ref[at] = dq
+        dq = (dq * SCALE).T.astype(BF16).reshape(span, tokens, HEAD_DIM)
+        o_ref[pl.ds(step * span, span), 0] = dq
+
+        @pl.when(step == steps - 1)
+        def _():
+            o_ref[:, 1] = (dk[...] * SCALE).astype(BF16).reshape(parts, tokens, HEAD_DIM)
+            o_ref[:, 2] = dv[...].astype(BF16).reshape(parts, tokens, HEAD_DIM)
 
     column = lambda i: (0, i)
-    shifted = lambda i: (0, i + which * steps)
     whole = lambda i: (0, 0)
-    sums = jax.ShapeDtypeStruct((total, HEAD_DIM), F32)
-    if final:
-        out_specs = pl.BlockSpec((parts, 3, tokens, HEAD_DIM), lambda i: (0, 0, 0, 0))
-        out_shape = jax.ShapeDtypeStruct((parts, 3, tokens, HEAD_DIM), BF16)
-        scratch = [pltpu.VMEM((total, HEAD_DIM), F32)] * 2
-    else:
-        out_specs = [
-            pl.BlockSpec((parts, half, HEAD_DIM), lambda i: (0, 0, 0)),
-            pl.BlockSpec((total, HEAD_DIM), whole),
-            pl.BlockSpec((total, HEAD_DIM), whole),
-        ]
-        out_shape = [jax.ShapeDtypeStruct((parts, half, HEAD_DIM), BF16), sums, sums]
-        scratch = []
     return pl.pallas_call(
         body,
         grid=(steps,),
         in_specs=[
-            pl.BlockSpec((total, BLOCK), shifted),
+            pl.BlockSpec((total, BLOCK), column),
             pl.BlockSpec((HEAD_DIM, BLOCK), column),
             pl.BlockSpec((8, BLOCK), column),
-            pl.BlockSpec((HEAD_DIM, BLOCK), shifted),
+            pl.BlockSpec((HEAD_DIM, BLOCK), column),
             pl.BlockSpec((HEAD_DIM, total), whole),
             pl.BlockSpec((total, 2 * HEAD_DIM), whole),
-        ]
-        + [
-            pl.BlockSpec(memory_space=pltpu.VMEM) for _ in earlier
         ],
-        out_specs=out_specs,
-        out_shape=out_shape,
-        scratch_shapes=scratch,
+        out_specs=pl.BlockSpec((parts, 3, tokens, HEAD_DIM), lambda i: (0, 0, 0, 0)),
+        out_shape=jax.ShapeDtypeStruct((parts, 3, tokens, HEAD_DIM), BF16),
+        scratch_shapes=[pltpu.VMEM((total, HEAD_DIM), F32)] * 2,
         compiler_params=PARAMS,
         cost_estimate=pl.CostEstimate(
-            flops=10 * total * total * HEAD_DIM // HALVES,
-            bytes_accessed=2 * total * total // HALVES,
+            flops=10 * total * total * HEAD_DIM,
+            bytes_accessed=2 * total * total,
             transcendentals=0,
         ),
         name="backward",
-    )(low, grad, delta, query, key, value, *earlier)
+    )(low, grad, delta, query, key, value)
 
 
 def swap(values, axis, size, bit):
@@ -354,15 +308,12 @@
     return values
 
 
-def scatter_over(values, axis, size):
-    bit = size // 2
-    while bit:
-        upper = lax.axis_index(axis) // bit % 2
-        keep = lax.dynamic_slice_in_dim(values, upper * bit, bit, 0)
-        give = lax.dynamic_slice_in_dim(values, (1 - upper) * bit, bit, 0)
-        values = keep + swap(give, axis, size, bit)
-        bit //= 2
-    return values[0]
+def move(values, z_step=0, y_step=0, core_step=0):
+    pairs = []
+    for i in range(16):
+        z, y, core = i // 4, i // 2 % 2, i % 2
+        pairs.append((i, ((z + z_step) % 4 * 2 + (y ^ y_step)) * 2 + (core ^ core_step)))
+    return lax.ppermute(values, "seq", pairs)
 
 
 def shards(
@@ -373,32 +324,57 @@
     inner_dim = queries.shape[2]
     width_dim = cotangent.shape[2]
     columns = width_dim // dp_size
-    half = queries.shape[1] // HALVES
+    tokens = queries.shape[1]
+    half = tokens // 2
     gate = attn_gate[0][None, :]
-    every = [
-        lax.all_gather(cotangent[0, i * half : (i + 1) * half], "seq", axis=0, tiled=True)
-        for i in range(HALVES)
-    ]
+
+    own = cotangent[0]
+    side = move(own, y_step=1)
+    below, above = move(own, z_step=1), move(own, z_step=3)
     packed = split_columns([queries[0], key_rows[0], value_rows[0]])
     packed = lax.all_to_all(packed, "seq", 0, 0, tiled=True)
+    far_low, far_high = move(below[:half], z_step=1), move(above[half:], z_step=3)
+    side_below, side_above = move(side, z_step=1), move(side, z_step=3)
+    packed, side, below, above, far_low, far_high, side_below, side_above = lax.optimization_barrier(
+        (packed, side, below, above, far_low, far_high, side_below, side_above)
+    )
+    side_low, side_high = move(far_low, y_step=1), move(far_high, y_step=1)
+    found = [
+        (own, 0, 0, 0),
+        (side, 0, 1, 0),
+        (below, 3, 0, 0),
+        (above, 1, 0, 0),
+        (side_below, 3, 1, 0),
+        (side_above, 1, 1, 0),
+        (far_low, 2, 0, 0),
+        (far_high, 2, 0, half),
+        (side_low, 2, 1, 0),
+        (side_high, 2, 1, half),
+    ]
+    me = lax.axis_index("seq")
+    z, y, core = me // 4, me // 2 % 2, me % 2
+    pieces, places = [], []
+    for core_step in range(2):
+        for rows, z_step, y_step, offset in found:
+            rows = move(rows, core_step=1) if core_step else rows
+            device = ((z + z_step) % 4 * 2 + (y ^ y_step)) * 2 + (core ^ core_step)
+            pieces.append((rows, len(places)))
+            places.append(device * tokens + offset)
+
     weight = w_out.astype(F32)
     gated = (weight * gate).astype(BF16)
     low, attended, query, inverse, key, value = forward(lengths, packed)
-
-    earlier, sums, outer = [], [], 0.0
-    for which in range(HALVES):
-        grad, delta, part = project(which, every[which], gated, attended, inverse)
-        outer = outer + part
-        back = backward(
-            which, low, grad, delta, query, key, value, seq_size, earlier + sums
-        )
-        if which < HALVES - 1:
-            earlier.append(back[0])
-            sums = list(back[1:])
+    grad, delta, outer = project(
+        jnp.stack(places).astype(jnp.int32), pieces, gated, attended, inverse
+    )
+
+    partial = (outer * gate).astype(BF16).reshape(HEAD_DIM, dp_size, columns)
+    partial = lax.all_to_all(partial.transpose(1, 0, 2), "dp", 0, 0, tiled=True)
+    back = backward(low, grad, delta, query, key, value, seq_size)
+    back, partial = lax.optimization_barrier((back, partial))
     back = lax.all_to_all(back, "seq", 0, 0, tiled=True)
 
-    partial = (outer * gate).reshape(HEAD_DIM, dp_size, columns).transpose(1, 0, 2)
-    grad_weight = scatter_over(partial, "dp", dp_size)
+    grad_weight = jnp.sum(partial.astype(F32), axis=0)
     squares = grad_weight * grad_weight + EPSILON
     gate_part = jnp.sum(weight * outer, axis=0)
     row_total = total_over(jnp.sum(squares, axis=1), "dp", dp_size)

time: 273 us -> 270 us (0.989)
  starting transfers between devices: 28.6 us -> 47 us
  between operations: 14.8 us -> 1.65 us
  Pallas kernels: 90.3 us -> 77.4 us
  waiting for transfers between devices: 119 us -> 126 us
  other arithmetic: 8.79 us -> 3.92 us
  local copies, waits for them, and re-layouts: 10.7 us -> 13.5 us
    ppermute x0 -> x19, waiting for transfers between devices: none -> 84.7 us  [move(): return lax.ppermute(values, 'seq', pairs)]
    all_to_all x1, waiting for transfers between devices: 65.1 us -> 0.01 us  [shards(): packed = lax.all_to_all(packed, 'seq', 0, 0, tiled=True)]
    all_gather x2 -> x0, waiting for transfers between devices: 17.3 us -> none  [shards(): lax.all_gather(cotangent[0, i * half:(i + 1) * half], 'seq', axis=0, tile...]
    ppermute x0 -> x19, starting transfers between devices: none -> 15.7 us  [move(): return lax.ppermute(values, 'seq', pairs)]
    pallas_call x2 -> x1, Pallas kernels: 45.5 us -> 35.3 us  [backward(): pl.pallas_call(body, grid=(steps,), in_specs=[pl.BlockSpec((total, BLOCK)...]
    unnamed x12 -> x54, local copies, waits for them, and re-layouts: 3.96 us -> 11.7 us
    all_to_all x0 -> x1, starting transfers between devices: none -> 6.63 us  [shards(): partial = lax.all_to_all(partial.transpose(1, 0, 2), 'dp', 0, 0, tiled=True)]
    ppermute x10 -> x7, waiting for transfers between devices: 36 us -> 41.2 us  [swap(): return lax.ppermute(values, axis, [(i, i ^ bit) for i in range(size)])]
  transfers between devices with their start and end apart: 14 -> 29, of which waited for: 10 -> 9; matrix products, arithmetic and copies ran while one was open for 5% -> 1% of each run, Pallas kernels for 13% -> 21%
where the time goes in v4:
time: 270 us; the launch traced here: 269 us
  waiting for transfers between devices  126 us (47%)
  Pallas kernels  77.4 us (29%)
  starting transfers between devices  47 us (17%)
  local copies, waits for them, and re-layouts  13.5 us (5%)
  other arithmetic  3.92 us (1%)
    ppermute x19, waiting for transfers between devices, move(): return lax.ppermute(values, 'seq', pairs)  84.7 us
    ppermute x7, waiting for transfers between devices, swap(): return lax.ppermute(values, axis, [(i, i ^ bit) for i in range(size)])  41.2 us
    pallas_call x1, Pallas kernels, backward(): pl.pallas_call(body, grid=(steps,), in_specs=[pl.BlockSpec((total, BLOCK)...  35.3 us
    pallas_call x1, Pallas kernels, forward(): pl.pallas_call(body, grid_spec=pltpu.PrefetchScalarGridSpec(num_scalar_pr...  20.4 us
    ppermute x19, starting transfers between devices, move(): return lax.ppermute(values, 'seq', pairs)  15.7 us
    pallas_call x1, Pallas kernels, project(): pl.pallas_call(body, in_specs=[pl.BlockSpec(memory_space=pltpu.SMEM)] + [...  14.9 us
    ppermute x7, starting transfers between devices, swap(): return lax.ppermute(values, axis, [(i, i ^ bit) for i in range(size)])  13.9 us
    unnamed x54, local copies, waits for them, and re-layouts  11.7 us
  transfers between devices with their start and end apart: 29, of which 9 were waited for; matrix products, arithmetic and copies ran while one was open for 1% of the time, Pallas kernels for 21%

profile of v4, /device:TPU:0, one launch (start us, length us, event | category | flops | bytes accessed | tf_op | source)
XLA Modules:
  0.0 269.3 jit_solution(13503384069409681273)
XLA Ops:
  0.6 4.5 %split_columns.1 = bf16[16,3,256,128]{3,2,1,0:T(8,128)(2,1)} custom-call(bf16[256,2048]{1,0:T(8,128)(2,1)} %bitcast.35, bf16[256,2048]{1,0:T(8,128)(2,1)} %bitcast.36, bf16[256,2048]{1,0:T(8,128)(2,1)} %bitcast.37), custom_call_target="tpu_custom_call" | custom-call | tf_op jit(solution)/shard_map/split_columns/pallas_call | solution.py:36
  5.1 6.5 %all-to-all-start = ((bf16[16,3,256,128]{3,2,1,0:T(8,128)(2,1)}), bf16[16,3,256,128]{3,2,1,0:T(8,128)(2,1)S(1)}, u32[]{:S(2)}, u32[]{:S(2)}) async-start(bf16[16,3,256,128]{3,2,1,0:T(8,128)(2,1)} %split_columns.1), calls=%async_computation | async-start | bytes 6291456 | tf_op jit(solution)/shard_map/all_to_all | solution.py:335
  11.6 1.9 collective-permute-start
  13.5 1.5 collective-permute-start.1
  15.0 1.8 collective-permute-start.2
  16.8 49.8 %collective-permute-done.refs_2_ = bf16[256,1536]{1,0:T(8,128)(2,1)S(1)} collective-permute-done((bf16[256,1536]{1,0:T(8,128)(2,1)}, bf16[256,1536]{1,0:T(8,128)(2,1)S(1)}, u32[]{:S(2)}, u32[]{:S(2)}) %collective-permute-start) | collective-permute-done | bytes 786464 | tf_op jit(solution)/shard_map/ppermute | solution.py:316
  67.0 2.7 %collective-permute-start.6 = (bf16[256,1536]{1,0:T(8,128)(2,1)S(1)}, bf16[256,1536]{1,0:T(8,128)(2,1)}, u32[]{:S(2)}, u32[]{:S(2)}) collective-permute-start(bf16[256,1536]{1,0:T(8,128)(2,1)S(1)} %collective-permute-done.refs_2_), channel_id=1, source_target_pairs={{0,12},{1,13},{2,14},{3,15},{4,0},{5,1},{6,2},{7,3},{8,4},{9,5},{1... | collective-permute-start | bytes 2359304 | tf_op jit(solution)/shard_map/ppermute | solution.py:316
  69.9 3.3 %collective-permute-start.4 = (bf16[128,1536]{1,0:T(8,128)(2,1)S(1)}, bf16[128,1536]{1,0:T(8,128)(2,1)S(1)}, u32[]{:S(2)}, u32[]{:S(2)}) collective-permute-start(bf16[128,1536]{1,0:T(8,128)(2,1)S(1)} %slice.17), channel_id=1, source_target_pairs={{0,12},{1,13},{2,14},{3,15},{4,0},{5,1},{6,2},{7,3},{8,4},{9,5},{1... | collective-permute-start | bytes 1179656 | tf_op jit(solution)/shard_map/ppermute | solution.py:316
  73.2 22.0 %collective-permute-done.3.refs_7_ = bf16[128,1536]{1,0:T(8,128)(2,1)S(1)} collective-permute-done((bf16[128,1536]{1,0:T(8,128)(2,1)S(1)}, bf16[128,1536]{1,0:T(8,128)(2,1)S(1)}, u32[]{:S(2)}, u32[]{:S(2)}) %collective-permute-start.3) | collective-permute-done | bytes 393248 | tf_op jit(solution)/shard_map/ppermute | solution.py:316
  99.8 1.3 collective-permute-start.8
  101.1 8.0 %collective-permute-done.7.refs_9_ = bf16[128,1536]{1,0:T(8,128)(2,1)} collective-permute-done((bf16[128,1536]{1,0:T(8,128)(2,1)S(1)}, bf16[128,1536]{1,0:T(8,128)(2,1)}, u32[]{:S(2)}, u32[]{:S(2)}) %collective-permute-start.7) | collective-permute-done | bytes 393248 | tf_op jit(solution)/shard_map/ppermute | solution.py:316
  110.2 4.9 %collective-permute-done.8.refs_10_ = bf16[128,1536]{1,0:T(8,128)(2,1)S(1)} collective-permute-done((bf16[128,1536]{1,0:T(8,128)(2,1)}, bf16[128,1536]{1,0:T(8,128)(2,1)S(1)}, u32[]{:S(2)}, u32[]{:S(2)}) %collective-permute-start.8) | collective-permute-done | bytes 393248 | tf_op jit(solution)/shard_map/ppermute | solution.py:316
  116.4 20.4 %forward.1 = (bf16[4096,4096]{1,0:T(8,128)(2,1)}, bf16[128,4096]{1,0:T(8,128)(2,1)S(1)}, bf16[128,4096]{1,0:T(8,128)(2,1)S(1)}, f32[8,4096]{1,0:T(8,128)S(1)}, b...) custom-call(s32[1]{0:T(128)S(6)} %copy.17.len_ref, bf16[16,3,256,128]{3,2,1,0:T(8,128)(2,1)S(1)} %all-to-all-done.p_ref), custom_call_target="tpu_custom_call" | custom-call | flops 12884901888 | bytes 33554432 | tf_op jit(solution)/shard_map/forward/pallas_call | solution.py:139
  137.7 1.3 copy-done.16
  139.2 14.9 %project.1 = (bf16[128,4096]{1,0:T(8,128)(2,1)}, f32[8,4096]{1,0:T(8,128)S(1)}, f32[128,1536]{1,0:T(8,128)S(1)}) custom-call(s32[20]{0:T(128)S(1)} %stack.83.refs_0_, bf16[256,1536]{1,0:T(8,128)(2,1)S(1)} %bitcast.34, bf16[256,1536]{1,0:T(8,128)(2,1)S(1)} %copy-done.8, bf16[256,1536]{1,0:T(8,128)(2,1)S(1)} %copy-done.2, bf16[256,1536]{1,0:T(8,128)(2,1)S(1)} %copy-done.4, ...), custom_call_target="tpu_custom_call" | custom-call | flops 3221225472 | bytes 12582912 | tf_op jit(solution)/shard_map/project/pallas_call | solution.py:210
  155.7 6.6 %all-to-all-start.1 = ((bf16[8,128,192]{1,2,0:T(8,128)(2,1)}), bf16[8,128,192]{1,2,0:T(8,128)(2,1)S(1)}, u32[]{:S(2)}, u32[]{:S(2)}) async-start(bf16[8,128,192]{1,2,0:T(8,128)(2,1)} %bitcast.25), calls=%async_computation.1 | async-start | bytes 786432 | tf_op jit(solution)/shard_map/all_to_all | solution.py:372
  164.5 1.6 copy-done.17
  166.1 1.2 copy-done.19
  167.3 1.2 copy-done.21
  168.6 35.3 %backward.1 = bf16[16,3,256,128]{3,2,1,0:T(8,128)(2,1)S(1)} custom-call(bf16[4096,4096]{1,0:T(8,128)(2,1)} %get-tuple-element.30.e_ref, bf16[128,4096]{1,0:T(8,128)(2,1)S(1)} %copy-done.13, f32[8,4096]{1,0:T(8,128)S(1)} %copy-done.15, bf16[128,4096]{1,0:T(8,128)(2,1)S(1)} %copy-done.19, bf16[128,4096]{1,0:T(8,128)(2,1)S(1)} %copy-done.21, ...), custom_call_target="tpu_custom_call" | custom-call | flops 21474836480 | bytes 33554432 | tf_op jit(solution)/shard_map/backward/pallas_call | solution.py:275
  203.9 1.6 copy-done
  205.6 4.2 %all-to-all-start.2 = ((bf16[16,3,256,128]{3,2,1,0:T(8,128)(2,1)}), bf16[16,3,256,128]{3,2,1,0:T(8,128)(2,1)S(1)}, u32[]{:S(2)}, u32[]{:S(2)}) async-start(bf16[16,3,256,128]{3,2,1,0:T(8,128)(2,1)} %copy-done), calls=%async_computation.2 | async-start | bytes 6291456 | tf_op jit(solution)/shard_map/all_to_all | solution.py:375
  211.3 1.9 collective-permute-start.20
  213.2 34.7 %collective-permute-done.20 = f32[1728]{0:T(1024)S(1)} collective-permute-done((f32[1728]{0:T(1024)S(1)}, f32[1728]{0:T(1024)S(1)}, u32[]{:S(2)}, u32[]{:S(2)}) %collective-permute-start.20) | collective-permute-done | bytes 6944 | tf_op jit(solution)/shard_map/ppermute | solution.py:300
  248.4 4.1 %collective-permute-start.23 = (f32[128]{0:T(128)S(1)}, f32[128]{0:T(128)S(1)}, u32[]{:S(2)}, u32[]{:S(2)}) collective-permute-start(f32[128]{0:T(128)S(1)} %get-tuple-element.51), channel_id=1, source_target_pairs={{0,16},{16,0},{32,48},{48,32},{64,80},{80,64},{96,112},{112,96},{1... | collective-permute-start | bytes 1544 | tf_op jit(solution)/shard_map/ppermute | solution.py:300
  252.5 1.5 collective-permute-done.23
  254.1 1.5 collective-permute-start.24
  255.5 2.1 collective-permute-done.24
  257.6 3.0 %collective-permute-start.25 = (f32[128]{0:T(128)S(1)}, f32[128]{0:T(128)S(1)}, u32[]{:S(2)}, u32[]{:S(2)}) collective-permute-start(f32[128]{0:T(128)S(1)} %add.236), channel_id=1, source_target_pairs={{0,64},{16,80},{32,96},{48,112},{64,0},{80,16},{96,32},{112,48},{1... | collective-permute-start | bytes 1544 | tf_op jit(solution)/shard_map/ppermute | solution.py:300
  260.6 2.6 collective-permute-start.22
  263.7 2.0 collective-permute-done.22
  267.0 2.3 join_columns.1
  (105 shorter events, 15.5 us)
Async XLA Ops:
  5.1 91.8 %all-to-all-start = ((bf16[16,3,256,128]{3,2,1,0:T(8,128)(2,1)}), bf16[16,3,256,128]{3,2,1,0:T(8,128)(2,1)S(1)}, u32[]{:S(2)}, u32[]{:S(2)}) async-start(bf16[16,3,256,128]{3,2,1,0:T(8,128)(2,1)} %split_columns.1), calls=%async_computation | async-start | bytes 6291456 | tf_op jit(solution)/shard_map/all_to_all | solution.py:335
  11.6 54.9 %collective-permute-start = (bf16[256,1536]{1,0:T(8,128)(2,1)}, bf16[256,1536]{1,0:T(8,128)(2,1)S(1)}, u32[]{:S(2)}, u32[]{:S(2)}) collective-permute-start(bf16[256,1536]{1,0:T(8,128)(2,1)} %bitcast.30), channel_id=1, source_target_pairs={{0,2},{1,3},{2,0},{3,1},{4,6},{5,7},{6,4},{7,5},{8,10},{9,11},{10,... | collective-permute-start | bytes 2359304 | tf_op jit(solution)/shard_map/ppermute | solution.py:316
  13.5 56.2 %collective-permute-start.1 = (bf16[256,1536]{1,0:T(8,128)(2,1)}, bf16[256,1536]{1,0:T(8,128)(2,1)S(1)}, u32[]{:S(2)}, u32[]{:S(2)}) collective-permute-start(bf16[256,1536]{1,0:T(8,128)(2,1)} %bitcast.31), channel_id=1, source_target_pairs={{0,4},{1,5},{2,6},{3,7},{4,8},{5,9},{6,10},{7,11},{8,12},{9,13},{1... | collective-permute-start | bytes 2359304 | tf_op jit(solution)/shard_map/ppermute | solution.py:316
  15.0 54.9 %collective-permute-start.2 = (bf16[256,1536]{1,0:T(8,128)(2,1)}, bf16[256,1536]{1,0:T(8,128)(2,1)S(1)}, u32[]{:S(2)}, u32[]{:S(2)}) collective-permute-start(bf16[256,1536]{1,0:T(8,128)(2,1)} %bitcast.32), channel_id=1, source_target_pairs={{0,12},{1,13},{2,14},{3,15},{4,0},{5,1},{6,2},{7,3},{8,4},{9,5},{1... | collective-permute-start | bytes 2359304 | tf_op jit(solution)/shard_map/ppermute | solution.py:316
  66.5 28.7 %collective-permute-start.5 = (bf16[256,1536]{1,0:T(8,128)(2,1)S(1)}, bf16[256,1536]{1,0:T(8,128)(2,1)S(1)}, u32[]{:S(2)}, u32[]{:S(2)}) collective-permute-start(bf16[256,1536]{1,0:T(8,128)(2,1)S(1)} %collective-permute-done.refs_2_), channel_id=1, source_target_pairs={{0,4},{1,5},{2,6},{3,7},{4,8},{5,9},{6,10},{7,11},{8,12},{9,13},{1... | collective-permute-start | bytes 2359304 | tf_op jit(solution)/shard_map/ppermute | solution.py:316
  67.0 29.8 %collective-permute-start.6 = (bf16[256,1536]{1,0:T(8,128)(2,1)S(1)}, bf16[256,1536]{1,0:T(8,128)(2,1)}, u32[]{:S(2)}, u32[]{:S(2)}) collective-permute-start(bf16[256,1536]{1,0:T(8,128)(2,1)S(1)} %collective-permute-done.refs_2_), channel_id=1, source_target_pairs={{0,12},{1,13},{2,14},{3,15},{4,0},{5,1},{6,2},{7,3},{8,4},{9,5},{1... | collective-permute-start | bytes 2359304 | tf_op jit(solution)/shard_map/ppermute | solution.py:316
  69.8 25.4 %collective-permute-start.3 = (bf16[128,1536]{1,0:T(8,128)(2,1)S(1)}, bf16[128,1536]{1,0:T(8,128)(2,1)S(1)}, u32[]{:S(2)}, u32[]{:S(2)}) collective-permute-start(bf16[128,1536]{1,0:T(8,128)(2,1)S(1)} %slice.16), channel_id=1, source_target_pairs={{0,4},{1,5},{2,6},{3,7},{4,8},{5,9},{6,10},{7,11},{8,12},{9,13},{1... | collective-permute-start | bytes 1179656 | tf_op jit(solution)/shard_map/ppermute | solution.py:316
  69.9 25.3 %collective-permute-start.4 = (bf16[128,1536]{1,0:T(8,128)(2,1)S(1)}, bf16[128,1536]{1,0:T(8,128)(2,1)S(1)}, u32[]{:S(2)}, u32[]{:S(2)}) collective-permute-start(bf16[128,1536]{1,0:T(8,128)(2,1)S(1)} %slice.17), channel_id=1, source_target_pairs={{0,12},{1,13},{2,14},{3,15},{4,0},{5,1},{6,2},{7,3},{8,4},{9,5},{1... | collective-permute-start | bytes 1179656 | tf_op jit(solution)/shard_map/ppermute | solution.py:316
  73.2 26.6 %collective-permute-start.9 = (bf16[256,1536]{1,0:T(8,128)(2,1)}, bf16[256,1536]{1,0:T(8,128)(2,1)}, u32[]{:S(2)}, u32[]{:S(2)}) collective-permute-start(bf16[256,1536]{1,0:T(8,128)(2,1)} %bitcast.33), channel_id=1, source_target_pairs={{0,1},{1,0},{2,3},{3,2},{4,5},{5,4},{6,7},{7,6},{8,9},{9,8},{10,11... | collective-permute-start | bytes 2359304 | tf_op jit(solution)/shard_map/ppermute | solution.py:316
  96.9 12.2 %collective-permute-start.7 = (bf16[128,1536]{1,0:T(8,128)(2,1)S(1)}, bf16[128,1536]{1,0:T(8,128)(2,1)}, u32[]{:S(2)}, u32[]{:S(2)}) collective-permute-start(bf16[128,1536]{1,0:T(8,128)(2,1)S(1)} %collective-permute-done.3.refs_7_), channel_id=1, source_target_pairs={{0,2},{1,3},{2,0},{3,1},{4,6},{5,7},{6,4},{7,5},{8,10},{9,11},{10,... | collective-permute-start | bytes 1179656 | tf_op jit(solution)/shard_map/ppermute | solution.py:316
  97.7 18.0 %collective-permute-start.10 = (bf16[256,1536]{1,0:T(8,128)(2,1)}, bf16[256,1536]{1,0:T(8,128)(2,1)}, u32[]{:S(2)}, u32[]{:S(2)}) collective-permute-start(bf16[256,1536]{1,0:T(8,128)(2,1)} %copy-done.7), channel_id=1, source_target_pairs={{0,1},{1,0},{2,3},{3,2},{4,5},{5,4},{6,7},{7,6},{8,9},{9,8},{10,11... | collective-permute-start | bytes 2359304 | tf_op jit(solution)/shard_map/ppermute | solution.py:316
  97.7 18.4 %collective-permute-start.11 = (bf16[256,1536]{1,0:T(8,128)(2,1)}, bf16[256,1536]{1,0:T(8,128)(2,1)}, u32[]{:S(2)}, u32[]{:S(2)}) collective-permute-start(bf16[256,1536]{1,0:T(8,128)(2,1)} %copy-done.1), channel_id=1, source_target_pairs={{0,1},{1,0},{2,3},{3,2},{4,5},{5,4},{6,7},{7,6},{8,9},{9,8},{10,11... | collective-permute-start | bytes 2359304 | tf_op jit(solution)/shard_map/ppermute | solution.py:316
  99.7 15.4 %collective-permute-start.15 = (bf16[128,1536]{1,0:T(8,128)(2,1)S(1)}, bf16[128,1536]{1,0:T(8,128)(2,1)S(1)}, u32[]{:S(2)}, u32[]{:S(2)}) collective-permute-start(bf16[128,1536]{1,0:T(8,128)(2,1)S(1)} %collective-permute-done.3.refs_7_), channel_id=1, source_target_pairs={{0,1},{1,0},{2,3},{3,2},{4,5},{5,4},{6,7},{7,6},{8,9},{9,8},{10,11... | collective-permute-start | bytes 1179656 | tf_op jit(solution)/shard_map/ppermute | solution.py:316
  99.8 15.3 %collective-permute-start.8 = (bf16[128,1536]{1,0:T(8,128)(2,1)}, bf16[128,1536]{1,0:T(8,128)(2,1)S(1)}, u32[]{:S(2)}, u32[]{:S(2)}) collective-permute-start(bf16[128,1536]{1,0:T(8,128)(2,1)} %copy-done.11), channel_id=1, source_target_pairs={{0,2},{1,3},{2,0},{3,1},{4,6},{5,7},{6,4},{7,5},{8,10},{9,11},{10,... | collective-permute-start | bytes 1179656 | tf_op jit(solution)/shard_map/ppermute | solution.py:316
  109.0 6.5 %collective-permute-start.16 = (bf16[128,1536]{1,0:T(8,128)(2,1)}, bf16[128,1536]{1,0:T(8,128)(2,1)S(1)}, u32[]{:S(2)}, u32[]{:S(2)}) collective-permute-start(bf16[128,1536]{1,0:T(8,128)(2,1)} %copy-done.11), channel_id=1, source_target_pairs={{0,1},{1,0},{2,3},{3,2},{4,5},{5,4},{6,7},{7,6},{8,9},{9,8},{10,11... | collective-permute-start | bytes 1179656 | tf_op jit(solution)/shard_map/ppermute | solution.py:316
  115.1 24.0 %collective-permute-start.12 = (bf16[256,1536]{1,0:T(8,128)(2,1)}, bf16[256,1536]{1,0:T(8,128)(2,1)S(1)}, u32[]{:S(2)}, u32[]{:S(2)}) collective-permute-start(bf16[256,1536]{1,0:T(8,128)(2,1)} %copy-done.3), channel_id=1, source_target_pairs={{0,1},{1,0},{2,3},{3,2},{4,5},{5,4},{6,7},{7,6},{8,9},{9,8},{10,11... | collective-permute-start | bytes 2359304 | tf_op jit(solution)/shard_map/ppermute | solution.py:316
  115.1 24.0 %collective-permute-start.13 = (bf16[256,1536]{1,0:T(8,128)(2,1)}, bf16[256,1536]{1,0:T(8,128)(2,1)S(1)}, u32[]{:S(2)}, u32[]{:S(2)}) collective-permute-start(bf16[256,1536]{1,0:T(8,128)(2,1)} %copy-done.9), channel_id=1, source_target_pairs={{0,1},{1,0},{2,3},{3,2},{4,5},{5,4},{6,7},{7,6},{8,9},{9,8},{10,11... | collective-permute-start | bytes 2359304 | tf_op jit(solution)/shard_map/ppermute | solution.py:316
  115.6 23.5 %collective-permute-start.14 = (bf16[256,1536]{1,0:T(8,128)(2,1)}, bf16[256,1536]{1,0:T(8,128)(2,1)S(1)}, u32[]{:S(2)}, u32[]{:S(2)}) collective-permute-start(bf16[256,1536]{1,0:T(8,128)(2,1)} %collective-permute-done.6.refs_6_), channel_id=1, source_target_pairs={{0,1},{1,0},{2,3},{3,2},{4,5},{5,4},{6,7},{7,6},{8,9},{9,8},{10,11... | collective-permute-start | bytes 2359304 | tf_op jit(solution)/shard_map/ppermute | solution.py:316
  115.7 23.4 %collective-permute-start.17 = (bf16[128,1536]{1,0:T(8,128)(2,1)}, bf16[128,1536]{1,0:T(8,128)(2,1)S(1)}, u32[]{:S(2)}, u32[]{:S(2)}) collective-permute-start(bf16[128,1536]{1,0:T(8,128)(2,1)} %collective-permute-done.7.refs_9_), channel_id=1, source_target_pairs={{0,1},{1,0},{2,3},{3,2},{4,5},{5,4},{6,7},{7,6},{8,9},{9,8},{10,11... | collective-permute-start | bytes 1179656 | tf_op jit(solution)/shard_map/ppermute | solution.py:316
  116.1 23.0 %collective-permute-start.18 = (bf16[128,1536]{1,0:T(8,128)(2,1)S(1)}, bf16[128,1536]{1,0:T(8,128)(2,1)S(1)}, u32[]{:S(2)}, u32[]{:S(2)}) collective-permute-start(bf16[128,1536]{1,0:T(8,128)(2,1)S(1)} %collective-permute-done.8.refs_10_), channel_id=1, source_target_pairs={{0,1},{1,0},{2,3},{3,2},{4,5},{5,4},{6,7},{7,6},{8,9},{9,8},{10,11... | collective-permute-start | bytes 1179656 | tf_op jit(solution)/shard_map/ppermute | solution.py:316
  155.7 49.8 %all-to-all-start.1 = ((bf16[8,128,192]{1,2,0:T(8,128)(2,1)}), bf16[8,128,192]{1,2,0:T(8,128)(2,1)S(1)}, u32[]{:S(2)}, u32[]{:S(2)}) async-start(bf16[8,128,192]{1,2,0:T(8,128)(2,1)} %bitcast.25), calls=%async_computation.1 | async-start | bytes 786432 | tf_op jit(solution)/shard_map/all_to_all | solution.py:372
  205.5 57.7 %copy-start.26 = (f32[128]{0:T(128)S(1)}, f32[128]{0:T(128)}, u32[]{:S(2)}) copy-start(f32[128]{0:T(128)} %param.16) | copy-start | bytes 1540
  205.5 60.9 %copy-start.25 = (f32[192]{0:T(256)S(1)}, f32[192]{0:T(256)}, u32[]{:S(2)}) copy-start(f32[192]{0:T(256)} %param.17) | copy-start | bytes 2308
  205.6 61.4 %all-to-all-start.2 = ((bf16[16,3,256,128]{3,2,1,0:T(8,128)(2,1)}), bf16[16,3,256,128]{3,2,1,0:T(8,128)(2,1)S(1)}, u32[]{:S(2)}, u32[]{:S(2)}) async-start(bf16[16,3,256,128]{3,2,1,0:T(8,128)(2,1)} %copy-done), calls=%async_computation.2 | async-start | bytes 6291456 | tf_op jit(solution)/shard_map/all_to_all | solution.py:375
  209.8 56.6 %copy-start.23 = (f32[128,192]{0,1:T(8,128)}, f32[128,192]{0,1:T(8,128)S(1)}, u32[]{:S(2)}) copy-start(f32[128,192]{0,1:T(8,128)S(1)} %convert_reduce_fusion) | copy-start | bytes 294916
  210.0 1.3 collective-permute-start.19
  211.3 36.6 %collective-permute-start.20 = (f32[1728]{0:T(1024)S(1)}, f32[1728]{0:T(1024)S(1)}, u32[]{:S(2)}, u32[]{:S(2)}) collective-permute-start(f32[1728]{0:T(1024)S(1)} %fusion.5), channel_id=1, source_target_pairs={{0,2},{1,3},{2,0},{3,1},{4,6},{5,7},{6,4},{7,5},{8,10},{9,11},{10,... | collective-permute-start | bytes 20744 | tf_op jit(solution)/shard_map/ppermute | solution.py:300
  247.9 12.6 %collective-permute-start.21 = (f32[1728]{0:T(1024)S(1)}, f32[1728]{0:T(1024)S(1)}, u32[]{:S(2)}, u32[]{:S(2)}) collective-permute-start(f32[1728]{0:T(1024)S(1)} %add.232), channel_id=1, source_target_pairs={{0,4},{1,5},{2,6},{3,7},{4,0},{5,1},{6,2},{7,3},{8,12},{9,13},{10,... | collective-permute-start | bytes 20744 | tf_op jit(solution)/shard_map/ppermute | solution.py:300
  248.4 5.6 %collective-permute-start.23 = (f32[128]{0:T(128)S(1)}, f32[128]{0:T(128)S(1)}, u32[]{:S(2)}, u32[]{:S(2)}) collective-permute-start(f32[128]{0:T(128)S(1)} %get-tuple-element.51), channel_id=1, source_target_pairs={{0,16},{16,0},{32,48},{48,32},{64,80},{80,64},{96,112},{112,96},{1... | collective-permute-start | bytes 1544 | tf_op jit(solution)/shard_map/ppermute | solution.py:300
  254.1 3.5 %collective-permute-start.24 = (f32[128]{0:T(128)S(1)}, f32[128]{0:T(128)S(1)}, u32[]{:S(2)}, u32[]{:S(2)}) collective-permute-start(f32[128]{0:T(128)S(1)} %add.235), channel_id=1, source_target_pairs={{0,32},{16,48},{32,0},{48,16},{64,96},{80,112},{96,64},{112,80},{1... | collective-permute-start | bytes 1544 | tf_op jit(solution)/shard_map/ppermute | solution.py:300
  257.6 5.6 %collective-permute-start.25 = (f32[128]{0:T(128)S(1)}, f32[128]{0:T(128)S(1)}, u32[]{:S(2)}, u32[]{:S(2)}) collective-permute-start(f32[128]{0:T(128)S(1)} %add.236), channel_id=1, source_target_pairs={{0,64},{16,80},{32,96},{48,112},{64,0},{80,16},{96,32},{112,48},{1... | collective-permute-start | bytes 1544 | tf_op jit(solution)/shard_map/ppermute | solution.py:300
  260.6 5.2 %collective-permute-start.22 = (f32[1728]{0:T(1024)S(1)}, f32[1728]{0:T(1024)S(1)}, u32[]{:S(2)}, u32[]{:S(2)}) collective-permute-start(f32[1728]{0:T(1024)S(1)} %add.233), channel_id=1, source_target_pairs={{0,8},{1,9},{2,10},{3,11},{4,12},{5,13},{6,14},{7,15},{8,0},{9,1},... | collective-permute-start | bytes 20744 | tf_op jit(solution)/shard_map/ppermute | solution.py:300
  (24 other events, 315.3 us)

commit v5 on v4

--- a/solution.py
+++ b/solution.py
@@ -12,7 +12,7 @@
 BLOCK = 512
 BF16 = jnp.bfloat16
 F32 = jnp.float32
-PARAMS = pltpu.CompilerParams(vmem_limit_bytes=40 * 2**20)
+PARAMS = pltpu.CompilerParams(vmem_limit_bytes=56 * 2**20)
 
 
 def contract(left, right, left_dim, right_dim):
@@ -167,7 +167,7 @@
             jax.ShapeDtypeStruct((HEAD_DIM, total), BF16),
             jax.ShapeDtypeStruct((total, 2 * HEAD_DIM), BF16),
         ],
-        compiler_params=PARAMS,
+        compiler_params=pltpu.CompilerParams(vmem_limit_bytes=40 * 2**20),
         cost_estimate=pl.CostEstimate(
             flops=6 * total * total * HEAD_DIM,
             bytes_accessed=2 * total * total,
@@ -177,32 +177,55 @@
     )(valid_len, packed)
 
 
-def project(places, pieces, gated, attended, inverse):
+def project(places, pieces, gated, attended, inverse, earlier):
     width = gated.shape[1]
     total = attended.shape[1]
     count = len(pieces)
+    sizes = [piece.shape[0] for piece in pieces]
+    starts = [sum(sizes[:i]) for i in range(count)]
+    groups, filled = [[]], 0
+    for i in range(count):
+        if filled == 1024:
+            groups.append([])
+            filled = 0
+        groups[-1].append(i)
+        filled += sizes[i]
 
     def body(*refs):
         place_ref, sources = refs[0], refs[1 : 1 + count]
-        w_ref, o_ref, inv_ref, g_ref, d_ref, a_ref = refs[1 + count : 7 + count]
-        buffers, sems = refs[7 + count : 7 + 2 * count], refs[7 + 2 * count]
+        w_ref, o_ref, inv_ref = refs[1 + count : 4 + count]
+        before = refs[4 + count : 4 + count + len(earlier)]
+        g_ref, d_ref, a_ref, held, sems = refs[4 + count + len(earlier) :]
         copies = [
-            pltpu.make_async_copy(sources[i], buffers[i], sems.at[i]) for i in range(count)
+            pltpu.make_async_copy(
+                sources[i], held.at[pl.ds(starts[i], sizes[i]), :], sems.at[i]
+            )
+            for i in range(count)
         ]
         for copy in copies:
             copy.start()
         outer = jnp.zeros((HEAD_DIM, width), F32)
-        for i in range(count):
-            size = pieces[i][0].shape[0]
-            lanes = pl.ds(pl.multiple_of(place_ref[pieces[i][1]], HEAD_DIM), size)
-            copies[i].wait()
-            rows = buffers[i][...]
+        if before:
+            g_ref[...] = before[0][...]
+            d_ref[...] = before[1][...]
+            outer = before[2][...]
+        for group in groups:
+            lanes = [
+                pl.ds(pl.multiple_of(place_ref[i], HEAD_DIM), sizes[i]) for i in group
+            ]
+            out = jnp.concatenate([o_ref[:, lane] for lane in lanes], axis=1)
+            inv = jnp.concatenate([inv_ref[0:1, lane] for lane in lanes], axis=1)
+            for i in group:
+                copies[i].wait()
+            first, last = group[0], group[-1]
+            rows = held[starts[first] : starts[last] + sizes[last], :]
             grad = contract(w_ref[...], rows, 1, 1).astype(BF16).astype(F32)
-            low = (grad * inv_ref[0:1, lanes]).astype(BF16)
-            g_ref[:, lanes] = low
-            out = o_ref[:, lanes]
+            low = (grad * inv).astype(BF16)
             delta = jnp.sum(low.astype(F32) * out.astype(F32), axis=0, keepdims=True)
-            d_ref[:, lanes] = jnp.broadcast_to(delta, (8, size))
+            for i, lane in zip(group, lanes):
+                at = slice(starts[i] - starts[first], starts[i] - starts[first] + sizes[i])
+                g_ref[:, lane] = low[:, at]
+                d_ref[:, lane] = jnp.broadcast_to(delta[:, at], (8, sizes[i]))
             outer = outer + contract(out, rows, 1, 0)
         a_ref[...] = outer
 
@@ -211,23 +234,25 @@
         body,
         in_specs=[pl.BlockSpec(memory_space=pltpu.SMEM)]
         + [pl.BlockSpec(memory_space=pl.ANY)] * count
-        + [vmem] * 3,
+        + [vmem] * (3 + len(earlier)),
         out_specs=[vmem] * 3,
         out_shape=[
             jax.ShapeDtypeStruct((HEAD_DIM, total), BF16),
             jax.ShapeDtypeStruct((8, total), F32),
             jax.ShapeDtypeStruct((HEAD_DIM, width), F32),
         ],
-        scratch_shapes=[pltpu.VMEM(rows.shape, BF16) for rows, _ in pieces]
-        + [pltpu.SemaphoreType.DMA((count,))],
+        scratch_shapes=[
+            pltpu.VMEM((sum(sizes), width), BF16),
+            pltpu.SemaphoreType.DMA((count,)),
+        ],
         compiler_params=PARAMS,
         cost_estimate=pl.CostEstimate(
-            flops=4 * total * width * HEAD_DIM,
-            bytes_accessed=2 * total * width,
+            flops=4 * sum(sizes) * width * HEAD_DIM,
+            bytes_accessed=2 * sum(sizes) * width,
             transcendentals=0,
         ),
         name="project",
-    )(places, *[rows for rows, _ in pieces], gated, attended, inverse)
+    )(places, *pieces, gated, attended, inverse, *earlier)
 
 
 def backward(low, grad, delta, query, key, value, parts):
@@ -332,41 +357,41 @@
     side = move(own, y_step=1)
     below, above = move(own, z_step=1), move(own, z_step=3)
     packed = split_columns([queries[0], key_rows[0], value_rows[0]])
+    packed, side, below, above = lax.optimization_barrier((packed, side, below, above))
     packed = lax.all_to_all(packed, "seq", 0, 0, tiled=True)
     far_low, far_high = move(below[:half], z_step=1), move(above[half:], z_step=3)
     side_below, side_above = move(side, z_step=1), move(side, z_step=3)
-    packed, side, below, above, far_low, far_high, side_below, side_above = lax.optimization_barrier(
-        (packed, side, below, above, far_low, far_high, side_below, side_above)
-    )
     side_low, side_high = move(far_low, y_step=1), move(far_high, y_step=1)
     found = [
         (own, 0, 0, 0),
         (side, 0, 1, 0),
         (below, 3, 0, 0),
         (above, 1, 0, 0),
+        (far_low, 2, 0, 0),
+        (far_high, 2, 0, half),
         (side_below, 3, 1, 0),
         (side_above, 1, 1, 0),
-        (far_low, 2, 0, 0),
-        (far_high, 2, 0, half),
         (side_low, 2, 1, 0),
         (side_high, 2, 1, half),
     ]
     me = lax.axis_index("seq")
     z, y, core = me // 4, me // 2 % 2, me % 2
-    pieces, places = [], []
-    for core_step in range(2):
-        for rows, z_step, y_step, offset in found:
-            rows = move(rows, core_step=1) if core_step else rows
-            device = ((z + z_step) % 4 * 2 + (y ^ y_step)) * 2 + (core ^ core_step)
-            pieces.append((rows, len(places)))
-            places.append(device * tokens + offset)
 
     weight = w_out.astype(F32)
     gated = (weight * gate).astype(BF16)
     low, attended, query, inverse, key, value = forward(lengths, packed)
-    grad, delta, outer = project(
-        jnp.stack(places).astype(jnp.int32), pieces, gated, attended, inverse
-    )
+    made = []
+    for some in (found[:8], found[8:]):
+        pieces, places = [], []
+        for core_step in range(2):
+            for rows, z_step, y_step, offset in some:
+                device = ((z + z_step) % 4 * 2 + (y ^ y_step)) * 2 + (core ^ core_step)
+                pieces.append(move(rows, core_step=1) if core_step else rows)
+                places.append(device * tokens + offset)
+        made = project(
+            jnp.stack(places).astype(jnp.int32), pieces, gated, attended, inverse, made
+        )
+    grad, delta, outer = made
 
     partial = (outer * gate).astype(BF16).reshape(HEAD_DIM, dp_size, columns)
     partial = lax.all_to_all(partial.transpose(1, 0, 2), "dp", 0, 0, tiled=True)

time: 270 us -> 267 us (0.989)
  Pallas kernels: 77.4 us -> 80.8 us
  local copies, waits for them, and re-layouts: 13.5 us -> 10.4 us
    unnamed x54 -> x26, local copies, waits for them, and re-layouts: 11.7 us -> 6.05 us
    pallas_call x1, Pallas kernels: 35.3 us -> 38.2 us  [backward(): pl.pallas_call(body, grid=(steps,), in_specs=[pl.BlockSpec((total, BLOCK)...]
    pallas_call x1 -> x2, Pallas kernels: 14.9 us -> 15.4 us  [project(): pl.pallas_call(body, in_specs=[pl.BlockSpec(memory_space=pltpu.SMEM)] + [...]
  transfers between devices with their start and end apart: 29 -> 29, of which waited for: 9 -> 11; matrix products, arithmetic and copies ran while one was open for 1% -> 3% of each run, Pallas kernels for 21% -> 27%
where the time goes in v5:
time: 267 us
  waiting for transfers between devices  124 us (46%)
  Pallas kernels  80.8 us (30%)
  starting transfers between devices  45.3 us (17%)
  local copies, waits for them, and re-layouts  10.4 us (4%)
  other arithmetic  4.87 us (2%)
    ppermute x19, waiting for transfers between devices, move(): return lax.ppermute(values, 'seq', pairs)  83.9 us
    ppermute x7, waiting for transfers between devices, swap(): return lax.ppermute(values, axis, [(i, i ^ bit) for i in range(size)])  40 us
    pallas_call x1, Pallas kernels, backward(): pl.pallas_call(body, grid=(steps,), in_specs=[pl.BlockSpec((total, BLOCK)...  38.2 us
    pallas_call x1, Pallas kernels, forward(): pl.pallas_call(body, grid_spec=pltpu.PrefetchScalarGridSpec(num_scalar_pr...  20.5 us
    ppermute x19, starting transfers between devices, move(): return lax.ppermute(values, 'seq', pairs)  16.3 us
    pallas_call x2, Pallas kernels, project(): pl.pallas_call(body, in_specs=[pl.BlockSpec(memory_space=pltpu.SMEM)] + [...  15.4 us
    ppermute x7, starting transfers between devices, swap(): return lax.ppermute(values, axis, [(i, i ^ bit) for i in range(size)])  14.4 us
    all_to_all x1, starting transfers between devices, shards(): partial = lax.all_to_all(partial.transpose(1, 0, 2), 'dp', 0, 0, tiled=True)  6.82 us
  transfers between devices with their start and end apart: 29, of which 11 were waited for; matrix products, arithmetic and copies ran while one was open for 3% of the time, Pallas kernels for 27%

profile of v5, /device:TPU:0, one launch (start us, length us, event | category | flops | bytes accessed | tf_op | source)
XLA Modules:
  0.0 266.6 jit_solution(7868996733068938279)
XLA Ops:
  0.6 1.7 collective-permute-start
  2.4 1.9 collective-permute-start.1
  4.3 2.1 collective-permute-start.2
  6.4 4.5 %split_columns.1 = bf16[16,3,256,128]{3,2,1,0:T(8,128)(2,1)} custom-call(bf16[256,2048]{1,0:T(8,128)(2,1)} %bitcast.30, bf16[256,2048]{1,0:T(8,128)(2,1)} %bitcast.31, bf16[256,2048]{1,0:T(8,128)(2,1)} %bitcast.32), custom_call_target="tpu_custom_call" | custom-call | tf_op jit(solution)/shard_map/split_columns/pallas_call | solution.py:36
  10.9 9.3 %collective-permute-done.refs_2_ = bf16[256,1536]{1,0:T(8,128)(2,1)S(1)} collective-permute-done((bf16[256,1536]{1,0:T(8,128)(2,1)}, bf16[256,1536]{1,0:T(8,128)(2,1)S(1)}, u32[]{:S(2)}, u32[]{:S(2)}) %collective-permute-start) | collective-permute-done | bytes 786464 | tf_op jit(solution)/shard_map/ppermute | solution.py:341
  20.1 3.8 %collective-permute-done.1.refs_3_ = bf16[256,1536]{1,0:T(8,128)(2,1)S(1)} collective-permute-done((bf16[256,1536]{1,0:T(8,128)(2,1)}, bf16[256,1536]{1,0:T(8,128)(2,1)S(1)}, u32[]{:S(2)}, u32[]{:S(2)}) %collective-permute-start.1) | collective-permute-done | bytes 786464 | tf_op jit(solution)/shard_map/ppermute | solution.py:341
  25.1 4.0 %all-to-all-start = ((bf16[16,3,256,128]{3,2,1,0:T(8,128)(2,1)}), bf16[16,3,256,128]{3,2,1,0:T(8,128)(2,1)S(1)}, u32[]{:S(2)}, u32[]{:S(2)}) async-start(bf16[16,3,256,128]{3,2,1,0:T(8,128)(2,1)} %split_columns.1), calls=%async_computation | async-start | bytes 6291456 | tf_op jit(solution)/shard_map/all_to_all | solution.py:361
  29.6 1.7 collective-permute-start.9
  31.2 1.6 collective-permute-start.10
  35.4 2.8 %collective-permute-start.5 = (bf16[128,1536]{1,0:T(8,128)(2,1)S(1)}, bf16[128,1536]{1,0:T(8,128)(2,1)}, u32[]{:S(2)}, u32[]{:S(2)}) collective-permute-start(bf16[128,1536]{1,0:T(8,128)(2,1)S(1)} %slice.13), channel_id=1, source_target_pairs={{0,12},{1,13},{2,14},{3,15},{4,0},{5,1},{6,2},{7,3},{8,4},{9,5},{1... | collective-permute-start | bytes 1179656 | tf_op jit(solution)/shard_map/ppermute | solution.py:341
  38.2 54.4 %collective-permute-done.3.refs_5_ = bf16[128,1536]{1,0:T(8,128)(2,1)} collective-permute-done((bf16[128,1536]{1,0:T(8,128)(2,1)S(1)}, bf16[128,1536]{1,0:T(8,128)(2,1)}, u32[]{:S(2)}, u32[]{:S(2)}) %collective-permute-start.3) | collective-permute-done | bytes 393248 | tf_op jit(solution)/shard_map/ppermute | solution.py:341
  95.2 1.5 collective-permute-start.4
  99.3 8.2 %collective-permute-done.4.refs_1_ = bf16[128,1536]{1,0:T(8,128)(2,1)} collective-permute-done((bf16[128,1536]{1,0:T(8,128)(2,1)}, bf16[128,1536]{1,0:T(8,128)(2,1)}, u32[]{:S(2)}, u32[]{:S(2)}) %collective-permute-start.4) | collective-permute-done | bytes 393248 | tf_op jit(solution)/shard_map/ppermute | solution.py:341
  107.5 8.0 %collective-permute-done.6.refs_2_ = bf16[128,1536]{1,0:T(8,128)(2,1)} collective-permute-done((bf16[128,1536]{1,0:T(8,128)(2,1)}, bf16[128,1536]{1,0:T(8,128)(2,1)}, u32[]{:S(2)}, u32[]{:S(2)}) %collective-permute-start.6) | collective-permute-done | bytes 393248 | tf_op jit(solution)/shard_map/ppermute | solution.py:341
  115.5 20.5 %forward.1 = (bf16[4096,4096]{1,0:T(8,128)(2,1)}, bf16[128,4096]{1,0:T(8,128)(2,1)S(1)}, bf16[128,4096]{1,0:T(8,128)(2,1)S(1)}, f32[8,4096]{1,0:T(8,128)S(1)}, b...) custom-call(s32[1]{0:T(128)S(6)} %copy.17.len_ref, bf16[16,3,256,128]{3,2,1,0:T(8,128)(2,1)S(1)} %all-to-all-done.p_ref), custom_call_target="tpu_custom_call" | custom-call | flops 12884901888 | bytes 33554432 | tf_op jit(solution)/shard_map/forward/pallas_call | solution.py:139
  137.5 1.3 copy-done.2
  140.8 10.0 %project.2 = (bf16[128,4096]{1,0:T(8,128)(2,1)}, f32[8,4096]{1,0:T(8,128)}, f32[128,1536]{1,0:T(8,128)}) custom-call(s32[16]{0:T(128)} %stack.87.refs_0_, bf16[256,1536]{1,0:T(8,128)(2,1)} %bitcast.37, bf16[256,1536]{1,0:T(8,128)(2,1)} %copy-done.8, bf16[256,1536]{1,0:T(8,128)(2,1)} %copy-done.5, bf16[256,1536]{1,0:T(8,128)(2,1)} %copy-done.6, ...), custom_call_target="tpu_custom_call" | custom-call | flops 2818572288 | bytes 11010048 | tf_op jit(solution)/shard_map/project/pallas_call | solution.py:233
  150.8 5.4 %project.3 = (bf16[128,4096]{1,0:T(8,128)(2,1)}, f32[8,4096]{1,0:T(8,128)}, f32[128,1536]{1,0:T(8,128)}) custom-call(s32[4]{0:T(128)} %pad_add_fusion.refs_0_, bf16[128,1536]{1,0:T(8,128)(2,1)} %collective-permute-done.4.refs_1_, bf16[128,1536]{1,0:T(8,128)(2,1)} %collective-permute-done.6.refs_2_, bf16[128,1536]{1,0:T(8,128)(2,1)} %collective-permute-done.7.refs_3_, ...), custom_call_target="tpu_custom_call" | custom-call | flops 402653184 | bytes 1572864 | tf_op jit(solution)/shard_map/project/pallas_call | solution.py:233
  156.2 1.3 fusion.1
  158.4 6.8 %all-to-all-start.1 = ((bf16[8,128,192]{1,2,0:T(8,128)(2,1)}), bf16[8,128,192]{1,2,0:T(8,128)(2,1)S(1)}, u32[]{:S(2)}, u32[]{:S(2)}) async-start(bf16[8,128,192]{1,2,0:T(8,128)(2,1)} %bitcast.25), calls=%async_computation.1 | async-start | bytes 786432 | tf_op jit(solution)/shard_map/all_to_all | solution.py:397
  165.2 38.2 %backward.1 = bf16[16,3,256,128]{3,2,1,0:T(8,128)(2,1)} custom-call(bf16[4096,4096]{1,0:T(8,128)(2,1)} %get-tuple-element.29.e_ref, bf16[128,4096]{1,0:T(8,128)(2,1)} %get-tuple-element.38.g_ref, f32[8,4096]{1,0:T(8,128)} %get-tuple-element.39.d_ref, bf16[128,4096]{1,0:T(8,128)(2,1)} %copy-done.3, bf16[128,4096]{1,0:T(8,128)(2,1)} %copy-done.4, ...), custom_call_target="tpu_custom_call" | custom-call | flops 21474836480 | bytes 33554432 | tf_op jit(solution)/shard_map/backward/pallas_call | solution.py:300
  203.4 3.8 %all-to-all-start.2 = ((bf16[16,3,256,128]{3,2,1,0:T(8,128)(2,1)}), bf16[16,3,256,128]{3,2,1,0:T(8,128)(2,1)S(1)}, u32[]{:S(2)}, u32[]{:S(2)}) async-start(bf16[16,3,256,128]{3,2,1,0:T(8,128)(2,1)} %backward.1), calls=%async_computation.2 | async-start | bytes 6291456 | tf_op jit(solution)/shard_map/all_to_all | solution.py:400
  208.7 1.8 collective-permute-start.20
  210.5 34.8 %collective-permute-done.20 = f32[1728]{0:T(1024)S(1)} collective-permute-done((f32[1728]{0:T(1024)S(1)}, f32[1728]{0:T(1024)S(1)}, u32[]{:S(2)}, u32[]{:S(2)}) %collective-permute-start.20) | collective-permute-done | bytes 6944 | tf_op jit(solution)/shard_map/ppermute | solution.py:325
  245.8 3.5 %collective-permute-start.23 = (f32[128]{0:T(128)S(1)}, f32[128]{0:T(128)S(1)}, u32[]{:S(2)}, u32[]{:S(2)}) collective-permute-start(f32[128]{0:T(128)S(1)} %get-tuple-element.49), channel_id=1, source_target_pairs={{0,16},{16,0},{32,48},{48,32},{64,80},{80,64},{96,112},{112,96},{1... | collective-permute-start | bytes 1544 | tf_op jit(solution)/shard_map/ppermute | solution.py:325
  249.3 1.5 collective-permute-done.23
  250.8 2.0 collective-permute-start.24
  252.9 1.5 collective-permute-done.24
  254.4 3.5 %collective-permute-start.25 = (f32[128]{0:T(128)S(1)}, f32[128]{0:T(128)S(1)}, u32[]{:S(2)}, u32[]{:S(2)}) collective-permute-start(f32[128]{0:T(128)S(1)} %add.236), channel_id=1, source_target_pairs={{0,64},{16,80},{32,96},{48,112},{64,0},{80,16},{96,32},{112,48},{1... | collective-permute-start | bytes 1544 | tf_op jit(solution)/shard_map/ppermute | solution.py:325
  257.9 2.7 %collective-permute-start.22 = (f32[1728]{0:T(1024)S(1)}, f32[1728]{0:T(1024)S(1)}, u32[]{:S(2)}, u32[]{:S(2)}) collective-permute-start(f32[1728]{0:T(1024)S(1)} %add.233), channel_id=1, source_target_pairs={{0,8},{1,9},{2,10},{3,11},{4,12},{5,13},{6,14},{7,15},{8,0},{9,1},... | collective-permute-start | bytes 20744 | tf_op jit(solution)/shard_map/ppermute | solution.py:325
  261.8 1.3 collective-permute-done.22
  264.3 2.3 join_columns.1
  (79 shorter events, 17.7 us)
Async XLA Ops:
  0.6 19.5 %collective-permute-start = (bf16[256,1536]{1,0:T(8,128)(2,1)}, bf16[256,1536]{1,0:T(8,128)(2,1)S(1)}, u32[]{:S(2)}, u32[]{:S(2)}) collective-permute-start(bf16[256,1536]{1,0:T(8,128)(2,1)} %bitcast.33), channel_id=1, source_target_pairs={{0,2},{1,3},{2,0},{3,1},{4,6},{5,7},{6,4},{7,5},{8,10},{9,11},{10,... | collective-permute-start | bytes 2359304 | tf_op jit(solution)/shard_map/ppermute | solution.py:341
  2.4 21.5 %collective-permute-start.1 = (bf16[256,1536]{1,0:T(8,128)(2,1)}, bf16[256,1536]{1,0:T(8,128)(2,1)S(1)}, u32[]{:S(2)}, u32[]{:S(2)}) collective-permute-start(bf16[256,1536]{1,0:T(8,128)(2,1)} %bitcast.34), channel_id=1, source_target_pairs={{0,4},{1,5},{2,6},{3,7},{4,8},{5,9},{6,10},{7,11},{8,12},{9,13},{1... | collective-permute-start | bytes 2359304 | tf_op jit(solution)/shard_map/ppermute | solution.py:341
  4.3 19.6 %collective-permute-start.2 = (bf16[256,1536]{1,0:T(8,128)(2,1)}, bf16[256,1536]{1,0:T(8,128)(2,1)S(1)}, u32[]{:S(2)}, u32[]{:S(2)}) collective-permute-start(bf16[256,1536]{1,0:T(8,128)(2,1)} %bitcast.35), channel_id=1, source_target_pairs={{0,12},{1,13},{2,14},{3,15},{4,0},{5,1},{6,2},{7,3},{8,4},{9,5},{1... | collective-permute-start | bytes 2359304 | tf_op jit(solution)/shard_map/ppermute | solution.py:341
  10.9 83.0 %copy-start.11 = (f32[1,1536]{1,0:T(1,128)S(1)}, f32[1,1536]{1,0:T(1,128)}, u32[]{:S(2)}) copy-start(f32[1,1536]{1,0:T(1,128)} %param.13) | copy-start | bytes 18436
  10.9 86.6 %copy-start.7 = (bf16[128,1536]{1,0:T(8,128)(2,1)S(1)}, bf16[128,1536]{1,0:T(8,128)(2,1)}, u32[]{:S(2)}) copy-start(bf16[128,1536]{1,0:T(8,128)(2,1)} %param.15) | copy-start | bytes 1179652
  25.1 90.4 %all-to-all-start = ((bf16[16,3,256,128]{3,2,1,0:T(8,128)(2,1)}), bf16[16,3,256,128]{3,2,1,0:T(8,128)(2,1)S(1)}, u32[]{:S(2)}, u32[]{:S(2)}) async-start(bf16[16,3,256,128]{3,2,1,0:T(8,128)(2,1)} %split_columns.1), calls=%async_computation | async-start | bytes 6291456 | tf_op jit(solution)/shard_map/all_to_all | solution.py:361
  29.1 63.4 %collective-permute-start.11 = (bf16[256,1536]{1,0:T(8,128)(2,1)}, bf16[256,1536]{1,0:T(8,128)(2,1)}, u32[]{:S(2)}, u32[]{:S(2)}) collective-permute-start(bf16[256,1536]{1,0:T(8,128)(2,1)} %bitcast.36), channel_id=1, source_target_pairs={{0,1},{1,0},{2,3},{3,2},{4,5},{5,4},{6,7},{7,6},{8,9},{9,8},{10,11... | collective-permute-start | bytes 2359304 | tf_op jit(solution)/shard_map/ppermute | solution.py:341
  29.6 65.7 %collective-permute-start.9 = (bf16[256,1536]{1,0:T(8,128)(2,1)}, bf16[256,1536]{1,0:T(8,128)(2,1)}, u32[]{:S(2)}, u32[]{:S(2)}) collective-permute-start(bf16[256,1536]{1,0:T(8,128)(2,1)} %copy-done.8), channel_id=1, source_target_pairs={{0,4},{1,5},{2,6},{3,7},{4,8},{5,9},{6,10},{7,11},{8,12},{9,13},{1... | collective-permute-start | bytes 2359304 | tf_op jit(solution)/shard_map/ppermute | solution.py:341
  31.2 65.5 %collective-permute-start.10 = (bf16[256,1536]{1,0:T(8,128)(2,1)}, bf16[256,1536]{1,0:T(8,128)(2,1)}, u32[]{:S(2)}, u32[]{:S(2)}) collective-permute-start(bf16[256,1536]{1,0:T(8,128)(2,1)} %copy-done.8), channel_id=1, source_target_pairs={{0,12},{1,13},{2,14},{3,15},{4,0},{5,1},{6,2},{7,3},{8,4},{9,5},{1... | collective-permute-start | bytes 2359304 | tf_op jit(solution)/shard_map/ppermute | solution.py:341
  33.8 58.8 %collective-permute-start.3 = (bf16[128,1536]{1,0:T(8,128)(2,1)S(1)}, bf16[128,1536]{1,0:T(8,128)(2,1)}, u32[]{:S(2)}, u32[]{:S(2)}) collective-permute-start(bf16[128,1536]{1,0:T(8,128)(2,1)S(1)} %slice.12), channel_id=1, source_target_pairs={{0,4},{1,5},{2,6},{3,7},{4,8},{5,9},{6,10},{7,11},{8,12},{9,13},{1... | collective-permute-start | bytes 1179656 | tf_op jit(solution)/shard_map/ppermute | solution.py:341
  35.4 57.7 %collective-permute-start.5 = (bf16[128,1536]{1,0:T(8,128)(2,1)S(1)}, bf16[128,1536]{1,0:T(8,128)(2,1)}, u32[]{:S(2)}, u32[]{:S(2)}) collective-permute-start(bf16[128,1536]{1,0:T(8,128)(2,1)S(1)} %slice.13), channel_id=1, source_target_pairs={{0,12},{1,13},{2,14},{3,15},{4,0},{5,1},{6,2},{7,3},{8,4},{9,5},{1... | collective-permute-start | bytes 1179656 | tf_op jit(solution)/shard_map/ppermute | solution.py:341
  92.6 4.3 %collective-permute-start.15 = (bf16[128,1536]{1,0:T(8,128)(2,1)}, bf16[128,1536]{1,0:T(8,128)(2,1)}, u32[]{:S(2)}, u32[]{:S(2)}) collective-permute-start(bf16[128,1536]{1,0:T(8,128)(2,1)} %collective-permute-done.3.refs_5_), channel_id=1, source_target_pairs={{0,1},{1,0},{2,3},{3,2},{4,5},{5,4},{6,7},{7,6},{8,9},{9,8},{10,11... | collective-permute-start | bytes 1179656 | tf_op jit(solution)/shard_map/ppermute | solution.py:341
  92.6 6.2 %collective-permute-start.12 = (bf16[256,1536]{1,0:T(8,128)(2,1)}, bf16[256,1536]{1,0:T(8,128)(2,1)}, u32[]{:S(2)}, u32[]{:S(2)}) collective-permute-start(bf16[256,1536]{1,0:T(8,128)(2,1)} %copy-done.8), channel_id=1, source_target_pairs={{0,1},{1,0},{2,3},{3,2},{4,5},{5,4},{6,7},{7,6},{8,9},{9,8},{10,11... | collective-permute-start | bytes 2359304 | tf_op jit(solution)/shard_map/ppermute | solution.py:341
  93.1 6.1 %collective-permute-start.13 = (bf16[256,1536]{1,0:T(8,128)(2,1)}, bf16[256,1536]{1,0:T(8,128)(2,1)}, u32[]{:S(2)}, u32[]{:S(2)}) collective-permute-start(bf16[256,1536]{1,0:T(8,128)(2,1)} %copy-done.5), channel_id=1, source_target_pairs={{0,1},{1,0},{2,3},{3,2},{4,5},{5,4},{6,7},{7,6},{8,9},{9,8},{10,11... | collective-permute-start | bytes 2359304 | tf_op jit(solution)/shard_map/ppermute | solution.py:341
  95.2 12.2 %collective-permute-start.4 = (bf16[128,1536]{1,0:T(8,128)(2,1)}, bf16[128,1536]{1,0:T(8,128)(2,1)}, u32[]{:S(2)}, u32[]{:S(2)}) collective-permute-start(bf16[128,1536]{1,0:T(8,128)(2,1)} %collective-permute-done.3.refs_5_), channel_id=1, source_target_pairs={{0,2},{1,3},{2,0},{3,1},{4,6},{5,7},{6,4},{7,5},{8,10},{9,11},{10,... | collective-permute-start | bytes 1179656 | tf_op jit(solution)/shard_map/ppermute | solution.py:341
  96.7 1.9 collective-permute-start.16
  96.9 18.6 %collective-permute-start.6 = (bf16[128,1536]{1,0:T(8,128)(2,1)}, bf16[128,1536]{1,0:T(8,128)(2,1)}, u32[]{:S(2)}, u32[]{:S(2)}) collective-permute-start(bf16[128,1536]{1,0:T(8,128)(2,1)} %collective-permute-done.5.refs_6_), channel_id=1, source_target_pairs={{0,2},{1,3},{2,0},{3,1},{4,6},{5,7},{6,4},{7,5},{8,10},{9,11},{10,... | collective-permute-start | bytes 1179656 | tf_op jit(solution)/shard_map/ppermute | solution.py:341
  98.6 42.1 %collective-permute-start.14 = (bf16[256,1536]{1,0:T(8,128)(2,1)}, bf16[256,1536]{1,0:T(8,128)(2,1)}, u32[]{:S(2)}, u32[]{:S(2)}) collective-permute-start(bf16[256,1536]{1,0:T(8,128)(2,1)} %copy-done.6), channel_id=1, source_target_pairs={{0,1},{1,0},{2,3},{3,2},{4,5},{5,4},{6,7},{7,6},{8,9},{9,8},{10,11... | collective-permute-start | bytes 2359304 | tf_op jit(solution)/shard_map/ppermute | solution.py:341
  98.8 42.0 %collective-permute-start.17 = (bf16[256,1536]{1,0:T(8,128)(2,1)}, bf16[256,1536]{1,0:T(8,128)(2,1)}, u32[]{:S(2)}, u32[]{:S(2)}) collective-permute-start(bf16[256,1536]{1,0:T(8,128)(2,1)} %collective-permute-done.9.refs_7_), channel_id=1, source_target_pairs={{0,1},{1,0},{2,3},{3,2},{4,5},{5,4},{6,7},{7,6},{8,9},{9,8},{10,11... | collective-permute-start | bytes 2359304 | tf_op jit(solution)/shard_map/ppermute | solution.py:341
  99.2 41.6 %collective-permute-start.18 = (bf16[256,1536]{1,0:T(8,128)(2,1)}, bf16[256,1536]{1,0:T(8,128)(2,1)}, u32[]{:S(2)}, u32[]{:S(2)}) collective-permute-start(bf16[256,1536]{1,0:T(8,128)(2,1)} %collective-permute-done.10.refs_8_), channel_id=1, source_target_pairs={{0,1},{1,0},{2,3},{3,2},{4,5},{5,4},{6,7},{7,6},{8,9},{9,8},{10,11... | collective-permute-start | bytes 2359304 | tf_op jit(solution)/shard_map/ppermute | solution.py:341
  107.5 43.3 %collective-permute-start.7 = (bf16[128,1536]{1,0:T(8,128)(2,1)}, bf16[128,1536]{1,0:T(8,128)(2,1)}, u32[]{:S(2)}, u32[]{:S(2)}) collective-permute-start(bf16[128,1536]{1,0:T(8,128)(2,1)} %collective-permute-done.4.refs_1_), channel_id=1, source_target_pairs={{0,1},{1,0},{2,3},{3,2},{4,5},{5,4},{6,7},{7,6},{8,9},{9,8},{10,11... | collective-permute-start | bytes 1179656 | tf_op jit(solution)/shard_map/ppermute | solution.py:341
  115.4 35.4 %collective-permute-start.8 = (bf16[128,1536]{1,0:T(8,128)(2,1)}, bf16[128,1536]{1,0:T(8,128)(2,1)}, u32[]{:S(2)}, u32[]{:S(2)}) collective-permute-start(bf16[128,1536]{1,0:T(8,128)(2,1)} %collective-permute-done.6.refs_2_), channel_id=1, source_target_pairs={{0,1},{1,0},{2,3},{3,2},{4,5},{5,4},{6,7},{7,6},{8,9},{9,8},{10,11... | collective-permute-start | bytes 1179656 | tf_op jit(solution)/shard_map/ppermute | solution.py:341
  158.4 45.0 %all-to-all-start.1 = ((bf16[8,128,192]{1,2,0:T(8,128)(2,1)}), bf16[8,128,192]{1,2,0:T(8,128)(2,1)S(1)}, u32[]{:S(2)}, u32[]{:S(2)}) async-start(bf16[8,128,192]{1,2,0:T(8,128)(2,1)} %bitcast.25), calls=%async_computation.1 | async-start | bytes 786432 | tf_op jit(solution)/shard_map/all_to_all | solution.py:397
  203.4 60.4 %copy-start.12 = (f32[192]{0:T(256)S(1)}, f32[192]{0:T(256)}, u32[]{:S(2)}) copy-start(f32[192]{0:T(256)} %param.17) | copy-start | bytes 2308
  203.4 60.9 %all-to-all-start.2 = ((bf16[16,3,256,128]{3,2,1,0:T(8,128)(2,1)}), bf16[16,3,256,128]{3,2,1,0:T(8,128)(2,1)S(1)}, u32[]{:S(2)}, u32[]{:S(2)}) async-start(bf16[16,3,256,128]{3,2,1,0:T(8,128)(2,1)} %backward.1), calls=%async_computation.2 | async-start | bytes 6291456 | tf_op jit(solution)/shard_map/all_to_all | solution.py:400
  207.4 1.2 collective-permute-start.19
  208.7 36.6 %collective-permute-start.20 = (f32[1728]{0:T(1024)S(1)}, f32[1728]{0:T(1024)S(1)}, u32[]{:S(2)}, u32[]{:S(2)}) collective-permute-start(f32[1728]{0:T(1024)S(1)} %fusion.5), channel_id=1, source_target_pairs={{0,2},{1,3},{2,0},{3,1},{4,6},{5,7},{6,4},{7,5},{8,10},{9,11},{10,... | collective-permute-start | bytes 20744 | tf_op jit(solution)/shard_map/ppermute | solution.py:325
  245.3 12.6 %collective-permute-start.21 = (f32[1728]{0:T(1024)S(1)}, f32[1728]{0:T(1024)S(1)}, u32[]{:S(2)}, u32[]{:S(2)}) collective-permute-start(f32[1728]{0:T(1024)S(1)} %add.232), channel_id=1, source_target_pairs={{0,4},{1,5},{2,6},{3,7},{4,0},{5,1},{6,2},{7,3},{8,12},{9,13},{10,... | collective-permute-start | bytes 20744 | tf_op jit(solution)/shard_map/ppermute | solution.py:325
  245.8 5.0 %collective-permute-start.23 = (f32[128]{0:T(128)S(1)}, f32[128]{0:T(128)S(1)}, u32[]{:S(2)}, u32[]{:S(2)}) collective-permute-start(f32[128]{0:T(128)S(1)} %get-tuple-element.49), channel_id=1, source_target_pairs={{0,16},{16,0},{32,48},{48,32},{64,80},{80,64},{96,112},{112,96},{1... | collective-permute-start | bytes 1544 | tf_op jit(solution)/shard_map/ppermute | solution.py:325
  250.8 3.5 %collective-permute-start.24 = (f32[128]{0:T(128)S(1)}, f32[128]{0:T(128)S(1)}, u32[]{:S(2)}, u32[]{:S(2)}) collective-permute-start(f32[128]{0:T(128)S(1)} %add.235), channel_id=1, source_target_pairs={{0,32},{16,48},{32,0},{48,16},{64,96},{80,112},{96,64},{112,80},{1... | collective-permute-start | bytes 1544 | tf_op jit(solution)/shard_map/ppermute | solution.py:325
  254.4 6.2 %collective-permute-start.25 = (f32[128]{0:T(128)S(1)}, f32[128]{0:T(128)S(1)}, u32[]{:S(2)}, u32[]{:S(2)}) collective-permute-start(f32[128]{0:T(128)S(1)} %add.236), channel_id=1, source_target_pairs={{0,64},{16,80},{32,96},{48,112},{64,0},{80,16},{96,32},{112,48},{1... | collective-permute-start | bytes 1544 | tf_op jit(solution)/shard_map/ppermute | solution.py:325
  257.9 5.2 %collective-permute-start.22 = (f32[1728]{0:T(1024)S(1)}, f32[1728]{0:T(1024)S(1)}, u32[]{:S(2)}, u32[]{:S(2)}) collective-permute-start(f32[1728]{0:T(1024)S(1)} %add.233), channel_id=1, source_target_pairs={{0,8},{1,9},{2,10},{3,11},{4,12},{5,13},{6,14},{7,15},{8,0},{9,1},... | collective-permute-start | bytes 20744 | tf_op jit(solution)/shard_map/ppermute | solution.py:325
  (10 other events, 84.0 us)

commit v6 on v5

--- a/solution.py
+++ b/solution.py
@@ -43,28 +43,46 @@
     )(*sources)
 
 
-def join_columns(stacked):
-    heads, count, tokens, _ = stacked.shape
+def join_columns(early, late):
+    heads, _, half, _ = early.shape
     inner = heads * HEAD_DIM
-    block = tokens // 4
-
-    def body(*refs):
-        rows = pl.ds(pl.program_id(0) * block, block)
-        for which in range(count):
+
+    def body(early_ref, late_ref, dq, dk, dv, sums):
+        step = pl.program_id(0)
+        for head in range(heads):
+            lanes = slice(head * HEAD_DIM, (head + 1) * HEAD_DIM)
+            dq[:, lanes] = late_ref[head, pl.ds(step * half, half), :]
+
+        @pl.when(step == 0)
+        def _():
             for head in range(heads):
-                refs[1 + which][:, head * HEAD_DIM : (head + 1) * HEAD_DIM] = refs[0][
-                    head, which, rows, :
-                ]
-
+                lanes = slice(head * HEAD_DIM, (head + 1) * HEAD_DIM)
+                dk[:, lanes] = early_ref[head, 0]
+                dv[:, lanes] = early_ref[head, 1]
+            total = jnp.zeros((16, HEAD_DIM), F32)
+            for head in range(heads):
+                total = total + late_ref[head, 4 * half : 4 * half + 16, :].astype(F32)
+                total = total + late_ref[head, 4 * half + 16 : 4 * half + 32, :].astype(F32)
+            sums[...] = total
+
+        @pl.when(step == 1)
+        def _():
+            for head in range(heads):
+                lanes = slice(head * HEAD_DIM, (head + 1) * HEAD_DIM)
+                dk[:, lanes] = late_ref[head, 2 * half : 3 * half, :]
+                dv[:, lanes] = late_ref[head, 3 * half : 4 * half, :]
+
+    rows = pl.BlockSpec((half, inner), lambda i: (i, 0))
     return pl.pallas_call(
         body,
-        grid=(tokens // block,),
-        in_specs=[pl.BlockSpec(memory_space=pltpu.VMEM)],
-        out_specs=[pl.BlockSpec((block, inner), lambda i: (i, 0))] * count,
-        out_shape=[jax.ShapeDtypeStruct((tokens, inner), BF16)] * count,
-        compiler_params=pltpu.CompilerParams(vmem_limit_bytes=12 * 2**20),
+        grid=(2,),
+        in_specs=[pl.BlockSpec(memory_space=pltpu.VMEM)] * 2,
+        out_specs=[rows, rows, rows, pl.BlockSpec((16, HEAD_DIM), lambda i: (0, 0))],
+        out_shape=[jax.ShapeDtypeStruct((2 * half, inner), BF16)] * 3
+        + [jax.ShapeDtypeStruct((16, HEAD_DIM), F32)],
+        compiler_params=pltpu.CompilerParams(vmem_limit_bytes=16 * 2**20),
         name="join_columns",
-    )(stacked)
+    )(early, late)
 
 
 def forward(valid_len, packed):
@@ -82,17 +100,25 @@
 
         @pl.when(step == 0)
         def _():
-            key_rows = p_ref[:, 1].reshape(total, HEAD_DIM)
-            value_rows = p_ref[:, 2].reshape(total, HEAD_DIM)
-            row = lax.broadcasted_iota(jnp.int32, (total, HEAD_DIM), 0)
-            col = lax.broadcasted_iota(jnp.int32, (total, HEAD_DIM), 1)
-            ka[:, :HEAD_DIM] = key_rows
-            ka[:, HEAD_DIM:] = jnp.where((row >= length) & (col == 0), -1e30, 0.0).astype(BF16)
-            vt[:HEAD_DIM, :] = value_rows.T
+            half = tokens // 2
+            some = total // 2
+            row = lax.broadcasted_iota(jnp.int32, (some, HEAD_DIM), 0)
+            col = lax.broadcasted_iota(jnp.int32, (some, HEAD_DIM), 1)
             vt[HEAD_DIM:, :] = jnp.ones((16, total), BF16)
-            kt_ref[...] = key_rows.T
-            va_ref[:, :HEAD_DIM] = value_rows
-            va_ref[:, HEAD_DIM:] = jnp.where(col < 2, 1.0, 0.0).astype(BF16)
+            for part in range(2):
+                of = slice(part * half, (part + 1) * half)
+                at = slice(part * some, (part + 1) * some)
+                key_rows = p_ref[:, 1, of, :].reshape(some, HEAD_DIM)
+                value_rows = p_ref[:, 2, of, :].reshape(some, HEAD_DIM)
+                slot = row // half * tokens + part * half + row % half
+                ka[at, :HEAD_DIM] = key_rows
+                ka[at, HEAD_DIM:] = jnp.where((slot >= length) & (col == 0), -1e30, 0.0).astype(
+                    BF16
+                )
+                vt[:HEAD_DIM, at] = value_rows.T
+                kt_ref[:, at] = key_rows.T
+                va_ref[at, :HEAD_DIM] = value_rows
+                va_ref[at, HEAD_DIM:] = jnp.where(col < 2, 1.0, 0.0).astype(BF16)
 
         def live(block):
             slot = block * BLOCK + lax.broadcasted_iota(jnp.int32, (1, BLOCK), 1)
@@ -245,7 +271,7 @@
             pltpu.VMEM((sum(sizes), width), BF16),
             pltpu.SemaphoreType.DMA((count,)),
         ],
-        compiler_params=PARAMS,
+        compiler_params=pltpu.CompilerParams(vmem_limit_bytes=28 * 2**20),
         cost_estimate=pl.CostEstimate(
             flops=4 * sum(sizes) * width * HEAD_DIM,
             bytes_accessed=2 * sum(sizes) * width,
@@ -255,14 +281,20 @@
     )(places, *pieces, gated, attended, inverse, *earlier)
 
 
-def backward(low, grad, delta, query, key, value, parts):
+def backward(which, low, grad, delta, query, key, value, parts, earlier):
     total = low.shape[0]
-    tokens = total // parts
-    span = BLOCK // tokens
+    half = total // parts // 2
+    span = BLOCK // (2 * half)
     steps = total // BLOCK
+    some = total // 2
     chunk = 1024
 
-    def body(e_ref, g_ref, d_ref, q_ref, k_ref, v_ref, o_ref, dk, dv):
+    def body(*refs):
+        e_ref, g_ref, d_ref, q_ref, k_ref, v_ref = refs[:6]
+        if which:
+            dq_ref, extra_ref, o_ref, dk, dv = refs[6:]
+        else:
+            sum_ref, o_ref, dk, dv = refs[6:]
         step = pl.program_id(0)
 
         @pl.when(step == 0)
@@ -278,8 +310,8 @@
         widened = jnp.concatenate([grad_block, extra], axis=0)
         grad_rows = grad_block.T
         query_rows = q_ref[...].T
-        dq = jnp.zeros((HEAD_DIM, BLOCK), F32)
-        for first in range(0, total, chunk):
+        dq = dq_ref[...] if which else jnp.zeros((HEAD_DIM, BLOCK), F32)
+        for first in range(0, some, chunk):
             rows = slice(first, first + chunk)
             dprob = contract(v_ref[rows, :], widened, 1, 0)
             probs = e_ref[rows, :]
@@ -287,50 +319,75 @@
             dq = dq + contract(k_ref[:, rows], dscore, 1, 0)
             dv[rows, :] += contract(probs, grad_rows, 1, 0)
             dk[rows, :] += contract(dscore, query_rows, 1, 0)
-        dq = (dq * SCALE).T.astype(BF16).reshape(span, tokens, HEAD_DIM)
-        o_ref[pl.ds(step * span, span), 0] = dq
+        if which:
+            o_ref[pl.ds(step * span, span), : 2 * half, :] = (
+                (dq * SCALE).T.astype(BF16).reshape(span, 2 * half, HEAD_DIM)
+            )
+        else:
+            sum_ref[...] = dq
 
         @pl.when(step == steps - 1)
         def _():
-            o_ref[:, 1] = (dk[...] * SCALE).astype(BF16).reshape(parts, tokens, HEAD_DIM)
-            o_ref[:, 2] = dv[...].astype(BF16).reshape(parts, tokens, HEAD_DIM)
+            dk_low = (dk[...] * SCALE).astype(BF16).reshape(parts, half, HEAD_DIM)
+            dv_low = dv[...].astype(BF16).reshape(parts, half, HEAD_DIM)
+            if which:
+                o_ref[:, 2 * half : 3 * half, :] = dk_low
+                o_ref[:, 3 * half : 4 * half, :] = dv_low
+                vector = extra_ref[...]
+                first = vector.astype(BF16)
+                rest = (vector - first.astype(F32)).astype(BF16)
+                both = jnp.concatenate([first, rest], axis=0)
+                o_ref[:, 4 * half :, :] = jnp.broadcast_to(both[None], (parts, 32, HEAD_DIM))
+            else:
+                o_ref[:, 0] = dk_low
+                o_ref[:, 1] = dv_low
 
     column = lambda i: (0, i)
-    whole = lambda i: (0, 0)
+    shape = (parts, 4 * half + 32, HEAD_DIM) if which else (parts, 2, half, HEAD_DIM)
+    out_specs = [pl.BlockSpec(shape, lambda i: (0,) * len(shape))]
+    out_shape = [jax.ShapeDtypeStruct(shape, BF16)]
+    more = []
+    if which:
+        more = [
+            pl.BlockSpec((HEAD_DIM, BLOCK), column),
+            pl.BlockSpec((16, HEAD_DIM), lambda i: (0, 0)),
+        ]
+    else:
+        out_specs = [pl.BlockSpec((HEAD_DIM, BLOCK), column)] + out_specs
+        out_shape = [jax.ShapeDtypeStruct((HEAD_DIM, total), F32)] + out_shape
     return pl.pallas_call(
         body,
         grid=(steps,),
         in_specs=[
-            pl.BlockSpec((total, BLOCK), column),
+            pl.BlockSpec((some, BLOCK), lambda i: (which, i)),
             pl.BlockSpec((HEAD_DIM, BLOCK), column),
             pl.BlockSpec((8, BLOCK), column),
             pl.BlockSpec((HEAD_DIM, BLOCK), column),
-            pl.BlockSpec((HEAD_DIM, total), whole),
-            pl.BlockSpec((total, 2 * HEAD_DIM), whole),
-        ],
-        out_specs=pl.BlockSpec((parts, 3, tokens, HEAD_DIM), lambda i: (0, 0, 0, 0)),
-        out_shape=jax.ShapeDtypeStruct((parts, 3, tokens, HEAD_DIM), BF16),
-        scratch_shapes=[pltpu.VMEM((total, HEAD_DIM), F32)] * 2,
+            pl.BlockSpec((HEAD_DIM, some), lambda i: (0, which)),
+            pl.BlockSpec((some, 2 * HEAD_DIM), lambda i: (which, 0)),
+        ]
+        + more,
+        out_specs=out_specs,
+        out_shape=out_shape,
+        scratch_shapes=[pltpu.VMEM((some, HEAD_DIM), F32)] * 2,
         compiler_params=PARAMS,
         cost_estimate=pl.CostEstimate(
-            flops=10 * total * total * HEAD_DIM,
-            bytes_accessed=2 * total * total,
+            flops=5 * total * total * HEAD_DIM,
+            bytes_accessed=total * total,
             transcendentals=0,
         ),
         name="backward",
-    )(low, grad, delta, query, key, value)
+    )(low, grad, delta, query, key, value, *earlier)
 
 
 def swap(values, axis, size, bit):
     return lax.ppermute(values, axis, [(i, i ^ bit) for i in range(size)])
 
 
-def total_over(values, axis, size):
-    bit = 1
-    while bit < size:
-        values = values + swap(values, axis, size, bit)
-        bit *= 2
-    return values
+def total_over(values, axis):
+    one, two, three = (swap(values, axis, 8, bit) for bit in (1, 2, 3))
+    values = (values + one) + (two + three)
+    return values + swap(values, axis, 8, 4)
 
 
 def move(values, z_step=0, y_step=0, core_step=0):
@@ -361,7 +418,15 @@
     packed = lax.all_to_all(packed, "seq", 0, 0, tiled=True)
     far_low, far_high = move(below[:half], z_step=1), move(above[half:], z_step=3)
     side_below, side_above = move(side, z_step=1), move(side, z_step=3)
-    side_low, side_high = move(far_low, y_step=1), move(far_high, y_step=1)
+
+    weight = w_out.astype(F32)
+    gated = (weight * gate).astype(BF16)
+    results = forward(lengths, packed)
+    results, far_low, far_high, side_below, side_above = lax.optimization_barrier(
+        (results, far_low, far_high, side_below, side_above)
+    )
+    low, attended, query, inverse, key, value = results
+    side_low, side_high = move(side_below[:half], z_step=1), move(side_above[half:], z_step=3)
     found = [
         (own, 0, 0, 0),
         (side, 0, 1, 0),
@@ -376,12 +441,8 @@
     ]
     me = lax.axis_index("seq")
     z, y, core = me // 4, me // 2 % 2, me % 2
-
-    weight = w_out.astype(F32)
-    gated = (weight * gate).astype(BF16)
-    low, attended, query, inverse, key, value = forward(lengths, packed)
     made = []
-    for some in (found[:8], found[8:]):
+    for some in (found[:4], found[4:]):
         pieces, places = [], []
         for core_step in range(2):
             for rows, z_step, y_step, offset in some:
@@ -395,24 +456,30 @@
 
     partial = (outer * gate).astype(BF16).reshape(HEAD_DIM, dp_size, columns)
     partial = lax.all_to_all(partial.transpose(1, 0, 2), "dp", 0, 0, tiled=True)
-    back = backward(low, grad, delta, query, key, value, seq_size)
-    back, partial = lax.optimization_barrier((back, partial))
-    back = lax.all_to_all(back, "seq", 0, 0, tiled=True)
-
+    some_q, early = backward(0, low, grad, delta, query, key, value, seq_size, [])
+    some_q, early, partial = lax.optimization_barrier((some_q, early, partial))
+    early = lax.all_to_all(early, "seq", 0, 0, tiled=True)
     grad_weight = jnp.sum(partial.astype(F32), axis=0)
     squares = grad_weight * grad_weight + EPSILON
     gate_part = jnp.sum(weight * outer, axis=0)
-    row_total = total_over(jnp.sum(squares, axis=1), "dp", dp_size)
-    joined = jnp.concatenate([jnp.sum(squares, axis=0), gate_part])
-    joined = total_over(joined, "seq", seq_size)
+    row_total = total_over(jnp.sum(squares, axis=1), "dp")
+    joined = jnp.concatenate(
+        [gate_part, jnp.sum(squares, axis=0), jnp.zeros((320,), F32)]
+    ).reshape(16, HEAD_DIM)
+    (late,) = backward(
+        1, low, grad, delta, query, key, value, seq_size, [some_q, joined]
+    )
+    early, late = lax.optimization_barrier((early, late))
+    late = lax.all_to_all(late, "seq", 0, 0, tiled=True)
+    grad_q, grad_k, grad_v, joined = join_columns(early, late)
+    joined = joined.reshape(2048)
     row_new = 0.8 * row_moment + 0.2 * (row_total / width_dim)
-    col_new = 0.8 * col_moment + 0.2 * (joined[:columns] / inner_dim)
-    grad_q, grad_k, grad_v = join_columns(back)
+    col_new = 0.8 * col_moment + 0.2 * (joined[width_dim : width_dim + columns] / inner_dim)
     return (
         grad_q[None],
         grad_k[None],
         grad_v[None],
-        joined[columns:][None],
+        joined[:width_dim][None],
         grad_weight,
         row_new,
         col_new,

time: 267 us -> 253 us (0.948)
  waiting for transfers between devices: 124 us -> 104 us
  local copies, waits for them, and re-layouts: 10.4 us -> 17.8 us
    ppermute x7 -> x4, waiting for transfers between devices: 40 us -> 27.2 us  [swap(): return lax.ppermute(values, axis, [(i, i ^ bit) for i in range(size)])]
    all_to_all x1 -> x2, starting transfers between devices: 3.75 us -> 11.1 us  [the longest x1 5.72 us: shards(): late = lax.all_to_all(late, 'seq', 0, 0, tiled=True)]
    ppermute x19, waiting for transfers between devices: 83.9 us -> 76.6 us  [move(): return lax.ppermute(values, 'seq', pairs)]
    ppermute x7 -> x4, starting transfers between devices: 14.4 us -> 8.85 us  [swap(): return lax.ppermute(values, axis, [(i, i ^ bit) for i in range(size)])]
    unnamed x26 -> x40, local copies, waits for them, and re-layouts: 6.05 us -> 11.3 us
    pallas_call x2, Pallas kernels: 15.4 us -> 10.8 us  [project(): pl.pallas_call(body, in_specs=[pl.BlockSpec(memory_space=pltpu.SMEM)] + [...]
    pallas_call x2 -> x3, Pallas kernels: 40.5 us -> 43.7 us  [the longest x2 41.6 us: backward(): pl.pallas_call(body, grid=(steps,), in_specs=[pl.BlockSpec((some, BLOCK),...]
  transfers between devices with their start and end apart: 29 -> 27, of which waited for: 11 -> 7; matrix products, arithmetic and copies ran while one was open for 3% -> 3% of each run, Pallas kernels for 27% -> 28%
where the time goes in v6:
time: 253 us; the launch traced here: 252 us
  waiting for transfers between devices  104 us (41%)
  Pallas kernels  79.4 us (31%)
  starting transfers between devices  47.3 us (19%)
  local copies, waits for them, and re-layouts  17.8 us (7%)
    ppermute x19, waiting for transfers between devices, move(): return lax.ppermute(values, 'seq', pairs)  76.6 us
    pallas_call x2, Pallas kernels, backward(): pl.pallas_call(body, grid=(steps,), in_specs=[pl.BlockSpec((some, BLOCK),...  41.6 us
    ppermute x4, waiting for transfers between devices, swap(): return lax.ppermute(values, axis, [(i, i ^ bit) for i in range(size)])  27.2 us
    pallas_call x1, Pallas kernels, forward(): pl.pallas_call(body, grid_spec=pltpu.PrefetchScalarGridSpec(num_scalar_pr...  20.5 us
    ppermute x19, starting transfers between devices, move(): return lax.ppermute(values, 'seq', pairs)  16.2 us
    unnamed x40, local copies, waits for them, and re-layouts  11.3 us
    pallas_call x2, Pallas kernels, project(): pl.pallas_call(body, in_specs=[pl.BlockSpec(memory_space=pltpu.SMEM)] + [...  10.8 us
    ppermute x4, starting transfers between devices, swap(): return lax.ppermute(values, axis, [(i, i ^ bit) for i in range(size)])  8.85 us
  transfers between devices with their start and end apart: 27, of which 7 were waited for; matrix products, arithmetic and copies ran while one was open for 3% of the time, Pallas kernels for 28%

profile of v6, /device:TPU:0, one launch (start us, length us, event | category | flops | bytes accessed | tf_op | source)
XLA Modules:
  0.0 252.2 jit_solution(15749205203839210018)
XLA Ops:
  0.6 1.7 collective-permute-start
  2.4 1.9 collective-permute-start.1
  4.3 2.1 collective-permute-start.2
  6.4 4.4 %split_columns.1 = bf16[16,3,256,128]{3,2,1,0:T(8,128)(2,1)} custom-call(bf16[256,2048]{1,0:T(8,128)(2,1)} %bitcast.44, bf16[256,2048]{1,0:T(8,128)(2,1)} %bitcast.45, bf16[256,2048]{1,0:T(8,128)(2,1)} %bitcast.46), custom_call_target="tpu_custom_call" | custom-call | tf_op jit(solution)/shard_map/split_columns/pallas_call | solution.py:36
  10.8 9.4 %collective-permute-done.refs_2_ = bf16[256,1536]{1,0:T(8,128)(2,1)S(1)} collective-permute-done((bf16[256,1536]{1,0:T(8,128)(2,1)}, bf16[256,1536]{1,0:T(8,128)(2,1)S(1)}, u32[]{:S(2)}, u32[]{:S(2)}) %collective-permute-start) | collective-permute-done | bytes 786464 | tf_op jit(solution)/shard_map/ppermute | solution.py:398
  20.1 3.9 %collective-permute-done.1.refs_3_ = bf16[256,1536]{1,0:T(8,128)(2,1)} collective-permute-done((bf16[256,1536]{1,0:T(8,128)(2,1)}, bf16[256,1536]{1,0:T(8,128)(2,1)}, u32[]{:S(2)}, u32[]{:S(2)}) %collective-permute-start.1) | collective-permute-done | bytes 786464 | tf_op jit(solution)/shard_map/ppermute | solution.py:398
  24.0 4.3 %all-to-all-start = ((bf16[16,3,256,128]{3,2,1,0:T(8,128)(2,1)}), bf16[16,3,256,128]{3,2,1,0:T(8,128)(2,1)S(1)}, u32[]{:S(2)}, u32[]{:S(2)}) async-start(bf16[16,3,256,128]{3,2,1,0:T(8,128)(2,1)} %split_columns.1), calls=%async_computation | async-start | bytes 6291456 | tf_op jit(solution)/shard_map/all_to_all | solution.py:418
  28.3 1.9 collective-permute-start.5
  31.3 1.5 collective-permute-start.3
  33.9 1.8 collective-permute-start.4
  36.6 55.1 %collective-permute-done.3.refs_1_ = bf16[128,1536]{1,0:T(8,128)(2,1)S(1)} collective-permute-done((bf16[128,1536]{1,0:T(8,128)(2,1)S(1)}, bf16[128,1536]{1,0:T(8,128)(2,1)S(1)}, u32[]{:S(2)}, u32[]{:S(2)}) %collective-permute-start.3) | collective-permute-done | bytes 393248 | tf_op jit(solution)/shard_map/ppermute | solution.py:398
  93.3 1.6 copy-done
  95.0 1.9 copy-done.1
  96.9 20.5 %forward.1 = (bf16[4096,4096]{1,0:T(8,128)(2,1)}, bf16[128,4096]{1,0:T(8,128)(2,1)S(1)}, bf16[128,4096]{1,0:T(8,128)(2,1)S(1)}, f32[8,4096]{1,0:T(8,128)S(1)}, b...) custom-call(s32[1]{0:T(128)S(6)} %copy.20.len_ref, bf16[16,3,256,128]{3,2,1,0:T(8,128)(2,1)S(1)} %copy-done.1), custom_call_target="tpu_custom_call" | custom-call | flops 12884901888 | bytes 33554432 | tf_op jit(solution)/shard_map/forward/pallas_call | solution.py:165
  117.4 1.3 copy-done.2
  120.5 1.8 slice.22
  122.3 3.2 %collective-permute-start.8 = (bf16[128,1536]{1,0:T(8,128)(2,1)}, bf16[128,1536]{1,0:T(8,128)(2,1)}, u32[]{:S(2)}, u32[]{:S(2)}) collective-permute-start(bf16[128,1536]{1,0:T(8,128)(2,1)} %slice.22), channel_id=1, source_target_pairs={{0,12},{1,13},{2,14},{3,15},{4,0},{5,1},{6,2},{7,3},{8,4},{9,5},{1... | collective-permute-start | bytes 1179656 | tf_op jit(solution)/shard_map/ppermute | solution.py:398
  126.4 7.2 %collective-permute-done.7.refs_5_ = bf16[128,1536]{1,0:T(8,128)(2,1)} collective-permute-done((bf16[128,1536]{1,0:T(8,128)(2,1)}, bf16[128,1536]{1,0:T(8,128)(2,1)}, u32[]{:S(2)}, u32[]{:S(2)}) %collective-permute-start.7) | collective-permute-done | bytes 393248 | tf_op jit(solution)/shard_map/ppermute | solution.py:398
  137.4 1.1 copy-done.10
  138.5 5.3 %project.2 = (bf16[128,4096]{1,0:T(8,128)(2,1)S(1)}, f32[8,4096]{1,0:T(8,128)S(1)}, f32[128,1536]{1,0:T(8,128)S(1)}) custom-call(s32[8]{0:T(128)S(1)} %stack.87.refs_0_, bf16[256,1536]{1,0:T(8,128)(2,1)S(1)} %bitcast.42, bf16[256,1536]{1,0:T(8,128)(2,1)S(1)} %copy-done.10, bf16[256,1536]{1,0:T(8,128)(2,1)} %collective-permute-done.1.refs_3_, ...), custom_call_target="tpu_custom_call" | custom-call | flops 1610612736 | bytes 6291456 | tf_op jit(solution)/shard_map/project/pallas_call | solution.py:259
  143.9 5.5 %project.3 = (bf16[128,4096]{1,0:T(8,128)(2,1)S(1)}, f32[8,4096]{1,0:T(8,128)S(1)}, f32[128,1536]{1,0:T(8,128)S(1)}) custom-call(s32[12]{0:T(128)S(1)} %stack.78.refs_0_, bf16[128,1536]{1,0:T(8,128)(2,1)S(1)} %copy-done.12, bf16[128,1536]{1,0:T(8,128)(2,1)} %collective-permute-done.4.refs_2_, bf16[256,1536]{1,0:T(8,128)(2,1)S(1)} %copy-done.4, ...), custom_call_target="tpu_custom_call" | custom-call | flops 1610612736 | bytes 6291456 | tf_op jit(solution)/shard_map/project/pallas_call | solution.py:259
  151.9 6.8 %all-to-all-start.1 = ((bf16[8,128,192]{1,2,0:T(8,128)(2,1)}), bf16[8,128,192]{1,2,0:T(8,128)(2,1)S(1)}, u32[]{:S(2)}, u32[]{:S(2)}) async-start(bf16[8,128,192]{1,2,0:T(8,128)(2,1)} %bitcast.25), calls=%async_computation.1 | async-start | bytes 786432 | tf_op jit(solution)/shard_map/all_to_all | solution.py:458
  158.7 20.6 %backward.2 = (f32[128,4096]{1,0:T(8,128)}, bf16[16,2,128,128]{3,2,1,0:T(8,128)(2,1)}) custom-call(bf16[4096,4096]{1,0:T(8,128)(2,1)} %get-tuple-element.54.refs_0_, bf16[128,4096]{1,0:T(8,128)(2,1)} %copy-done.7, f32[8,4096]{1,0:T(8,128)} %copy-done.13, bf16[128,4096]{1,0:T(8,128)(2,1)} %copy-done.5, bf16[128,4096]{1,0:T(8,128)(2,1)} %copy-done.6, ...), custom_call_target="tpu_custom_call" | custom-call | flops 10737418240 | bytes 16777216 | tf_op jit(solution)/shard_map/backward/pallas_call | solution.py:358
  179.5 5.4 %all-to-all-start.2 = ((bf16[16,2,128,128]{3,2,1,0:T(8,128)(2,1)}), bf16[16,2,128,128]{3,2,1,0:T(8,128)(2,1)S(1)}, u32[]{:S(2)}, u32[]{:S(2)}) async-start(bf16[16,2,128,128]{3,2,1,0:T(8,128)(2,1)} %get-tuple-element.72), calls=%async_computation.2 | async-start | bytes 2097152 | tf_op jit(solution)/shard_map/all_to_all | solution.py:461
  185.6 21.1 %backward.3 = bf16[16,544,128]{2,1,0:T(8,128)(2,1)} custom-call(bf16[4096,4096]{1,0:T(8,128)(2,1)} %get-tuple-element.54.refs_0_, bf16[128,4096]{1,0:T(8,128)(2,1)} %copy-done.7, f32[8,4096]{1,0:T(8,128)} %copy-done.13, bf16[128,4096]{1,0:T(8,128)(2,1)} %copy-done.5, bf16[128,4096]{1,0:T(8,128)(2,1)} %copy-done.6, bf16[4096,256]{1,0:T(8,128)(2,1)} %copy-done.2, ...), custom_call_target="tpu_custom_call" | custom-call | flops 10737418240 | bytes 16777216 | tf_op jit(solution)/shard_map/backward/pallas_call | solution.py:358
  206.6 5.7 %all-to-all-start.3 = ((bf16[16,544,128]{2,1,0:T(8,128)(2,1)}), bf16[16,544,128]{2,1,0:T(8,128)(2,1)S(1)}, u32[]{:S(2)}, u32[]{:S(2)}) async-start(bf16[16,544,128]{2,1,0:T(8,128)(2,1)} %backward.3), calls=%async_computation.3 | async-start | bytes 4456448 | tf_op jit(solution)/shard_map/all_to_all | solution.py:473
  212.4 4.3 %collective-permute-start.19 = (f32[128]{0:T(128)S(1)}, f32[128]{0:T(128)S(1)}, u32[]{:S(2)}, u32[]{:S(2)}) collective-permute-start(f32[128]{0:T(128)S(1)} %get-tuple-element.81), channel_id=1, source_target_pairs={{0,16},{16,0},{32,48},{48,32},{64,80},{80,64},{96,112},{112,96},{1... | collective-permute-start | bytes 1544 | tf_op jit(solution)/shard_map/ppermute | solution.py:384
  216.6 1.5 collective-permute-start.20
  218.2 25.1 %collective-permute-done.19 = f32[128]{0:T(128)S(1)} collective-permute-done((f32[128]{0:T(128)S(1)}, f32[128]{0:T(128)S(1)}, u32[]{:S(2)}, u32[]{:S(2)}) %collective-permute-start.19) | collective-permute-done | bytes 544 | tf_op jit(solution)/shard_map/ppermute | solution.py:384
  243.3 3.0 %collective-permute-start.22 = (f32[128]{0:T(128)S(1)}, f32[128]{0:T(128)S(1)}, u32[]{:S(2)}, u32[]{:S(2)}) collective-permute-start(f32[128]{0:T(128)S(1)} %add_add_fusion), channel_id=1, source_target_pairs={{0,64},{16,80},{32,96},{48,112},{64,0},{80,16},{96,32},{112,48},{1... | collective-permute-start | bytes 1544 | tf_op jit(solution)/shard_map/ppermute | solution.py:384
  246.3 2.1 collective-permute-done.22
  248.9 2.1 join_columns.1
  (86 shorter events, 15.5 us)
Async XLA Ops:
  0.6 19.5 %collective-permute-start = (bf16[256,1536]{1,0:T(8,128)(2,1)}, bf16[256,1536]{1,0:T(8,128)(2,1)S(1)}, u32[]{:S(2)}, u32[]{:S(2)}) collective-permute-start(bf16[256,1536]{1,0:T(8,128)(2,1)} %bitcast.38), channel_id=1, source_target_pairs={{0,2},{1,3},{2,0},{3,1},{4,6},{5,7},{6,4},{7,5},{8,10},{9,11},{10,... | collective-permute-start | bytes 2359304 | tf_op jit(solution)/shard_map/ppermute | solution.py:398
  2.4 21.6 %collective-permute-start.1 = (bf16[256,1536]{1,0:T(8,128)(2,1)}, bf16[256,1536]{1,0:T(8,128)(2,1)}, u32[]{:S(2)}, u32[]{:S(2)}) collective-permute-start(bf16[256,1536]{1,0:T(8,128)(2,1)} %bitcast.39), channel_id=1, source_target_pairs={{0,4},{1,5},{2,6},{3,7},{4,8},{5,9},{6,10},{7,11},{8,12},{9,13},{1... | collective-permute-start | bytes 2359304 | tf_op jit(solution)/shard_map/ppermute | solution.py:398
  4.3 19.7 %collective-permute-start.2 = (bf16[256,1536]{1,0:T(8,128)(2,1)}, bf16[256,1536]{1,0:T(8,128)(2,1)}, u32[]{:S(2)}, u32[]{:S(2)}) collective-permute-start(bf16[256,1536]{1,0:T(8,128)(2,1)} %bitcast.40), channel_id=1, source_target_pairs={{0,12},{1,13},{2,14},{3,15},{4,0},{5,1},{6,2},{7,3},{8,4},{9,5},{1... | collective-permute-start | bytes 2359304 | tf_op jit(solution)/shard_map/ppermute | solution.py:398
  24.0 69.3 %all-to-all-start = ((bf16[16,3,256,128]{3,2,1,0:T(8,128)(2,1)}), bf16[16,3,256,128]{3,2,1,0:T(8,128)(2,1)S(1)}, u32[]{:S(2)}, u32[]{:S(2)}) async-start(bf16[16,3,256,128]{3,2,1,0:T(8,128)(2,1)} %split_columns.1), calls=%async_computation | async-start | bytes 6291456 | tf_op jit(solution)/shard_map/all_to_all | solution.py:418
  28.3 63.8 %collective-permute-start.5 = (bf16[256,1536]{1,0:T(8,128)(2,1)}, bf16[256,1536]{1,0:T(8,128)(2,1)S(1)}, u32[]{:S(2)}, u32[]{:S(2)}) collective-permute-start(bf16[256,1536]{1,0:T(8,128)(2,1)} %copy-done.9), channel_id=1, source_target_pairs={{0,4},{1,5},{2,6},{3,7},{4,8},{5,9},{6,10},{7,11},{8,12},{9,13},{1... | collective-permute-start | bytes 2359304 | tf_op jit(solution)/shard_map/ppermute | solution.py:398
  31.3 60.4 %collective-permute-start.3 = (bf16[128,1536]{1,0:T(8,128)(2,1)S(1)}, bf16[128,1536]{1,0:T(8,128)(2,1)S(1)}, u32[]{:S(2)}, u32[]{:S(2)}) collective-permute-start(bf16[128,1536]{1,0:T(8,128)(2,1)S(1)} %slice.19), channel_id=1, source_target_pairs={{0,4},{1,5},{2,6},{3,7},{4,8},{5,9},{6,10},{7,11},{8,12},{9,13},{1... | collective-permute-start | bytes 1179656 | tf_op jit(solution)/shard_map/ppermute | solution.py:398
  32.8 93.3 %copy-start.16 = (f32[1,1536]{1,0:T(1,128)S(1)}, f32[1,1536]{1,0:T(1,128)}, u32[]{:S(2)}) copy-start(f32[1,1536]{1,0:T(1,128)} %param.13) | copy-start | bytes 18436
  33.9 57.8 %collective-permute-start.4 = (bf16[128,1536]{1,0:T(8,128)(2,1)S(1)}, bf16[128,1536]{1,0:T(8,128)(2,1)}, u32[]{:S(2)}, u32[]{:S(2)}) collective-permute-start(bf16[128,1536]{1,0:T(8,128)(2,1)S(1)} %slice.20), channel_id=1, source_target_pairs={{0,12},{1,13},{2,14},{3,15},{4,0},{5,1},{6,2},{7,3},{8,4},{9,5},{1... | collective-permute-start | bytes 1179656 | tf_op jit(solution)/shard_map/ppermute | solution.py:398
  35.7 86.6 %collective-permute-start.15 = (bf16[256,1536]{1,0:T(8,128)(2,1)}, bf16[256,1536]{1,0:T(8,128)(2,1)}, u32[]{:S(2)}, u32[]{:S(2)}) collective-permute-start(bf16[256,1536]{1,0:T(8,128)(2,1)} %bitcast.41), channel_id=1, source_target_pairs={{0,1},{1,0},{2,3},{3,2},{4,5},{5,4},{6,7},{7,6},{8,9},{9,8},{10,11... | collective-permute-start | bytes 2359304 | tf_op jit(solution)/shard_map/ppermute | solution.py:398
  36.4 83.3 %collective-permute-start.6 = (bf16[256,1536]{1,0:T(8,128)(2,1)}, bf16[256,1536]{1,0:T(8,128)(2,1)}, u32[]{:S(2)}, u32[]{:S(2)}) collective-permute-start(bf16[256,1536]{1,0:T(8,128)(2,1)} %copy-done.9), channel_id=1, source_target_pairs={{0,12},{1,13},{2,14},{3,15},{4,0},{5,1},{6,2},{7,3},{8,4},{9,5},{1... | collective-permute-start | bytes 2359304 | tf_op jit(solution)/shard_map/ppermute | solution.py:398
  91.7 33.9 %collective-permute-start.16 = (bf16[256,1536]{1,0:T(8,128)(2,1)}, bf16[256,1536]{1,0:T(8,128)(2,1)}, u32[]{:S(2)}, u32[]{:S(2)}) collective-permute-start(bf16[256,1536]{1,0:T(8,128)(2,1)} %copy-done.9), channel_id=1, source_target_pairs={{0,1},{1,0},{2,3},{3,2},{4,5},{5,4},{6,7},{7,6},{8,9},{9,8},{10,11... | collective-permute-start | bytes 2359304 | tf_op jit(solution)/shard_map/ppermute | solution.py:398
  91.7 33.9 %collective-permute-start.17 = (bf16[256,1536]{1,0:T(8,128)(2,1)}, bf16[256,1536]{1,0:T(8,128)(2,1)}, u32[]{:S(2)}, u32[]{:S(2)}) collective-permute-start(bf16[256,1536]{1,0:T(8,128)(2,1)} %collective-permute-done.1.refs_3_), channel_id=1, source_target_pairs={{0,1},{1,0},{2,3},{3,2},{4,5},{5,4},{6,7},{7,6},{8,9},{9,8},{10,11... | collective-permute-start | bytes 2359304 | tf_op jit(solution)/shard_map/ppermute | solution.py:398
  93.3 32.8 %collective-permute-start.18 = (bf16[256,1536]{1,0:T(8,128)(2,1)}, bf16[256,1536]{1,0:T(8,128)(2,1)}, u32[]{:S(2)}, u32[]{:S(2)}) collective-permute-start(bf16[256,1536]{1,0:T(8,128)(2,1)} %collective-permute-done.2.refs_4_), channel_id=1, source_target_pairs={{0,1},{1,0},{2,3},{3,2},{4,5},{5,4},{6,7},{7,6},{8,9},{9,8},{10,11... | collective-permute-start | bytes 2359304 | tf_op jit(solution)/shard_map/ppermute | solution.py:398
  96.9 22.8 %copy-start.4 = (bf16[256,1536]{1,0:T(8,128)(2,1)S(1)}, bf16[256,1536]{1,0:T(8,128)(2,1)}, u32[]{:S(2)}) copy-start(bf16[256,1536]{1,0:T(8,128)(2,1)} %copy-done.3) | copy-start | bytes 2359300
  120.5 13.1 %collective-permute-start.7 = (bf16[128,1536]{1,0:T(8,128)(2,1)}, bf16[128,1536]{1,0:T(8,128)(2,1)}, u32[]{:S(2)}, u32[]{:S(2)}) collective-permute-start(bf16[128,1536]{1,0:T(8,128)(2,1)} %slice.21), channel_id=1, source_target_pairs={{0,4},{1,5},{2,6},{3,7},{4,8},{5,9},{6,10},{7,11},{8,12},{9,13},{1... | collective-permute-start | bytes 1179656 | tf_op jit(solution)/shard_map/ppermute | solution.py:398
  122.3 12.3 %collective-permute-start.8 = (bf16[128,1536]{1,0:T(8,128)(2,1)}, bf16[128,1536]{1,0:T(8,128)(2,1)}, u32[]{:S(2)}, u32[]{:S(2)}) collective-permute-start(bf16[128,1536]{1,0:T(8,128)(2,1)} %slice.22), channel_id=1, source_target_pairs={{0,12},{1,13},{2,14},{3,15},{4,0},{5,1},{6,2},{7,3},{8,4},{9,5},{1... | collective-permute-start | bytes 1179656 | tf_op jit(solution)/shard_map/ppermute | solution.py:398
  125.5 9.1 %collective-permute-start.10 = (bf16[128,1536]{1,0:T(8,128)(2,1)}, bf16[128,1536]{1,0:T(8,128)(2,1)}, u32[]{:S(2)}, u32[]{:S(2)}) collective-permute-start(bf16[128,1536]{1,0:T(8,128)(2,1)} %collective-permute-done.4.refs_2_), channel_id=1, source_target_pairs={{0,1},{1,0},{2,3},{3,2},{4,5},{5,4},{6,7},{7,6},{8,9},{9,8},{10,11... | collective-permute-start | bytes 1179656 | tf_op jit(solution)/shard_map/ppermute | solution.py:398
  125.6 18.2 %collective-permute-start.11 = (bf16[256,1536]{1,0:T(8,128)(2,1)S(1)}, bf16[256,1536]{1,0:T(8,128)(2,1)S(1)}, u32[]{:S(2)}, u32[]{:S(2)}) collective-permute-start(bf16[256,1536]{1,0:T(8,128)(2,1)S(1)} %copy-done.4), channel_id=1, source_target_pairs={{0,1},{1,0},{2,3},{3,2},{4,5},{5,4},{6,7},{7,6},{8,9},{9,8},{10,11... | collective-permute-start | bytes 2359304 | tf_op jit(solution)/shard_map/ppermute | solution.py:398
  126.1 17.7 %collective-permute-start.12 = (bf16[256,1536]{1,0:T(8,128)(2,1)}, bf16[256,1536]{1,0:T(8,128)(2,1)S(1)}, u32[]{:S(2)}, u32[]{:S(2)}) collective-permute-start(bf16[256,1536]{1,0:T(8,128)(2,1)} %collective-permute-done.6.refs_4_), channel_id=1, source_target_pairs={{0,1},{1,0},{2,3},{3,2},{4,5},{5,4},{6,7},{7,6},{8,9},{9,8},{10,11... | collective-permute-start | bytes 2359304 | tf_op jit(solution)/shard_map/ppermute | solution.py:398
  133.6 10.2 %collective-permute-start.9 = (bf16[128,1536]{1,0:T(8,128)(2,1)}, bf16[128,1536]{1,0:T(8,128)(2,1)S(1)}, u32[]{:S(2)}, u32[]{:S(2)}) collective-permute-start(bf16[128,1536]{1,0:T(8,128)(2,1)} %copy-done.11), channel_id=1, source_target_pairs={{0,1},{1,0},{2,3},{3,2},{4,5},{5,4},{6,7},{7,6},{8,9},{9,8},{10,11... | collective-permute-start | bytes 1179656 | tf_op jit(solution)/shard_map/ppermute | solution.py:398
  134.6 9.2 %collective-permute-start.13 = (bf16[128,1536]{1,0:T(8,128)(2,1)}, bf16[128,1536]{1,0:T(8,128)(2,1)S(1)}, u32[]{:S(2)}, u32[]{:S(2)}) collective-permute-start(bf16[128,1536]{1,0:T(8,128)(2,1)} %collective-permute-done.7.refs_5_), channel_id=1, source_target_pairs={{0,1},{1,0},{2,3},{3,2},{4,5},{5,4},{6,7},{7,6},{8,9},{9,8},{10,11... | collective-permute-start | bytes 1179656 | tf_op jit(solution)/shard_map/ppermute | solution.py:398
  134.6 9.2 %collective-permute-start.14 = (bf16[128,1536]{1,0:T(8,128)(2,1)}, bf16[128,1536]{1,0:T(8,128)(2,1)S(1)}, u32[]{:S(2)}, u32[]{:S(2)}) collective-permute-start(bf16[128,1536]{1,0:T(8,128)(2,1)} %collective-permute-done.8.refs_6_), channel_id=1, source_target_pairs={{0,1},{1,0},{2,3},{3,2},{4,5},{5,4},{6,7},{7,6},{8,9},{9,8},{10,11... | collective-permute-start | bytes 1179656 | tf_op jit(solution)/shard_map/ppermute | solution.py:398
  151.9 27.4 %all-to-all-start.1 = ((bf16[8,128,192]{1,2,0:T(8,128)(2,1)}), bf16[8,128,192]{1,2,0:T(8,128)(2,1)S(1)}, u32[]{:S(2)}, u32[]{:S(2)}) async-start(bf16[8,128,192]{1,2,0:T(8,128)(2,1)} %bitcast.25), calls=%async_computation.1 | async-start | bytes 786432 | tf_op jit(solution)/shard_map/all_to_all | solution.py:458
  179.3 27.3 %copy-start.15 = (f32[128,192]{0,1:T(8,128)}, f32[128,192]{0,1:T(8,128)S(1)}, u32[]{:S(2)}) copy-start(f32[128,192]{0,1:T(8,128)S(1)} %convert_reduce_fusion) | copy-start | bytes 294916
  179.5 27.2 %all-to-all-start.2 = ((bf16[16,2,128,128]{3,2,1,0:T(8,128)(2,1)}), bf16[16,2,128,128]{3,2,1,0:T(8,128)(2,1)S(1)}, u32[]{:S(2)}, u32[]{:S(2)}) async-start(bf16[16,2,128,128]{3,2,1,0:T(8,128)(2,1)} %get-tuple-element.72), calls=%async_computation.2 | async-start | bytes 2097152 | tf_op jit(solution)/shard_map/all_to_all | solution.py:461
  206.6 41.8 %copy-start.18 = (f32[128]{0:T(128)S(1)}, f32[128]{0:T(128)}, u32[]{:S(2)}) copy-start(f32[128]{0:T(128)} %param.16) | copy-start | bytes 1540
  206.6 42.3 %all-to-all-start.3 = ((bf16[16,544,128]{2,1,0:T(8,128)(2,1)}), bf16[16,544,128]{2,1,0:T(8,128)(2,1)S(1)}, u32[]{:S(2)}, u32[]{:S(2)}) async-start(bf16[16,544,128]{2,1,0:T(8,128)(2,1)} %backward.3), calls=%async_computation.3 | async-start | bytes 4456448 | tf_op jit(solution)/shard_map/all_to_all | solution.py:473
  212.4 39.3 %copy-start.17 = (f32[192]{0:T(256)S(1)}, f32[192]{0:T(256)}, u32[]{:S(2)}) copy-start(f32[192]{0:T(256)} %param.17) | copy-start | bytes 2308
  212.4 30.9 %collective-permute-start.19 = (f32[128]{0:T(128)S(1)}, f32[128]{0:T(128)S(1)}, u32[]{:S(2)}, u32[]{:S(2)}) collective-permute-start(f32[128]{0:T(128)S(1)} %get-tuple-element.81), channel_id=1, source_target_pairs={{0,16},{16,0},{32,48},{48,32},{64,80},{80,64},{96,112},{112,96},{1... | collective-permute-start | bytes 1544 | tf_op jit(solution)/shard_map/ppermute | solution.py:384
  216.6 26.7 %collective-permute-start.20 = (f32[128]{0:T(128)S(1)}, f32[128]{0:T(128)S(1)}, u32[]{:S(2)}, u32[]{:S(2)}) collective-permute-start(f32[128]{0:T(128)S(1)} %get-tuple-element.81), channel_id=1, source_target_pairs={{0,32},{16,48},{32,0},{48,16},{64,96},{80,112},{96,64},{112,80},{1... | collective-permute-start | bytes 1544 | tf_op jit(solution)/shard_map/ppermute | solution.py:384
  218.1 25.2 %collective-permute-start.21 = (f32[128]{0:T(128)S(1)}, f32[128]{0:T(128)S(1)}, u32[]{:S(2)}, u32[]{:S(2)}) collective-permute-start(f32[128]{0:T(128)S(1)} %get-tuple-element.81), channel_id=1, source_target_pairs={{0,48},{16,32},{32,16},{48,0},{64,112},{80,96},{96,80},{112,64},{1... | collective-permute-start | bytes 1544 | tf_op jit(solution)/shard_map/ppermute | solution.py:384
  243.3 5.1 %collective-permute-start.22 = (f32[128]{0:T(128)S(1)}, f32[128]{0:T(128)S(1)}, u32[]{:S(2)}, u32[]{:S(2)}) collective-permute-start(f32[128]{0:T(128)S(1)} %add_add_fusion), channel_id=1, source_target_pairs={{0,64},{16,80},{32,96},{48,112},{64,0},{80,16},{96,32},{112,48},{1... | collective-permute-start | bytes 1544 | tf_op jit(solution)/shard_map/ppermute | solution.py:384
  (14 other events, 33.0 us)

commit v7 on v6

--- a/solution.py
+++ b/solution.py
@@ -221,15 +221,7 @@
         place_ref, sources = refs[0], refs[1 : 1 + count]
         w_ref, o_ref, inv_ref = refs[1 + count : 4 + count]
         before = refs[4 + count : 4 + count + len(earlier)]
-        g_ref, d_ref, a_ref, held, sems = refs[4 + count + len(earlier) :]
-        copies = [
-            pltpu.make_async_copy(
-                sources[i], held.at[pl.ds(starts[i], sizes[i]), :], sems.at[i]
-            )
-            for i in range(count)
-        ]
-        for copy in copies:
-            copy.start()
+        g_ref, d_ref, a_ref = refs[4 + count + len(earlier) :]
         outer = jnp.zeros((HEAD_DIM, width), F32)
         if before:
             g_ref[...] = before[0][...]
@@ -241,10 +233,8 @@
             ]
             out = jnp.concatenate([o_ref[:, lane] for lane in lanes], axis=1)
             inv = jnp.concatenate([inv_ref[0:1, lane] for lane in lanes], axis=1)
-            for i in group:
-                copies[i].wait()
-            first, last = group[0], group[-1]
-            rows = held[starts[first] : starts[last] + sizes[last], :]
+            first = group[0]
+            rows = jnp.concatenate([sources[i][...] for i in group], axis=0)
             grad = contract(w_ref[...], rows, 1, 1).astype(BF16).astype(F32)
             low = (grad * inv).astype(BF16)
             delta = jnp.sum(low.astype(F32) * out.astype(F32), axis=0, keepdims=True)
@@ -259,19 +249,15 @@
     return pl.pallas_call(
         body,
         in_specs=[pl.BlockSpec(memory_space=pltpu.SMEM)]
-        + [pl.BlockSpec(memory_space=pl.ANY)] * count
-        + [vmem] * (3 + len(earlier)),
-        out_specs=[vmem] * 3,
+        + [pl.BlockSpec(memory_space=pltpu.VMEM)] * count
+        + [pl.BlockSpec()] * (3 + len(earlier)),
+        out_specs=[pl.BlockSpec()] * 3,
         out_shape=[
             jax.ShapeDtypeStruct((HEAD_DIM, total), BF16),
             jax.ShapeDtypeStruct((8, total), F32),
             jax.ShapeDtypeStruct((HEAD_DIM, width), F32),
         ],
-        scratch_shapes=[
-            pltpu.VMEM((sum(sizes), width), BF16),
-            pltpu.SemaphoreType.DMA((count,)),
-        ],
-        compiler_params=pltpu.CompilerParams(vmem_limit_bytes=28 * 2**20),
+        compiler_params=pltpu.CompilerParams(vmem_limit_bytes=24 * 2**20),
         cost_estimate=pl.CostEstimate(
             flops=4 * sum(sizes) * width * HEAD_DIM,
             bytes_accessed=2 * sum(sizes) * width,
@@ -385,9 +371,22 @@
 
 
 def total_over(values, axis):
-    one, two, three = (swap(values, axis, 8, bit) for bit in (1, 2, 3))
-    values = (values + one) + (two + three)
-    return values + swap(values, axis, 8, 4)
+    got = [values] + [swap(values, axis, 8, bit) for bit in range(1, 8)]
+    while len(got) > 1:
+        got = [got[i] + got[i + 1] for i in range(0, len(got), 2)]
+    return got[0]
+
+
+def after(token, arrays):
+    anywhere = pl.BlockSpec(memory_space=pl.ANY)
+    return pl.pallas_call(
+        lambda *refs: None,
+        in_specs=[anywhere] * (1 + len(arrays)),
+        out_specs=[anywhere] * len(arrays),
+        out_shape=[jax.ShapeDtypeStruct(x.shape, x.dtype) for x in arrays],
+        input_output_aliases={i + 1: i for i in range(len(arrays))},
+        name="after",
+    )(token, *arrays)
 
 
 def move(values, z_step=0, y_step=0, core_step=0):
@@ -421,11 +420,10 @@
 
     weight = w_out.astype(F32)
     gated = (weight * gate).astype(BF16)
-    results = forward(lengths, packed)
-    results, far_low, far_high, side_below, side_above = lax.optimization_barrier(
-        (results, far_low, far_high, side_below, side_above)
+    low, attended, query, inverse, key, value = forward(lengths, packed)
+    side, below, above, far_low, far_high, side_below, side_above = after(
+        inverse, [side, below, above, far_low, far_high, side_below, side_above]
     )
-    low, attended, query, inverse, key, value = results
     side_low, side_high = move(side_below[:half], z_step=1), move(side_above[half:], z_step=3)
     found = [
         (own, 0, 0, 0),

time: 253 us -> 232 us (0.917)
  waiting for transfers between devices: 104 us -> 78.1 us
  starting transfers between devices: 47.3 us -> 54.4 us
  local copies, waits for them, and re-layouts: 17.8 us -> 13.6 us
    ppermute x19, waiting for transfers between devices: 76.6 us -> 21.4 us  [move(): return lax.ppermute(values, 'seq', pairs)]
    all_to_all x1, waiting for transfers between devices: 0.01 us -> 30.9 us  [shards(): packed = lax.all_to_all(packed, 'seq', 0, 0, tiled=True)]
    ppermute x4 -> x7, starting transfers between devices: 8.85 us -> 14.4 us  [swap(): return lax.ppermute(values, axis, [(i, i ^ bit) for i in range(size)])]
    unnamed x40 -> x54, local copies, waits for them, and re-layouts: 11.3 us -> 8.88 us
    ppermute x4 -> x7, waiting for transfers between devices: 27.2 us -> 25.8 us  [swap(): return lax.ppermute(values, axis, [(i, i ^ bit) for i in range(size)])]
  transfers between devices with their start and end apart: 27 -> 30, of which waited for: 7 -> 8; matrix products, arithmetic and copies ran while one was open for 3% -> 2% of each run, Pallas kernels for 28% -> 32%
where the time goes in v7:
time: 232 us; the launch traced here: 231 us
  Pallas kernels  80.7 us (35%)
  waiting for transfers between devices  78.1 us (34%)
  starting transfers between devices  54.4 us (23%)
  local copies, waits for them, and re-layouts  13.6 us (6%)
  other arithmetic  2.47 us (1%)
    pallas_call x2, Pallas kernels, backward(): pl.pallas_call(body, grid=(steps,), in_specs=[pl.BlockSpec((some, BLOCK),...  41.7 us
    all_to_all x1, waiting for transfers between devices, shards(): packed = lax.all_to_all(packed, 'seq', 0, 0, tiled=True)  30.9 us
    ppermute x7, waiting for transfers between devices, swap(): return lax.ppermute(values, axis, [(i, i ^ bit) for i in range(size)])  25.8 us
    pallas_call x1, Pallas kernels, forward(): pl.pallas_call(body, grid_spec=pltpu.PrefetchScalarGridSpec(num_scalar_pr...  22.4 us
    ppermute x19, waiting for transfers between devices, move(): return lax.ppermute(values, 'seq', pairs)  21.4 us
    ppermute x19, starting transfers between devices, move(): return lax.ppermute(values, 'seq', pairs)  17.9 us
    ppermute x7, starting transfers between devices, swap(): return lax.ppermute(values, axis, [(i, i ^ bit) for i in range(size)])  14.4 us
    pallas_call x2, Pallas kernels, project(): pl.pallas_call(body, in_specs=[pl.BlockSpec(memory_space=pltpu.SMEM)] + [...  9.99 us
  transfers between devices with their start and end apart: 30, of which 8 were waited for; matrix products, arithmetic and copies ran while one was open for 2% of the time, Pallas kernels for 32%

profile of v7, /device:TPU:0, one launch (start us, length us, event | category | flops | bytes accessed | tf_op | source)
XLA Modules:
  0.0 231.0 jit_solution(4587104956608646705)
XLA Ops:
  0.6 1.7 collective-permute-start
  2.4 1.9 collective-permute-start.1
  4.3 2.1 collective-permute-start.2
  6.4 4.5 %split_columns.1 = bf16[16,3,256,128]{3,2,1,0:T(8,128)(2,1)} custom-call(bf16[256,2048]{1,0:T(8,128)(2,1)} %bitcast.39, bf16[256,2048]{1,0:T(8,128)(2,1)} %bitcast.40, bf16[256,2048]{1,0:T(8,128)(2,1)} %bitcast.41), custom_call_target="tpu_custom_call" | custom-call | tf_op jit(solution)/shard_map/split_columns/pallas_call | solution.py:36
  10.9 9.4 %collective-permute-done.refs_1_ = bf16[256,1536]{1,0:T(8,128)(2,1)} collective-permute-done((bf16[256,1536]{1,0:T(8,128)(2,1)}, bf16[256,1536]{1,0:T(8,128)(2,1)}, u32[]{:S(2)}, u32[]{:S(2)}) %collective-permute-start) | collective-permute-done | bytes 786464 | tf_op jit(solution)/shard_map/ppermute | solution.py:397
  20.2 3.7 %collective-permute-done.1.refs_2_ = bf16[256,1536]{1,0:T(8,128)(2,1)S(1)} collective-permute-done((bf16[256,1536]{1,0:T(8,128)(2,1)}, bf16[256,1536]{1,0:T(8,128)(2,1)S(1)}, u32[]{:S(2)}, u32[]{:S(2)}) %collective-permute-start.1) | collective-permute-done | bytes 786464 | tf_op jit(solution)/shard_map/ppermute | solution.py:397
  23.9 4.5 %all-to-all-start = ((bf16[16,3,256,128]{3,2,1,0:T(8,128)(2,1)}), bf16[16,3,256,128]{3,2,1,0:T(8,128)(2,1)}, u32[]{:S(2)}, u32[]{:S(2)}) async-start(bf16[16,3,256,128]{3,2,1,0:T(8,128)(2,1)} %split_columns.1), calls=%async_computation | async-start | bytes 6291456 | tf_op jit(solution)/shard_map/all_to_all | solution.py:417
  29.3 1.8 collective-permute-start.5
  31.1 1.5 collective-permute-start.6
  33.9 2.8 %collective-permute-start.4 = (bf16[128,1536]{1,0:T(8,128)(2,1)S(1)}, bf16[128,1536]{1,0:T(8,128)(2,1)}, u32[]{:S(2)}, u32[]{:S(2)}) collective-permute-start(bf16[128,1536]{1,0:T(8,128)(2,1)S(1)} %slice.20), channel_id=1, source_target_pairs={{0,12},{1,13},{2,14},{3,15},{4,0},{5,1},{6,2},{7,3},{8,4},{9,5},{1... | collective-permute-start | bytes 1179656 | tf_op jit(solution)/shard_map/ppermute | solution.py:397
  36.7 30.9 %all-to-all-done.p_ref = bf16[16,3,256,128]{3,2,1,0:T(8,128)(2,1)} async-done(((bf16[16,3,256,128]{3,2,1,0:T(8,128)(2,1)}), bf16[16,3,256,128]{3,2,1,0:T(8,128)(2,1)}, u32[]{:S(2)}, u32[]{:S(2)}) %all-to-all-start) | async-done | bytes 3145760 | tf_op jit(solution)/shard_map/all_to_all | solution.py:417
  67.6 22.4 %forward.1 = (bf16[4096,4096]{1,0:T(8,128)(2,1)}, bf16[128,4096]{1,0:T(8,128)(2,1)S(1)}, bf16[128,4096]{1,0:T(8,128)(2,1)S(1)}, f32[8,4096]{1,0:T(8,128)S(1)}, b...) custom-call(s32[1]{0:T(128)S(6)} %copy.34.len_ref, bf16[16,3,256,128]{3,2,1,0:T(8,128)(2,1)} %all-to-all-done.p_ref), custom_call_target="tpu_custom_call" | custom-call | flops 12884901888 | bytes 33554432 | tf_op jit(solution)/shard_map/forward/pallas_call | solution.py:165
  90.0 1.4 copy-done.8
  98.4 3.0 %collective-permute-start.8 = (bf16[128,1536]{1,0:T(8,128)(2,1)S(1)}, bf16[128,1536]{1,0:T(8,128)(2,1)}, u32[]{:S(2)}, u32[]{:S(2)}) collective-permute-start(bf16[128,1536]{1,0:T(8,128)(2,1)S(1)} %slice.22), channel_id=1, source_target_pairs={{0,12},{1,13},{2,14},{3,15},{4,0},{5,1},{6,2},{7,3},{8,4},{9,5},{1... | collective-permute-start | bytes 1179656 | tf_op jit(solution)/shard_map/ppermute | solution.py:397
  101.4 7.0 %collective-permute-done.7.refs_5_ = bf16[128,1536]{1,0:T(8,128)(2,1)S(1)} collective-permute-done((bf16[128,1536]{1,0:T(8,128)(2,1)S(1)}, bf16[128,1536]{1,0:T(8,128)(2,1)S(1)}, u32[]{:S(2)}, u32[]{:S(2)}) %collective-permute-start.7) | collective-permute-done | bytes 393248 | tf_op jit(solution)/shard_map/ppermute | solution.py:397
  109.1 1.4 collective-permute-done.8.refs_6_
  113.9 5.5 %project.2 = (bf16[128,4096]{1,0:T(8,128)(2,1)S(1)}, f32[8,4096]{1,0:T(8,128)S(1)}, f32[128,1536]{1,0:T(8,128)S(1)}) custom-call(s32[8]{0:T(128)S(1)} %stack.87.refs_0_, bf16[256,1536]{1,0:T(8,128)(2,1)} %bitcast.3.refs_1_, bf16[256,1536]{1,0:T(8,128)(2,1)} %get-tuple-element.52.refs_2_, bf16[256,1536]{1,0:T(8,128)(2,1)S(1)} %copy-done.5, ...), custom_call_target="tpu_custom_call" | custom-call | flops 1610612736 | bytes 6291456 | tf_op jit(solution)/shard_map/project/pallas_call | solution.py:249
  119.5 4.5 %project.3 = (bf16[128,4096]{1,0:T(8,128)(2,1)S(1)}, f32[8,4096]{1,0:T(8,128)S(1)}, f32[128,1536]{1,0:T(8,128)S(1)}) custom-call(s32[12]{0:T(128)S(1)} %stack.78.refs_0_, bf16[128,1536]{1,0:T(8,128)(2,1)S(1)} %copy-done.10, bf16[128,1536]{1,0:T(8,128)(2,1)} %get-tuple-element.48.refs_2_, bf16[256,1536]{1,0:T(8,128)(2,1)S(1)} %copy-done.1, ...), custom_call_target="tpu_custom_call" | custom-call | flops 1610612736 | bytes 6291456 | tf_op jit(solution)/shard_map/project/pallas_call | solution.py:249
  126.6 6.7 %all-to-all-start.1 = ((bf16[8,128,192]{1,2,0:T(8,128)(2,1)}), bf16[8,128,192]{1,2,0:T(8,128)(2,1)S(1)}, u32[]{:S(2)}, u32[]{:S(2)}) async-start(bf16[8,128,192]{1,2,0:T(8,128)(2,1)} %bitcast.25), calls=%async_computation.1 | async-start | bytes 786432 | tf_op jit(solution)/shard_map/all_to_all | solution.py:456
  133.4 20.6 %backward.2 = (f32[128,4096]{1,0:T(8,128)}, bf16[16,2,128,128]{3,2,1,0:T(8,128)(2,1)}) custom-call(bf16[4096,4096]{1,0:T(8,128)(2,1)} %get-tuple-element.42.refs_0_, bf16[128,4096]{1,0:T(8,128)(2,1)} %copy-done.15, f32[8,4096]{1,0:T(8,128)} %copy-done.20, bf16[128,4096]{1,0:T(8,128)(2,1)} %copy-done.13, bf16[128,4096]{1,0:T(8,128)(2,1)} %copy-done.14, ...), custom_call_target="tpu_custom_call" | custom-call | flops 10737418240 | bytes 16777216 | tf_op jit(solution)/shard_map/backward/pallas_call | solution.py:344
  154.1 5.2 %all-to-all-start.2 = ((bf16[16,2,128,128]{3,2,1,0:T(8,128)(2,1)}), bf16[16,2,128,128]{3,2,1,0:T(8,128)(2,1)S(1)}, u32[]{:S(2)}, u32[]{:S(2)}) async-start(bf16[16,2,128,128]{3,2,1,0:T(8,128)(2,1)} %get-tuple-element.66), calls=%async_computation.2 | async-start | bytes 2097152 | tf_op jit(solution)/shard_map/all_to_all | solution.py:459
  160.0 21.1 %backward.3 = bf16[16,544,128]{2,1,0:T(8,128)(2,1)} custom-call(bf16[4096,4096]{1,0:T(8,128)(2,1)} %get-tuple-element.42.refs_0_, bf16[128,4096]{1,0:T(8,128)(2,1)} %copy-done.15, f32[8,4096]{1,0:T(8,128)} %copy-done.20, bf16[128,4096]{1,0:T(8,128)(2,1)} %copy-done.13, bf16[128,4096]{1,0:T(8,128)(2,1)} %copy-done.14, bf16[4096,256]{1,0:T(8,128)(2,1)} %copy-done.8, ...), custom_call_target="tpu_custom_call" | custom-call | flops 10737418240 | bytes 16777216 | tf_op jit(solution)/shard_map/backward/pallas_call | solution.py:344
  181.1 5.7 %all-to-all-start.3 = ((bf16[16,544,128]{2,1,0:T(8,128)(2,1)}), bf16[16,544,128]{2,1,0:T(8,128)(2,1)S(1)}, u32[]{:S(2)}, u32[]{:S(2)}) async-start(bf16[16,544,128]{2,1,0:T(8,128)(2,1)} %backward.3), calls=%async_computation.3 | async-start | bytes 4456448 | tf_op jit(solution)/shard_map/all_to_all | solution.py:471
  186.9 3.8 %collective-permute-start.19 = (f32[128]{0:T(128)S(1)}, f32[128]{0:T(128)S(1)}, u32[]{:S(2)}, u32[]{:S(2)}) collective-permute-start(f32[128]{0:T(128)S(1)} %get-tuple-element.75), channel_id=1, source_target_pairs={{0,16},{16,0},{32,48},{48,32},{64,80},{80,64},{96,112},{112,96},{1... | collective-permute-start | bytes 1544 | tf_op jit(solution)/shard_map/ppermute | solution.py:370
  190.7 1.5 collective-permute-start.20
  192.2 3.2 %collective-permute-start.22 = (f32[128]{0:T(128)S(1)}, f32[128]{0:T(128)S(1)}, u32[]{:S(2)}, u32[]{:S(2)}) collective-permute-start(f32[128]{0:T(128)S(1)} %get-tuple-element.75), channel_id=1, source_target_pairs={{0,64},{16,80},{32,96},{48,112},{64,0},{80,16},{96,32},{112,48},{1... | collective-permute-start | bytes 1544 | tf_op jit(solution)/shard_map/ppermute | solution.py:370
  195.4 3.2 %collective-permute-start.23 = (f32[128]{0:T(128)S(1)}, f32[128]{0:T(128)S(1)}, u32[]{:S(2)}, u32[]{:S(2)}) collective-permute-start(f32[128]{0:T(128)S(1)} %get-tuple-element.75), channel_id=1, source_target_pairs={{0,80},{16,64},{32,112},{48,96},{64,16},{80,0},{96,48},{112,32},{1... | collective-permute-start | bytes 1544 | tf_op jit(solution)/shard_map/ppermute | solution.py:370
  198.6 18.7 %collective-permute-done.19 = f32[128]{0:T(128)S(1)} collective-permute-done((f32[128]{0:T(128)S(1)}, f32[128]{0:T(128)S(1)}, u32[]{:S(2)}, u32[]{:S(2)}) %collective-permute-start.19) | collective-permute-done | bytes 544 | tf_op jit(solution)/shard_map/ppermute | solution.py:370
  217.3 2.7 %collective-permute-start.24 = (f32[128]{0:T(128)S(1)}, f32[128]{0:T(128)S(1)}, u32[]{:S(2)}, u32[]{:S(2)}) collective-permute-start(f32[128]{0:T(128)S(1)} %get-tuple-element.75), channel_id=1, source_target_pairs={{0,96},{16,112},{32,64},{48,80},{64,32},{80,48},{96,0},{112,16},{1... | collective-permute-start | bytes 1544 | tf_op jit(solution)/shard_map/ppermute | solution.py:370
  220.0 2.0 collective-permute-done.24
  222.1 5.1 %collective-permute-done.25 = f32[128]{0:T(128)S(1)} collective-permute-done((f32[128]{0:T(128)S(1)}, f32[128]{0:T(128)S(1)}, u32[]{:S(2)}, u32[]{:S(2)}) %collective-permute-start.25) | collective-permute-done | bytes 544 | tf_op jit(solution)/shard_map/ppermute | solution.py:370
  227.7 2.1 join_columns.1
  (106 shorter events, 17.9 us)
Async XLA Ops:
  0.6 19.6 %collective-permute-start = (bf16[256,1536]{1,0:T(8,128)(2,1)}, bf16[256,1536]{1,0:T(8,128)(2,1)}, u32[]{:S(2)}, u32[]{:S(2)}) collective-permute-start(bf16[256,1536]{1,0:T(8,128)(2,1)} %bitcast.3.refs_1_), channel_id=1, source_target_pairs={{0,2},{1,3},{2,0},{3,1},{4,6},{5,7},{6,4},{7,5},{8,10},{9,11},{10,... | collective-permute-start | bytes 2359304 | tf_op jit(solution)/shard_map/ppermute | solution.py:397
  2.4 21.5 %collective-permute-start.1 = (bf16[256,1536]{1,0:T(8,128)(2,1)}, bf16[256,1536]{1,0:T(8,128)(2,1)S(1)}, u32[]{:S(2)}, u32[]{:S(2)}) collective-permute-start(bf16[256,1536]{1,0:T(8,128)(2,1)} %bitcast.3.refs_1_), channel_id=1, source_target_pairs={{0,4},{1,5},{2,6},{3,7},{4,8},{5,9},{6,10},{7,11},{8,12},{9,13},{1... | collective-permute-start | bytes 2359304 | tf_op jit(solution)/shard_map/ppermute | solution.py:397
  4.3 19.6 %collective-permute-start.2 = (bf16[256,1536]{1,0:T(8,128)(2,1)}, bf16[256,1536]{1,0:T(8,128)(2,1)S(1)}, u32[]{:S(2)}, u32[]{:S(2)}) collective-permute-start(bf16[256,1536]{1,0:T(8,128)(2,1)} %bitcast.3.refs_1_), channel_id=1, source_target_pairs={{0,12},{1,13},{2,14},{3,15},{4,0},{5,1},{6,2},{7,3},{8,4},{9,5},{1... | collective-permute-start | bytes 2359304 | tf_op jit(solution)/shard_map/ppermute | solution.py:397
  23.9 43.7 %all-to-all-start = ((bf16[16,3,256,128]{3,2,1,0:T(8,128)(2,1)}), bf16[16,3,256,128]{3,2,1,0:T(8,128)(2,1)}, u32[]{:S(2)}, u32[]{:S(2)}) async-start(bf16[16,3,256,128]{3,2,1,0:T(8,128)(2,1)} %split_columns.1), calls=%async_computation | async-start | bytes 6291456 | tf_op jit(solution)/shard_map/all_to_all | solution.py:417
  28.4 70.0 %collective-permute-start.15 = (bf16[256,1536]{1,0:T(8,128)(2,1)}, bf16[256,1536]{1,0:T(8,128)(2,1)}, u32[]{:S(2)}, u32[]{:S(2)}) collective-permute-start(bf16[256,1536]{1,0:T(8,128)(2,1)} %bitcast.3.refs_1_), channel_id=1, source_target_pairs={{0,1},{1,0},{2,3},{3,2},{4,5},{5,4},{6,7},{7,6},{8,9},{9,8},{10,11... | collective-permute-start | bytes 2359304 | tf_op jit(solution)/shard_map/ppermute | solution.py:397
  29.3 64.7 %collective-permute-start.5 = (bf16[256,1536]{1,0:T(8,128)(2,1)}, bf16[256,1536]{1,0:T(8,128)(2,1)S(1)}, u32[]{:S(2)}, u32[]{:S(2)}) collective-permute-start(bf16[256,1536]{1,0:T(8,128)(2,1)} %collective-permute-done.refs_1_), channel_id=1, source_target_pairs={{0,4},{1,5},{2,6},{3,7},{4,8},{5,9},{6,10},{7,11},{8,12},{9,13},{1... | collective-permute-start | bytes 2359304 | tf_op jit(solution)/shard_map/ppermute | solution.py:397
  31.1 62.9 %collective-permute-start.6 = (bf16[256,1536]{1,0:T(8,128)(2,1)}, bf16[256,1536]{1,0:T(8,128)(2,1)S(1)}, u32[]{:S(2)}, u32[]{:S(2)}) collective-permute-start(bf16[256,1536]{1,0:T(8,128)(2,1)} %collective-permute-done.refs_1_), channel_id=1, source_target_pairs={{0,12},{1,13},{2,14},{3,15},{4,0},{5,1},{6,2},{7,3},{8,4},{9,5},{1... | collective-permute-start | bytes 2359304 | tf_op jit(solution)/shard_map/ppermute | solution.py:397
  33.4 60.6 %collective-permute-start.3 = (bf16[128,1536]{1,0:T(8,128)(2,1)}, bf16[128,1536]{1,0:T(8,128)(2,1)S(1)}, u32[]{:S(2)}, u32[]{:S(2)}) collective-permute-start(bf16[128,1536]{1,0:T(8,128)(2,1)} %slice.19), channel_id=1, source_target_pairs={{0,4},{1,5},{2,6},{3,7},{4,8},{5,9},{6,10},{7,11},{8,12},{9,13},{1... | collective-permute-start | bytes 1179656 | tf_op jit(solution)/shard_map/ppermute | solution.py:397
  33.9 60.1 %collective-permute-start.4 = (bf16[128,1536]{1,0:T(8,128)(2,1)S(1)}, bf16[128,1536]{1,0:T(8,128)(2,1)}, u32[]{:S(2)}, u32[]{:S(2)}) collective-permute-start(bf16[128,1536]{1,0:T(8,128)(2,1)S(1)} %slice.20), channel_id=1, source_target_pairs={{0,12},{1,13},{2,14},{3,15},{4,0},{5,1},{6,2},{7,3},{8,4},{9,5},{1... | collective-permute-start | bytes 1179656 | tf_op jit(solution)/shard_map/ppermute | solution.py:397
  96.5 11.9 %collective-permute-start.7 = (bf16[128,1536]{1,0:T(8,128)(2,1)S(1)}, bf16[128,1536]{1,0:T(8,128)(2,1)S(1)}, u32[]{:S(2)}, u32[]{:S(2)}) collective-permute-start(bf16[128,1536]{1,0:T(8,128)(2,1)S(1)} %slice.21), channel_id=1, source_target_pairs={{0,4},{1,5},{2,6},{3,7},{4,8},{5,9},{6,10},{7,11},{8,12},{9,13},{1... | collective-permute-start | bytes 1179656 | tf_op jit(solution)/shard_map/ppermute | solution.py:397
  96.9 15.0 %collective-permute-start.16 = (bf16[256,1536]{1,0:T(8,128)(2,1)}, bf16[256,1536]{1,0:T(8,128)(2,1)}, u32[]{:S(2)}, u32[]{:S(2)}) collective-permute-start(bf16[256,1536]{1,0:T(8,128)(2,1)} %get-tuple-element.52.refs_2_), channel_id=1, source_target_pairs={{0,1},{1,0},{2,3},{3,2},{4,5},{5,4},{6,7},{7,6},{8,9},{9,8},{10,11... | collective-permute-start | bytes 2359304 | tf_op jit(solution)/shard_map/ppermute | solution.py:397
  96.9 15.1 %collective-permute-start.17 = (bf16[256,1536]{1,0:T(8,128)(2,1)}, bf16[256,1536]{1,0:T(8,128)(2,1)}, u32[]{:S(2)}, u32[]{:S(2)}) collective-permute-start(bf16[256,1536]{1,0:T(8,128)(2,1)} %get-tuple-element.53.refs_3_), channel_id=1, source_target_pairs={{0,1},{1,0},{2,3},{3,2},{4,5},{5,4},{6,7},{7,6},{8,9},{9,8},{10,11... | collective-permute-start | bytes 2359304 | tf_op jit(solution)/shard_map/ppermute | solution.py:397
  97.4 15.1 %collective-permute-start.18 = (bf16[256,1536]{1,0:T(8,128)(2,1)}, bf16[256,1536]{1,0:T(8,128)(2,1)}, u32[]{:S(2)}, u32[]{:S(2)}) collective-permute-start(bf16[256,1536]{1,0:T(8,128)(2,1)} %get-tuple-element.54.refs_4_), channel_id=1, source_target_pairs={{0,1},{1,0},{2,3},{3,2},{4,5},{5,4},{6,7},{7,6},{8,9},{9,8},{10,11... | collective-permute-start | bytes 2359304 | tf_op jit(solution)/shard_map/ppermute | solution.py:397
  98.4 12.0 %collective-permute-start.8 = (bf16[128,1536]{1,0:T(8,128)(2,1)S(1)}, bf16[128,1536]{1,0:T(8,128)(2,1)}, u32[]{:S(2)}, u32[]{:S(2)}) collective-permute-start(bf16[128,1536]{1,0:T(8,128)(2,1)S(1)} %slice.22), channel_id=1, source_target_pairs={{0,12},{1,13},{2,14},{3,15},{4,0},{5,1},{6,2},{7,3},{8,4},{9,5},{1... | collective-permute-start | bytes 1179656 | tf_op jit(solution)/shard_map/ppermute | solution.py:397
  108.3 2.1 collective-permute-start.10
  110.4 9.0 %collective-permute-start.11 = (bf16[256,1536]{1,0:T(8,128)(2,1)}, bf16[256,1536]{1,0:T(8,128)(2,1)S(1)}, u32[]{:S(2)}, u32[]{:S(2)}) collective-permute-start(bf16[256,1536]{1,0:T(8,128)(2,1)} %get-tuple-element.49.refs_3_), channel_id=1, source_target_pairs={{0,1},{1,0},{2,3},{3,2},{4,5},{5,4},{6,7},{7,6},{8,9},{9,8},{10,11... | collective-permute-start | bytes 2359304 | tf_op jit(solution)/shard_map/ppermute | solution.py:397
  111.2 8.3 %collective-permute-start.12 = (bf16[256,1536]{1,0:T(8,128)(2,1)}, bf16[256,1536]{1,0:T(8,128)(2,1)}, u32[]{:S(2)}, u32[]{:S(2)}) collective-permute-start(bf16[256,1536]{1,0:T(8,128)(2,1)} %get-tuple-element.50.refs_4_), channel_id=1, source_target_pairs={{0,1},{1,0},{2,3},{3,2},{4,5},{5,4},{6,7},{7,6},{8,9},{9,8},{10,11... | collective-permute-start | bytes 2359304 | tf_op jit(solution)/shard_map/ppermute | solution.py:397
  111.9 7.5 %collective-permute-start.9 = (bf16[128,1536]{1,0:T(8,128)(2,1)}, bf16[128,1536]{1,0:T(8,128)(2,1)S(1)}, u32[]{:S(2)}, u32[]{:S(2)}) collective-permute-start(bf16[128,1536]{1,0:T(8,128)(2,1)} %get-tuple-element.47.refs_1_), channel_id=1, source_target_pairs={{0,1},{1,0},{2,3},{3,2},{4,5},{5,4},{6,7},{7,6},{8,9},{9,8},{10,11... | collective-permute-start | bytes 1179656 | tf_op jit(solution)/shard_map/ppermute | solution.py:397
  112.0 7.4 %collective-permute-start.13 = (bf16[128,1536]{1,0:T(8,128)(2,1)}, bf16[128,1536]{1,0:T(8,128)(2,1)S(1)}, u32[]{:S(2)}, u32[]{:S(2)}) collective-permute-start(bf16[128,1536]{1,0:T(8,128)(2,1)} %copy-done.16), channel_id=1, source_target_pairs={{0,1},{1,0},{2,3},{3,2},{4,5},{5,4},{6,7},{7,6},{8,9},{9,8},{10,11... | collective-permute-start | bytes 1179656 | tf_op jit(solution)/shard_map/ppermute | solution.py:397
  112.5 7.0 %collective-permute-start.14 = (bf16[128,1536]{1,0:T(8,128)(2,1)}, bf16[128,1536]{1,0:T(8,128)(2,1)S(1)}, u32[]{:S(2)}, u32[]{:S(2)}) collective-permute-start(bf16[128,1536]{1,0:T(8,128)(2,1)} %collective-permute-done.8.refs_6_), channel_id=1, source_target_pairs={{0,1},{1,0},{2,3},{3,2},{4,5},{5,4},{6,7},{7,6},{8,9},{9,8},{10,11... | collective-permute-start | bytes 1179656 | tf_op jit(solution)/shard_map/ppermute | solution.py:397
  126.6 27.3 %all-to-all-start.1 = ((bf16[8,128,192]{1,2,0:T(8,128)(2,1)}), bf16[8,128,192]{1,2,0:T(8,128)(2,1)S(1)}, u32[]{:S(2)}, u32[]{:S(2)}) async-start(bf16[8,128,192]{1,2,0:T(8,128)(2,1)} %bitcast.25), calls=%async_computation.1 | async-start | bytes 786432 | tf_op jit(solution)/shard_map/all_to_all | solution.py:456
  154.1 27.0 %all-to-all-start.2 = ((bf16[16,2,128,128]{3,2,1,0:T(8,128)(2,1)}), bf16[16,2,128,128]{3,2,1,0:T(8,128)(2,1)S(1)}, u32[]{:S(2)}, u32[]{:S(2)}) async-start(bf16[16,2,128,128]{3,2,1,0:T(8,128)(2,1)} %get-tuple-element.66), calls=%async_computation.2 | async-start | bytes 2097152 | tf_op jit(solution)/shard_map/all_to_all | solution.py:459
  181.1 46.0 %copy-start.25 = (f32[128]{0:T(128)S(1)}, f32[128]{0:T(128)}, u32[]{:S(2)}) copy-start(f32[128]{0:T(128)} %param.16) | copy-start | bytes 1540
  181.1 46.5 %all-to-all-start.3 = ((bf16[16,544,128]{2,1,0:T(8,128)(2,1)}), bf16[16,544,128]{2,1,0:T(8,128)(2,1)S(1)}, u32[]{:S(2)}, u32[]{:S(2)}) async-start(bf16[16,544,128]{2,1,0:T(8,128)(2,1)} %backward.3), calls=%async_computation.3 | async-start | bytes 4456448 | tf_op jit(solution)/shard_map/all_to_all | solution.py:471
  186.9 43.5 %copy-start.24 = (f32[192]{0:T(256)S(1)}, f32[192]{0:T(256)}, u32[]{:S(2)}) copy-start(f32[192]{0:T(256)} %param.17) | copy-start | bytes 2308
  186.9 30.4 %collective-permute-start.19 = (f32[128]{0:T(128)S(1)}, f32[128]{0:T(128)S(1)}, u32[]{:S(2)}, u32[]{:S(2)}) collective-permute-start(f32[128]{0:T(128)S(1)} %get-tuple-element.75), channel_id=1, source_target_pairs={{0,16},{16,0},{32,48},{48,32},{64,80},{80,64},{96,112},{112,96},{1... | collective-permute-start | bytes 1544 | tf_op jit(solution)/shard_map/ppermute | solution.py:370
  190.7 29.3 %collective-permute-start.20 = (f32[128]{0:T(128)S(1)}, f32[128]{0:T(128)S(1)}, u32[]{:S(2)}, u32[]{:S(2)}) collective-permute-start(f32[128]{0:T(128)S(1)} %get-tuple-element.75), channel_id=1, source_target_pairs={{0,32},{16,48},{32,0},{48,16},{64,96},{80,112},{96,64},{112,80},{1... | collective-permute-start | bytes 1544 | tf_op jit(solution)/shard_map/ppermute | solution.py:370
  192.1 27.9 %collective-permute-start.21 = (f32[128]{0:T(128)S(1)}, f32[128]{0:T(128)S(1)}, u32[]{:S(2)}, u32[]{:S(2)}) collective-permute-start(f32[128]{0:T(128)S(1)} %get-tuple-element.75), channel_id=1, source_target_pairs={{0,48},{16,32},{32,16},{48,0},{64,112},{80,96},{96,80},{112,64},{1... | collective-permute-start | bytes 1544 | tf_op jit(solution)/shard_map/ppermute | solution.py:370
  192.2 27.8 %collective-permute-start.22 = (f32[128]{0:T(128)S(1)}, f32[128]{0:T(128)S(1)}, u32[]{:S(2)}, u32[]{:S(2)}) collective-permute-start(f32[128]{0:T(128)S(1)} %get-tuple-element.75), channel_id=1, source_target_pairs={{0,64},{16,80},{32,96},{48,112},{64,0},{80,16},{96,32},{112,48},{1... | collective-permute-start | bytes 1544 | tf_op jit(solution)/shard_map/ppermute | solution.py:370
  195.4 24.6 %collective-permute-start.23 = (f32[128]{0:T(128)S(1)}, f32[128]{0:T(128)S(1)}, u32[]{:S(2)}, u32[]{:S(2)}) collective-permute-start(f32[128]{0:T(128)S(1)} %get-tuple-element.75), channel_id=1, source_target_pairs={{0,80},{16,64},{32,112},{48,96},{64,16},{80,0},{96,48},{112,32},{1... | collective-permute-start | bytes 1544 | tf_op jit(solution)/shard_map/ppermute | solution.py:370
  217.3 4.8 %collective-permute-start.24 = (f32[128]{0:T(128)S(1)}, f32[128]{0:T(128)S(1)}, u32[]{:S(2)}, u32[]{:S(2)}) collective-permute-start(f32[128]{0:T(128)S(1)} %get-tuple-element.75), channel_id=1, source_target_pairs={{0,96},{16,112},{32,64},{48,80},{64,32},{80,48},{96,0},{112,16},{1... | collective-permute-start | bytes 1544 | tf_op jit(solution)/shard_map/ppermute | solution.py:370
  220.0 7.2 %collective-permute-start.25 = (f32[128]{0:T(128)S(1)}, f32[128]{0:T(128)S(1)}, u32[]{:S(2)}, u32[]{:S(2)}) collective-permute-start(f32[128]{0:T(128)S(1)} %get-tuple-element.75), channel_id=1, source_target_pairs={{0,112},{16,96},{32,80},{48,64},{64,48},{80,32},{96,16},{112,0},{1... | collective-permute-start | bytes 1544 | tf_op jit(solution)/shard_map/ppermute | solution.py:370
  (24 other events, 161.5 us)

commit v8 on v7

--- a/solution.py
+++ b/solution.py
@@ -186,12 +186,12 @@
             ],
         ),
         out_shape=[
-            jax.ShapeDtypeStruct((total, total), BF16),
-            jax.ShapeDtypeStruct((HEAD_DIM, total), BF16),
-            jax.ShapeDtypeStruct((HEAD_DIM, total), BF16),
-            jax.ShapeDtypeStruct((8, total), F32),
-            jax.ShapeDtypeStruct((HEAD_DIM, total), BF16),
-            jax.ShapeDtypeStruct((total, 2 * HEAD_DIM), BF16),
+            pltpu.HBM((total, total), BF16),
+            pltpu.HBM((HEAD_DIM, total), BF16),
+            pltpu.HBM((HEAD_DIM, total), BF16),
+            pltpu.HBM((8, total), F32),
+            pltpu.HBM((HEAD_DIM, total), BF16),
+            pltpu.HBM((total, 2 * HEAD_DIM), BF16),
         ],
         compiler_params=pltpu.CompilerParams(vmem_limit_bytes=40 * 2**20),
         cost_estimate=pl.CostEstimate(
@@ -253,9 +253,9 @@
         + [pl.BlockSpec()] * (3 + len(earlier)),
         out_specs=[pl.BlockSpec()] * 3,
         out_shape=[
-            jax.ShapeDtypeStruct((HEAD_DIM, total), BF16),
-            jax.ShapeDtypeStruct((8, total), F32),
-            jax.ShapeDtypeStruct((HEAD_DIM, width), F32),
+            pltpu.HBM((HEAD_DIM, total), BF16),
+            pltpu.HBM((8, total), F32),
+            pltpu.HBM((HEAD_DIM, width), F32),
         ],
         compiler_params=pltpu.CompilerParams(vmem_limit_bytes=24 * 2**20),
         cost_estimate=pl.CostEstimate(
@@ -371,10 +371,9 @@
 
 
 def total_over(values, axis):
-    got = [values] + [swap(values, axis, 8, bit) for bit in range(1, 8)]
-    while len(got) > 1:
-        got = [got[i] + got[i + 1] for i in range(0, len(got), 2)]
-    return got[0]
+    one, two, three = (swap(values, axis, 8, bit) for bit in (1, 2, 3))
+    values = (values + one) + (two + three)
+    return values + swap(values, axis, 8, 4)
 
 
 def after(token, arrays):
@@ -441,6 +440,9 @@
     z, y, core = me // 4, me // 2 % 2, me % 2
     made = []
     for some in (found[:4], found[4:]):
+        if made:
+            late = after(made[1], [side_low, side_high])
+            some = some[:4] + [(late[0],) + some[4][1:], (late[1],) + some[5][1:]]
         pieces, places = [], []
         for core_step in range(2):
             for rows, z_step, y_step, offset in some:

time: 232 us -> 228 us (0.983)
  starting transfers between devices: 54.4 us -> 47.1 us
  local copies, waits for them, and re-layouts: 13.6 us -> 17.4 us
  waiting for transfers between devices: 78.1 us -> 74.6 us
  Pallas kernels: 80.7 us -> 83.3 us
    ppermute x7 -> x4, starting transfers between devices: 14.4 us -> 8.33 us  [swap(): return lax.ppermute(values, axis, [(i, i ^ bit) for i in range(size)])]
    ppermute x19, waiting for transfers between devices: 21.4 us -> 15.9 us  [move(): return lax.ppermute(values, 'seq', pairs)]
    unnamed x54, local copies, waits for them, and re-layouts: 8.88 us -> 13.6 us
    ppermute x7 -> x4, waiting for transfers between devices: 25.8 us -> 27.2 us  [swap(): return lax.ppermute(values, axis, [(i, i ^ bit) for i in range(size)])]
  transfers between devices with their start and end apart: 30 -> 27, of which waited for: 8 -> 9; matrix products, arithmetic and copies ran while one was open for 2% -> 2% of each run, Pallas kernels for 32% -> 33%
where the time goes in v8:
time: 228 us; the launch traced here: 227 us
  Pallas kernels  83.3 us (37%)
  waiting for transfers between devices  74.6 us (33%)
  starting transfers between devices  47.1 us (21%)
  local copies, waits for them, and re-layouts  17.4 us (8%)
  other arithmetic  3.31 us (1%)
    pallas_call x2, Pallas kernels, backward(): pl.pallas_call(body, grid=(steps,), in_specs=[pl.BlockSpec((some, BLOCK),...  41.7 us
    all_to_all x1, waiting for transfers between devices, shards(): packed = lax.all_to_all(packed, 'seq', 0, 0, tiled=True)  31.6 us
    ppermute x4, waiting for transfers between devices, swap(): return lax.ppermute(values, axis, [(i, i ^ bit) for i in range(size)])  27.2 us
    pallas_call x1, Pallas kernels, forward(): pl.pallas_call(body, grid_spec=pltpu.PrefetchScalarGridSpec(num_scalar_pr...  23.3 us
    ppermute x19, starting transfers between devices, move(): return lax.ppermute(values, 'seq', pairs)  18.2 us
    ppermute x19, waiting for transfers between devices, move(): return lax.ppermute(values, 'seq', pairs)  15.9 us
    unnamed x54, local copies, waits for them, and re-layouts  13.6 us
    pallas_call x2, Pallas kernels, project(): pl.pallas_call(body, in_specs=[pl.BlockSpec(memory_space=pltpu.SMEM)] + [...  11.8 us
  transfers between devices with their start and end apart: 27, of which 9 were waited for; matrix products, arithmetic and copies ran while one was open for 2% of the time, Pallas kernels for 33%

profile of v8, /device:TPU:0, one launch (start us, length us, event | category | flops | bytes accessed | tf_op | source)
XLA Modules:
  0.0 227.3 jit_solution(9529823122511877620)
XLA Ops:
  0.6 1.7 collective-permute-start
  2.4 1.9 collective-permute-start.1
  4.3 2.1 collective-permute-start.2
  6.4 4.4 %split_columns.1 = bf16[16,3,256,128]{3,2,1,0:T(8,128)(2,1)} custom-call(bf16[256,2048]{1,0:T(8,128)(2,1)} %bitcast.39, bf16[256,2048]{1,0:T(8,128)(2,1)} %bitcast.40, bf16[256,2048]{1,0:T(8,128)(2,1)} %bitcast.41), custom_call_target="tpu_custom_call" | custom-call | tf_op jit(solution)/shard_map/split_columns/pallas_call | solution.py:36
  10.8 9.4 %collective-permute-done.refs_1_ = bf16[256,1536]{1,0:T(8,128)(2,1)} collective-permute-done((bf16[256,1536]{1,0:T(8,128)(2,1)}, bf16[256,1536]{1,0:T(8,128)(2,1)}, u32[]{:S(2)}, u32[]{:S(2)}) %collective-permute-start) | collective-permute-done | bytes 786464 | tf_op jit(solution)/shard_map/ppermute | solution.py:396
  20.2 3.7 %collective-permute-done.1.refs_2_ = bf16[256,1536]{1,0:T(8,128)(2,1)S(1)} collective-permute-done((bf16[256,1536]{1,0:T(8,128)(2,1)}, bf16[256,1536]{1,0:T(8,128)(2,1)S(1)}, u32[]{:S(2)}, u32[]{:S(2)}) %collective-permute-start.1) | collective-permute-done | bytes 786464 | tf_op jit(solution)/shard_map/ppermute | solution.py:396
  23.9 4.5 %all-to-all-start = ((bf16[16,3,256,128]{3,2,1,0:T(8,128)(2,1)}), bf16[16,3,256,128]{3,2,1,0:T(8,128)(2,1)}, u32[]{:S(2)}, u32[]{:S(2)}) async-start(bf16[16,3,256,128]{3,2,1,0:T(8,128)(2,1)} %split_columns.1), calls=%async_computation | async-start | bytes 6291456 | tf_op jit(solution)/shard_map/all_to_all | solution.py:416
  29.3 1.8 collective-permute-start.5
  31.1 1.5 collective-permute-start.6
  33.2 2.8 %collective-permute-start.4 = (bf16[128,1536]{1,0:T(8,128)(2,1)S(1)}, bf16[128,1536]{1,0:T(8,128)(2,1)}, u32[]{:S(2)}, u32[]{:S(2)}) collective-permute-start(bf16[128,1536]{1,0:T(8,128)(2,1)S(1)} %slice.20), channel_id=1, source_target_pairs={{0,12},{1,13},{2,14},{3,15},{4,0},{5,1},{6,2},{7,3},{8,4},{9,5},{1... | collective-permute-start | bytes 1179656 | tf_op jit(solution)/shard_map/ppermute | solution.py:396
  36.0 31.6 %all-to-all-done.p_ref = bf16[16,3,256,128]{3,2,1,0:T(8,128)(2,1)} async-done(((bf16[16,3,256,128]{3,2,1,0:T(8,128)(2,1)}), bf16[16,3,256,128]{3,2,1,0:T(8,128)(2,1)}, u32[]{:S(2)}, u32[]{:S(2)}) %all-to-all-start) | async-done | bytes 3145760 | tf_op jit(solution)/shard_map/all_to_all | solution.py:416
  67.6 23.3 %forward.1 = (bf16[4096,4096]{1,0:T(8,128)(2,1)}, bf16[128,4096]{1,0:T(8,128)(2,1)}, bf16[128,4096]{1,0:T(8,128)(2,1)}, f32[8,4096]{1,0:T(8,128)}, bf16[128,4096]{1,0:T(8,128)(2,1)}, /*index=5*/bf16[4096,256]{1,0:T(8,128)(2,1)}) custom-call(s32[1]{0:T(128)S(6)} %copy.38.len_ref, bf16[16,3,256,128]{3,2,1,0:T(8,128)(2,1)} %all-to-all-done.p_ref), custom_call_target="tpu_custom_call" | custom-call | flops 12884901888 | bytes 33554432 | tf_op jit(solution)/shard_map/forward/pallas_call | solution.py:165
  98.2 3.0 %collective-permute-start.12 = (bf16[128,1536]{1,0:T(8,128)(2,1)S(1)}, bf16[128,1536]{1,0:T(8,128)(2,1)}, u32[]{:S(2)}, u32[]{:S(2)}) collective-permute-start(bf16[128,1536]{1,0:T(8,128)(2,1)S(1)} %slice.22), channel_id=1, source_target_pairs={{0,12},{1,13},{2,14},{3,15},{4,0},{5,1},{6,2},{7,3},{8,4},{9,5},{1... | collective-permute-start | bytes 1179656 | tf_op jit(solution)/shard_map/ppermute | solution.py:396
  101.3 1.2 copy-done.8
  104.6 1.1 copy-done.19
  105.7 5.9 %project.2 = (bf16[128,4096]{1,0:T(8,128)(2,1)}, f32[8,4096]{1,0:T(8,128)}, f32[128,1536]{1,0:T(8,128)}) custom-call(s32[8]{0:T(128)S(1)} %stack.87.refs_0_, bf16[256,1536]{1,0:T(8,128)(2,1)} %bitcast.3.refs_1_, bf16[256,1536]{1,0:T(8,128)(2,1)} %get-tuple-element.53.refs_2_, bf16[256,1536]{1,0:T(8,128)(2,1)S(1)} %copy-done.5, ...), custom_call_target="tpu_custom_call" | custom-call | flops 1610612736 | bytes 6291456 | tf_op jit(solution)/shard_map/project/pallas_call | solution.py:249
  114.8 1.2 copy-done.9
  117.9 1.2 copy-done.14
  119.1 1.1 copy-done.15
  121.2 5.9 %project.3 = (bf16[128,4096]{1,0:T(8,128)(2,1)}, f32[8,4096]{1,0:T(8,128)}, f32[128,1536]{1,0:T(8,128)}) custom-call(s32[12]{0:T(128)S(1)} %stack.78.refs_0_, bf16[128,1536]{1,0:T(8,128)(2,1)S(1)} %copy-done.11, bf16[128,1536]{1,0:T(8,128)(2,1)} %get-tuple-element.50.refs_2_, bf16[256,1536]{1,0:T(8,128)(2,1)S(1)} %copy-done.1, ...), custom_call_target="tpu_custom_call" | custom-call | flops 1610612736 | bytes 6291456 | tf_op jit(solution)/shard_map/project/pallas_call | solution.py:249
  127.1 1.3 fusion.1
  129.3 6.8 %all-to-all-start.1 = ((bf16[8,128,192]{1,2,0:T(8,128)(2,1)}), bf16[8,128,192]{1,2,0:T(8,128)(2,1)S(1)}, u32[]{:S(2)}, u32[]{:S(2)}) async-start(bf16[8,128,192]{1,2,0:T(8,128)(2,1)} %bitcast.25), calls=%async_computation.1 | async-start | bytes 786432 | tf_op jit(solution)/shard_map/all_to_all | solution.py:458
  136.0 20.6 %backward.2 = (f32[128,4096]{1,0:T(8,128)}, bf16[16,2,128,128]{3,2,1,0:T(8,128)(2,1)}) custom-call(bf16[4096,4096]{1,0:T(8,128)(2,1)} %get-tuple-element.44.refs_0_, bf16[128,4096]{1,0:T(8,128)(2,1)} %get-tuple-element.62.refs_1_, f32[8,4096]{1,0:T(8,128)} %get-tuple-element.63.refs_2_, bf16[128,4096]{1,0:T(8,128)(2,1)} %get-tuple-element.64.refs_3_, ...), custom_call_target="tpu_custom_call" | custom-call | flops 10737418240 | bytes 16777216 | tf_op jit(solution)/shard_map/backward/pallas_call | solution.py:344
  156.8 3.7 %all-to-all-start.2 = ((bf16[16,2,128,128]{3,2,1,0:T(8,128)(2,1)}), bf16[16,2,128,128]{3,2,1,0:T(8,128)(2,1)S(1)}, u32[]{:S(2)}, u32[]{:S(2)}) async-start(bf16[16,2,128,128]{3,2,1,0:T(8,128)(2,1)} %get-tuple-element.70), calls=%async_computation.2 | async-start | bytes 2097152 | tf_op jit(solution)/shard_map/all_to_all | solution.py:461
  161.2 21.1 %backward.3 = bf16[16,544,128]{2,1,0:T(8,128)(2,1)} custom-call(bf16[4096,4096]{1,0:T(8,128)(2,1)} %get-tuple-element.44.refs_0_, bf16[128,4096]{1,0:T(8,128)(2,1)} %get-tuple-element.62.refs_1_, f32[8,4096]{1,0:T(8,128)} %get-tuple-element.63.refs_2_, bf16[128,4096]{1,0:T(8,128)(2,1)} %get-tuple-element.64.refs_3_, ...), custom_call_target="tpu_custom_call" | custom-call | flops 10737418240 | bytes 16777216 | tf_op jit(solution)/shard_map/backward/pallas_call | solution.py:344
  182.3 5.7 %all-to-all-start.3 = ((bf16[16,544,128]{2,1,0:T(8,128)(2,1)}), bf16[16,544,128]{2,1,0:T(8,128)(2,1)S(1)}, u32[]{:S(2)}, u32[]{:S(2)}) async-start(bf16[16,544,128]{2,1,0:T(8,128)(2,1)} %backward.3), calls=%async_computation.3 | async-start | bytes 4456448 | tf_op jit(solution)/shard_map/all_to_all | solution.py:473
  188.0 3.7 %collective-permute-start.19 = (f32[128]{0:T(128)S(1)}, f32[128]{0:T(128)S(1)}, u32[]{:S(2)}, u32[]{:S(2)}) collective-permute-start(f32[128]{0:T(128)S(1)} %get-tuple-element.79), channel_id=1, source_target_pairs={{0,16},{16,0},{32,48},{48,32},{64,80},{80,64},{96,112},{112,96},{1... | collective-permute-start | bytes 1544 | tf_op jit(solution)/shard_map/ppermute | solution.py:370
  191.7 1.5 collective-permute-start.20
  193.2 25.1 %collective-permute-done.19 = f32[128]{0:T(128)S(1)} collective-permute-done((f32[128]{0:T(128)S(1)}, f32[128]{0:T(128)S(1)}, u32[]{:S(2)}, u32[]{:S(2)}) %collective-permute-start.19) | collective-permute-done | bytes 544 | tf_op jit(solution)/shard_map/ppermute | solution.py:370
  218.3 3.0 %collective-permute-start.22 = (f32[128]{0:T(128)S(1)}, f32[128]{0:T(128)S(1)}, u32[]{:S(2)}, u32[]{:S(2)}) collective-permute-start(f32[128]{0:T(128)S(1)} %add_add_fusion), channel_id=1, source_target_pairs={{0,64},{16,80},{32,96},{48,112},{64,0},{80,16},{96,32},{112,48},{1... | collective-permute-start | bytes 1544 | tf_op jit(solution)/shard_map/ppermute | solution.py:370
  221.4 2.1 collective-permute-done.22
  224.0 2.1 join_columns.1
  (102 shorter events, 19.7 us)
Async XLA Ops:
  0.6 19.6 %collective-permute-start = (bf16[256,1536]{1,0:T(8,128)(2,1)}, bf16[256,1536]{1,0:T(8,128)(2,1)}, u32[]{:S(2)}, u32[]{:S(2)}) collective-permute-start(bf16[256,1536]{1,0:T(8,128)(2,1)} %bitcast.3.refs_1_), channel_id=1, source_target_pairs={{0,2},{1,3},{2,0},{3,1},{4,6},{5,7},{6,4},{7,5},{8,10},{9,11},{10,... | collective-permute-start | bytes 2359304 | tf_op jit(solution)/shard_map/ppermute | solution.py:396
  2.4 21.5 %collective-permute-start.1 = (bf16[256,1536]{1,0:T(8,128)(2,1)}, bf16[256,1536]{1,0:T(8,128)(2,1)S(1)}, u32[]{:S(2)}, u32[]{:S(2)}) collective-permute-start(bf16[256,1536]{1,0:T(8,128)(2,1)} %bitcast.3.refs_1_), channel_id=1, source_target_pairs={{0,4},{1,5},{2,6},{3,7},{4,8},{5,9},{6,10},{7,11},{8,12},{9,13},{1... | collective-permute-start | bytes 2359304 | tf_op jit(solution)/shard_map/ppermute | solution.py:396
  4.3 19.6 %collective-permute-start.2 = (bf16[256,1536]{1,0:T(8,128)(2,1)}, bf16[256,1536]{1,0:T(8,128)(2,1)S(1)}, u32[]{:S(2)}, u32[]{:S(2)}) collective-permute-start(bf16[256,1536]{1,0:T(8,128)(2,1)} %bitcast.3.refs_1_), channel_id=1, source_target_pairs={{0,12},{1,13},{2,14},{3,15},{4,0},{5,1},{6,2},{7,3},{8,4},{9,5},{1... | collective-permute-start | bytes 2359304 | tf_op jit(solution)/shard_map/ppermute | solution.py:396
  23.9 9.3 %copy-start.6 = (bf16[256,1536]{1,0:T(8,128)(2,1)}, bf16[256,1536]{1,0:T(8,128)(2,1)S(1)}, u32[]{:S(2)}) copy-start(bf16[256,1536]{1,0:T(8,128)(2,1)S(1)} %collective-permute-done.2.refs_3_) | copy-start | bytes 2359300
  23.9 43.7 %all-to-all-start = ((bf16[16,3,256,128]{3,2,1,0:T(8,128)(2,1)}), bf16[16,3,256,128]{3,2,1,0:T(8,128)(2,1)}, u32[]{:S(2)}, u32[]{:S(2)}) async-start(bf16[16,3,256,128]{3,2,1,0:T(8,128)(2,1)} %split_columns.1), calls=%async_computation | async-start | bytes 6291456 | tf_op jit(solution)/shard_map/all_to_all | solution.py:416
  28.4 68.5 %collective-permute-start.7 = (bf16[256,1536]{1,0:T(8,128)(2,1)}, bf16[256,1536]{1,0:T(8,128)(2,1)}, u32[]{:S(2)}, u32[]{:S(2)}) collective-permute-start(bf16[256,1536]{1,0:T(8,128)(2,1)} %bitcast.3.refs_1_), channel_id=1, source_target_pairs={{0,1},{1,0},{2,3},{3,2},{4,5},{5,4},{6,7},{7,6},{8,9},{9,8},{10,11... | collective-permute-start | bytes 2359304 | tf_op jit(solution)/shard_map/ppermute | solution.py:396
  29.3 62.3 %collective-permute-start.5 = (bf16[256,1536]{1,0:T(8,128)(2,1)}, bf16[256,1536]{1,0:T(8,128)(2,1)S(1)}, u32[]{:S(2)}, u32[]{:S(2)}) collective-permute-start(bf16[256,1536]{1,0:T(8,128)(2,1)} %collective-permute-done.refs_1_), channel_id=1, source_target_pairs={{0,4},{1,5},{2,6},{3,7},{4,8},{5,9},{6,10},{7,11},{8,12},{9,13},{1... | collective-permute-start | bytes 2359304 | tf_op jit(solution)/shard_map/ppermute | solution.py:396
  31.1 60.6 %collective-permute-start.6 = (bf16[256,1536]{1,0:T(8,128)(2,1)}, bf16[256,1536]{1,0:T(8,128)(2,1)S(1)}, u32[]{:S(2)}, u32[]{:S(2)}) collective-permute-start(bf16[256,1536]{1,0:T(8,128)(2,1)} %collective-permute-done.refs_1_), channel_id=1, source_target_pairs={{0,12},{1,13},{2,14},{3,15},{4,0},{5,1},{6,2},{7,3},{8,4},{9,5},{1... | collective-permute-start | bytes 2359304 | tf_op jit(solution)/shard_map/ppermute | solution.py:396
  32.6 59.0 %collective-permute-start.3 = (bf16[128,1536]{1,0:T(8,128)(2,1)S(1)}, bf16[128,1536]{1,0:T(8,128)(2,1)S(1)}, u32[]{:S(2)}, u32[]{:S(2)}) collective-permute-start(bf16[128,1536]{1,0:T(8,128)(2,1)S(1)} %slice.19), channel_id=1, source_target_pairs={{0,4},{1,5},{2,6},{3,7},{4,8},{5,9},{6,10},{7,11},{8,12},{9,13},{1... | collective-permute-start | bytes 1179656 | tf_op jit(solution)/shard_map/ppermute | solution.py:396
  33.2 58.4 %collective-permute-start.4 = (bf16[128,1536]{1,0:T(8,128)(2,1)S(1)}, bf16[128,1536]{1,0:T(8,128)(2,1)}, u32[]{:S(2)}, u32[]{:S(2)}) collective-permute-start(bf16[128,1536]{1,0:T(8,128)(2,1)S(1)} %slice.20), channel_id=1, source_target_pairs={{0,12},{1,13},{2,14},{3,15},{4,0},{5,1},{6,2},{7,3},{8,4},{9,5},{1... | collective-permute-start | bytes 1179656 | tf_op jit(solution)/shard_map/ppermute | solution.py:396
  92.9 4.2 %collective-permute-start.10 = (bf16[256,1536]{1,0:T(8,128)(2,1)}, bf16[256,1536]{1,0:T(8,128)(2,1)S(1)}, u32[]{:S(2)}, u32[]{:S(2)}) collective-permute-start(bf16[256,1536]{1,0:T(8,128)(2,1)} %get-tuple-element.55.refs_4_), channel_id=1, source_target_pairs={{0,1},{1,0},{2,3},{3,2},{4,5},{5,4},{6,7},{7,6},{8,9},{9,8},{10,11... | collective-permute-start | bytes 2359304 | tf_op jit(solution)/shard_map/ppermute | solution.py:396
  93.0 5.2 %collective-permute-start.8 = (bf16[256,1536]{1,0:T(8,128)(2,1)}, bf16[256,1536]{1,0:T(8,128)(2,1)S(1)}, u32[]{:S(2)}, u32[]{:S(2)}) collective-permute-start(bf16[256,1536]{1,0:T(8,128)(2,1)} %get-tuple-element.53.refs_2_), channel_id=1, source_target_pairs={{0,1},{1,0},{2,3},{3,2},{4,5},{5,4},{6,7},{7,6},{8,9},{9,8},{10,11... | collective-permute-start | bytes 2359304 | tf_op jit(solution)/shard_map/ppermute | solution.py:396
  93.4 7.8 %collective-permute-start.9 = (bf16[256,1536]{1,0:T(8,128)(2,1)}, bf16[256,1536]{1,0:T(8,128)(2,1)}, u32[]{:S(2)}, u32[]{:S(2)}) collective-permute-start(bf16[256,1536]{1,0:T(8,128)(2,1)} %get-tuple-element.54.refs_3_), channel_id=1, source_target_pairs={{0,1},{1,0},{2,3},{3,2},{4,5},{5,4},{6,7},{7,6},{8,9},{9,8},{10,11... | collective-permute-start | bytes 2359304 | tf_op jit(solution)/shard_map/ppermute | solution.py:396
  95.4 18.3 %collective-permute-start.15 = (bf16[256,1536]{1,0:T(8,128)(2,1)}, bf16[256,1536]{1,0:T(8,128)(2,1)}, u32[]{:S(2)}, u32[]{:S(2)}) collective-permute-start(bf16[256,1536]{1,0:T(8,128)(2,1)} %get-tuple-element.51.refs_3_), channel_id=1, source_target_pairs={{0,1},{1,0},{2,3},{3,2},{4,5},{5,4},{6,7},{7,6},{8,9},{9,8},{10,11... | collective-permute-start | bytes 2359304 | tf_op jit(solution)/shard_map/ppermute | solution.py:396
  96.9 16.7 %collective-permute-start.16 = (bf16[256,1536]{1,0:T(8,128)(2,1)}, bf16[256,1536]{1,0:T(8,128)(2,1)}, u32[]{:S(2)}, u32[]{:S(2)}) collective-permute-start(bf16[256,1536]{1,0:T(8,128)(2,1)} %get-tuple-element.52.refs_4_), channel_id=1, source_target_pairs={{0,1},{1,0},{2,3},{3,2},{4,5},{5,4},{6,7},{7,6},{8,9},{9,8},{10,11... | collective-permute-start | bytes 2359304 | tf_op jit(solution)/shard_map/ppermute | solution.py:396
  98.0 13.6 %collective-permute-start.11 = (bf16[128,1536]{1,0:T(8,128)(2,1)S(1)}, bf16[128,1536]{1,0:T(8,128)(2,1)}, u32[]{:S(2)}, u32[]{:S(2)}) collective-permute-start(bf16[128,1536]{1,0:T(8,128)(2,1)S(1)} %slice.21), channel_id=1, source_target_pairs={{0,4},{1,5},{2,6},{3,7},{4,8},{5,9},{6,10},{7,11},{8,12},{9,13},{1... | collective-permute-start | bytes 1179656 | tf_op jit(solution)/shard_map/ppermute | solution.py:396
  98.2 13.9 %collective-permute-start.12 = (bf16[128,1536]{1,0:T(8,128)(2,1)S(1)}, bf16[128,1536]{1,0:T(8,128)(2,1)}, u32[]{:S(2)}, u32[]{:S(2)}) collective-permute-start(bf16[128,1536]{1,0:T(8,128)(2,1)S(1)} %slice.22), channel_id=1, source_target_pairs={{0,12},{1,13},{2,14},{3,15},{4,0},{5,1},{6,2},{7,3},{8,4},{9,5},{1... | collective-permute-start | bytes 1179656 | tf_op jit(solution)/shard_map/ppermute | solution.py:396
  101.2 11.0 %collective-permute-start.13 = (bf16[128,1536]{1,0:T(8,128)(2,1)}, bf16[128,1536]{1,0:T(8,128)(2,1)}, u32[]{:S(2)}, u32[]{:S(2)}) collective-permute-start(bf16[128,1536]{1,0:T(8,128)(2,1)} %get-tuple-element.49.refs_1_), channel_id=1, source_target_pairs={{0,1},{1,0},{2,3},{3,2},{4,5},{5,4},{6,7},{7,6},{8,9},{9,8},{10,11... | collective-permute-start | bytes 1179656 | tf_op jit(solution)/shard_map/ppermute | solution.py:396
  105.7 9.0 %copy-start.3 = (bf16[256,1536]{1,0:T(8,128)(2,1)S(1)}, bf16[256,1536]{1,0:T(8,128)(2,1)}, u32[]{:S(2)}) copy-start(bf16[256,1536]{1,0:T(8,128)(2,1)} %get-tuple-element.52.refs_4_) | copy-start | bytes 2359300
  111.6 2.0 collective-permute-start.14
  112.1 2.1 collective-permute-start.17
  112.2 2.6 %collective-permute-start.18 = (bf16[128,1536]{1,0:T(8,128)(2,1)}, bf16[128,1536]{1,0:T(8,128)(2,1)S(1)}, u32[]{:S(2)}, u32[]{:S(2)}) collective-permute-start(bf16[128,1536]{1,0:T(8,128)(2,1)} %get-tuple-element.59.refs_6_), channel_id=1, source_target_pairs={{0,1},{1,0},{2,3},{3,2},{4,5},{5,4},{6,7},{7,6},{8,9},{9,8},{10,11... | collective-permute-start | bytes 1179656 | tf_op jit(solution)/shard_map/ppermute | solution.py:396
  129.3 27.4 %all-to-all-start.1 = ((bf16[8,128,192]{1,2,0:T(8,128)(2,1)}), bf16[8,128,192]{1,2,0:T(8,128)(2,1)S(1)}, u32[]{:S(2)}, u32[]{:S(2)}) async-start(bf16[8,128,192]{1,2,0:T(8,128)(2,1)} %bitcast.25), calls=%async_computation.1 | async-start | bytes 786432 | tf_op jit(solution)/shard_map/all_to_all | solution.py:458
  156.7 25.6 %copy-start.23 = (f32[128,192]{0,1:T(8,128)}, f32[128,192]{0,1:T(8,128)S(1)}, u32[]{:S(2)}) copy-start(f32[128,192]{0,1:T(8,128)S(1)} %convert_reduce_fusion) | copy-start | bytes 294916
  156.8 25.4 %all-to-all-start.2 = ((bf16[16,2,128,128]{3,2,1,0:T(8,128)(2,1)}), bf16[16,2,128,128]{3,2,1,0:T(8,128)(2,1)S(1)}, u32[]{:S(2)}, u32[]{:S(2)}) async-start(bf16[16,2,128,128]{3,2,1,0:T(8,128)(2,1)} %get-tuple-element.70), calls=%async_computation.2 | async-start | bytes 2097152 | tf_op jit(solution)/shard_map/all_to_all | solution.py:461
  182.3 41.2 %copy-start.25 = (f32[128]{0:T(128)S(1)}, f32[128]{0:T(128)}, u32[]{:S(2)}) copy-start(f32[128]{0:T(128)} %param.16) | copy-start | bytes 1540
  182.3 41.7 %all-to-all-start.3 = ((bf16[16,544,128]{2,1,0:T(8,128)(2,1)}), bf16[16,544,128]{2,1,0:T(8,128)(2,1)S(1)}, u32[]{:S(2)}, u32[]{:S(2)}) async-start(bf16[16,544,128]{2,1,0:T(8,128)(2,1)} %backward.3), calls=%async_computation.3 | async-start | bytes 4456448 | tf_op jit(solution)/shard_map/all_to_all | solution.py:473
  187.9 38.8 %copy-start.24 = (f32[192]{0:T(256)S(1)}, f32[192]{0:T(256)}, u32[]{:S(2)}) copy-start(f32[192]{0:T(256)} %param.17) | copy-start | bytes 2308
  188.0 30.4 %collective-permute-start.19 = (f32[128]{0:T(128)S(1)}, f32[128]{0:T(128)S(1)}, u32[]{:S(2)}, u32[]{:S(2)}) collective-permute-start(f32[128]{0:T(128)S(1)} %get-tuple-element.79), channel_id=1, source_target_pairs={{0,16},{16,0},{32,48},{48,32},{64,80},{80,64},{96,112},{112,96},{1... | collective-permute-start | bytes 1544 | tf_op jit(solution)/shard_map/ppermute | solution.py:370
  191.7 26.7 %collective-permute-start.20 = (f32[128]{0:T(128)S(1)}, f32[128]{0:T(128)S(1)}, u32[]{:S(2)}, u32[]{:S(2)}) collective-permute-start(f32[128]{0:T(128)S(1)} %get-tuple-element.79), channel_id=1, source_target_pairs={{0,32},{16,48},{32,0},{48,16},{64,96},{80,112},{96,64},{112,80},{1... | collective-permute-start | bytes 1544 | tf_op jit(solution)/shard_map/ppermute | solution.py:370
  193.1 25.2 %collective-permute-start.21 = (f32[128]{0:T(128)S(1)}, f32[128]{0:T(128)S(1)}, u32[]{:S(2)}, u32[]{:S(2)}) collective-permute-start(f32[128]{0:T(128)S(1)} %get-tuple-element.79), channel_id=1, source_target_pairs={{0,48},{16,32},{32,16},{48,0},{64,112},{80,96},{96,80},{112,64},{1... | collective-permute-start | bytes 1544 | tf_op jit(solution)/shard_map/ppermute | solution.py:370
  218.3 5.1 %collective-permute-start.22 = (f32[128]{0:T(128)S(1)}, f32[128]{0:T(128)S(1)}, u32[]{:S(2)}, u32[]{:S(2)}) collective-permute-start(f32[128]{0:T(128)S(1)} %add_add_fusion), channel_id=1, source_target_pairs={{0,64},{16,80},{32,96},{48,112},{64,0},{80,16},{96,32},{112,48},{1... | collective-permute-start | bytes 1544 | tf_op jit(solution)/shard_map/ppermute | solution.py:370
  (21 other events, 66.6 us)

commit v9 on v8

--- a/solution.py
+++ b/solution.py
@@ -203,10 +203,12 @@
     )(valid_len, packed)
 
 
-def project(places, pieces, gated, attended, inverse, earlier):
+def project(places, pieces, gated, attended, inverse, earlier, gate=None):
     width = gated.shape[1]
     total = attended.shape[1]
     count = len(pieces)
+    eighth = width // 8
+    operands = list(earlier) + ([] if gate is None else [gate])
     sizes = [piece.shape[0] for piece in pieces]
     starts = [sum(sizes[:i]) for i in range(count)]
     groups, filled = [[]], 0
@@ -221,7 +223,17 @@
         place_ref, sources = refs[0], refs[1 : 1 + count]
         w_ref, o_ref, inv_ref = refs[1 + count : 4 + count]
         before = refs[4 + count : 4 + count + len(earlier)]
-        g_ref, d_ref, a_ref = refs[4 + count + len(earlier) :]
+        outs = refs[4 + count + len(operands) :]
+        g_ref, d_ref, a_ref = outs[:3]
+        held, sems = outs[-2:]
+        copies = [
+            pltpu.make_async_copy(
+                sources[i], held.at[pl.ds(starts[i], sizes[i]), :], sems.at[i]
+            )
+            for i in range(count)
+        ]
+        for copy in copies:
+            copy.start()
         outer = jnp.zeros((HEAD_DIM, width), F32)
         if before:
             g_ref[...] = before[0][...]
@@ -234,7 +246,10 @@
             out = jnp.concatenate([o_ref[:, lane] for lane in lanes], axis=1)
             inv = jnp.concatenate([inv_ref[0:1, lane] for lane in lanes], axis=1)
             first = group[0]
-            rows = jnp.concatenate([sources[i][...] for i in group], axis=0)
+            last = group[-1]
+            for i in group:
+                copies[i].wait()
+            rows = held[starts[first] : starts[last] + sizes[last], :]
             grad = contract(w_ref[...], rows, 1, 1).astype(BF16).astype(F32)
             low = (grad * inv).astype(BF16)
             delta = jnp.sum(low.astype(F32) * out.astype(F32), axis=0, keepdims=True)
@@ -244,18 +259,28 @@
                 d_ref[:, lane] = jnp.broadcast_to(delta[:, at], (8, sizes[i]))
             outer = outer + contract(out, rows, 1, 0)
         a_ref[...] = outer
-
-    vmem = pl.BlockSpec(memory_space=pltpu.VMEM)
+        if gate is not None:
+            partial = (outer * refs[4 + count + len(earlier)][...]).astype(BF16)
+            for i in range(8):
+                outs[3][i] = partial[:, i * eighth : (i + 1) * eighth]
+
+    out_shape = [
+        pltpu.HBM((HEAD_DIM, total), BF16),
+        pltpu.HBM((8, total), F32),
+        pltpu.HBM((HEAD_DIM, width), F32),
+    ]
+    if gate is not None:
+        out_shape.append(pltpu.HBM((8, HEAD_DIM, eighth), BF16))
     return pl.pallas_call(
         body,
         in_specs=[pl.BlockSpec(memory_space=pltpu.SMEM)]
-        + [pl.BlockSpec(memory_space=pltpu.VMEM)] * count
-        + [pl.BlockSpec()] * (3 + len(earlier)),
-        out_specs=[pl.BlockSpec()] * 3,
-        out_shape=[
-            pltpu.HBM((HEAD_DIM, total), BF16),
-            pltpu.HBM((8, total), F32),
-            pltpu.HBM((HEAD_DIM, width), F32),
+        + [pl.BlockSpec(memory_space=pl.ANY)] * count
+        + [pl.BlockSpec()] * (3 + len(operands)),
+        out_specs=[pl.BlockSpec()] * len(out_shape),
+        out_shape=out_shape,
+        scratch_shapes=[
+            pltpu.VMEM((sum(sizes), width), BF16),
+            pltpu.SemaphoreType.DMA((count,)),
         ],
         compiler_params=pltpu.CompilerParams(vmem_limit_bytes=24 * 2**20),
         cost_estimate=pl.CostEstimate(
@@ -264,7 +289,15 @@
             transcendentals=0,
         ),
         name="project",
-    )(places, *pieces, gated, attended, inverse, *earlier)
+    )(
+        places,
+        *[pltpu.with_memory_space_constraint(x, pltpu.HBM) for x in pieces],
+        gated,
+        *[
+            pltpu.with_memory_space_constraint(x, pltpu.HBM)
+            for x in [attended, inverse] + operands
+        ],
+    )
 
 
 def backward(which, low, grad, delta, query, key, value, parts, earlier):
@@ -382,10 +415,10 @@
         lambda *refs: None,
         in_specs=[anywhere] * (1 + len(arrays)),
         out_specs=[anywhere] * len(arrays),
-        out_shape=[jax.ShapeDtypeStruct(x.shape, x.dtype) for x in arrays],
+        out_shape=[pltpu.HBM(x.shape, x.dtype) for x in arrays],
         input_output_aliases={i + 1: i for i in range(len(arrays))},
         name="after",
-    )(token, *arrays)
+    )(token, *[pltpu.with_memory_space_constraint(x, pltpu.HBM) for x in arrays])
 
 
 def move(values, z_step=0, y_step=0, core_step=0):
@@ -423,7 +456,7 @@
     side, below, above, far_low, far_high, side_below, side_above = after(
         inverse, [side, below, above, far_low, far_high, side_below, side_above]
     )
-    side_low, side_high = move(side_below[:half], z_step=1), move(side_above[half:], z_step=3)
+    side_low, side_high = move(far_low, y_step=1), move(far_high, y_step=1)
     found = [
         (own, 0, 0, 0),
         (side, 0, 1, 0),
@@ -450,12 +483,16 @@
                 pieces.append(move(rows, core_step=1) if core_step else rows)
                 places.append(device * tokens + offset)
         made = project(
-            jnp.stack(places).astype(jnp.int32), pieces, gated, attended, inverse, made
+            jnp.stack(places).astype(jnp.int32),
+            pieces,
+            gated,
+            attended,
+            inverse,
+            made,
+            gate if made else None,
         )
-    grad, delta, outer = made
-
-    partial = (outer * gate).astype(BF16).reshape(HEAD_DIM, dp_size, columns)
-    partial = lax.all_to_all(partial.transpose(1, 0, 2), "dp", 0, 0, tiled=True)
+    grad, delta, outer, partial = made
+    partial = lax.all_to_all(partial, "dp", 0, 0, tiled=True)
     some_q, early = backward(0, low, grad, delta, query, key, value, seq_size, [])
     some_q, early, partial = lax.optimization_barrier((some_q, early, partial))
     early = lax.all_to_all(early, "seq", 0, 0, tiled=True)

time: 228 us -> 227 us (level)
  waiting for transfers between devices: 74.6 us -> 81 us
  local copies, waits for them, and re-layouts: 17.4 us -> 11.3 us
    ppermute x19, waiting for transfers between devices: 15.9 us -> 25.8 us  [move(): return lax.ppermute(values, 'seq', pairs)]
    unnamed x54 -> x41, local copies, waits for them, and re-layouts: 13.6 us -> 4.93 us
    pallas_call x2, Pallas kernels: 11.8 us -> 15.4 us  [project(): pl.pallas_call(body, in_specs=[pl.BlockSpec(memory_space=pltpu.SMEM)] + [...]
    all_to_all x1, waiting for transfers between devices: 31.6 us -> 28 us  [shards(): packed = lax.all_to_all(packed, 'seq', 0, 0, tiled=True)]
  transfers between devices with their start and end apart: 27 -> 27, of which waited for: 9 -> 11; matrix products, arithmetic and copies ran while one was open for 2% -> 2% of each run, Pallas kernels for 33% -> 33%
where the time goes in v9:
time: 227 us; the launch traced here: 226 us
  Pallas kernels  85.1 us (37%)
  waiting for transfers between devices  81 us (36%)
  starting transfers between devices  46 us (20%)
  local copies, waits for them, and re-layouts  11.3 us (5%)
    pallas_call x2, Pallas kernels, backward(): pl.pallas_call(body, grid=(steps,), in_specs=[pl.BlockSpec((some, BLOCK),...  41.7 us
    all_to_all x1, waiting for transfers between devices, shards(): packed = lax.all_to_all(packed, 'seq', 0, 0, tiled=True)  28 us
    ppermute x4, waiting for transfers between devices, swap(): return lax.ppermute(values, axis, [(i, i ^ bit) for i in range(size)])  27.2 us
    ppermute x19, waiting for transfers between devices, move(): return lax.ppermute(values, 'seq', pairs)  25.8 us
    pallas_call x1, Pallas kernels, forward(): pl.pallas_call(body, grid_spec=pltpu.PrefetchScalarGridSpec(num_scalar_pr...  21.5 us
    ppermute x19, starting transfers between devices, move(): return lax.ppermute(values, 'seq', pairs)  17.6 us
    pallas_call x2, Pallas kernels, project(): pl.pallas_call(body, in_specs=[pl.BlockSpec(memory_space=pltpu.SMEM)] + [...  15.4 us
    ppermute x4, starting transfers between devices, swap(): return lax.ppermute(values, axis, [(i, i ^ bit) for i in range(size)])  8.18 us
  transfers between devices with their start and end apart: 27, of which 11 were waited for; matrix products, arithmetic and copies ran while one was open for 2% of the time, Pallas kernels for 33%

profile of v9, /device:TPU:0, one launch (start us, length us, event | category | flops | bytes accessed | tf_op | source)
XLA Modules:
  0.0 226.4 jit_solution(8660890013905303985)
XLA Ops:
  0.6 1.7 collective-permute-start
  2.4 1.9 collective-permute-start.1
  4.3 2.1 collective-permute-start.2
  6.4 4.4 %split_columns.1 = bf16[16,3,256,128]{3,2,1,0:T(8,128)(2,1)} custom-call(bf16[256,2048]{1,0:T(8,128)(2,1)} %bitcast.36, bf16[256,2048]{1,0:T(8,128)(2,1)} %bitcast.37, bf16[256,2048]{1,0:T(8,128)(2,1)} %bitcast.38), custom_call_target="tpu_custom_call" | custom-call | tf_op jit(solution)/shard_map/split_columns/pallas_call | solution.py:36
  10.8 9.3 %collective-permute-done.refs_1_ = bf16[256,1536]{1,0:T(8,128)(2,1)S(1)} collective-permute-done((bf16[256,1536]{1,0:T(8,128)(2,1)}, bf16[256,1536]{1,0:T(8,128)(2,1)S(1)}, u32[]{:S(2)}, u32[]{:S(2)}) %collective-permute-start) | collective-permute-done | bytes 786464 | tf_op jit(solution)/shard_map/ppermute | solution.py:429
  20.1 3.8 %collective-permute-done.1.refs_2_ = bf16[256,1536]{1,0:T(8,128)(2,1)S(1)} collective-permute-done((bf16[256,1536]{1,0:T(8,128)(2,1)}, bf16[256,1536]{1,0:T(8,128)(2,1)S(1)}, u32[]{:S(2)}, u32[]{:S(2)}) %collective-permute-start.1) | collective-permute-done | bytes 786464 | tf_op jit(solution)/shard_map/ppermute | solution.py:429
  25.0 4.1 %all-to-all-start = ((bf16[16,3,256,128]{3,2,1,0:T(8,128)(2,1)}), bf16[16,3,256,128]{3,2,1,0:T(8,128)(2,1)S(1)}, u32[]{:S(2)}, u32[]{:S(2)}) async-start(bf16[16,3,256,128]{3,2,1,0:T(8,128)(2,1)} %split_columns.1), calls=%async_computation | async-start | bytes 6291456 | tf_op jit(solution)/shard_map/all_to_all | solution.py:449
  30.2 1.7 collective-permute-start.5
  31.9 1.6 collective-permute-start.6
  33.5 1.8 slice.13
  35.7 1.8 slice.14
  37.5 2.8 %collective-permute-start.4 = (bf16[128,1536]{1,0:T(8,128)(2,1)}, bf16[128,1536]{1,0:T(8,128)(2,1)}, u32[]{:S(2)}, u32[]{:S(2)}) collective-permute-start(bf16[128,1536]{1,0:T(8,128)(2,1)} %slice.14), channel_id=1, source_target_pairs={{0,12},{1,13},{2,14},{3,15},{4,0},{5,1},{6,2},{7,3},{8,4},{9,5},{1... | collective-permute-start | bytes 1179656 | tf_op jit(solution)/shard_map/ppermute | solution.py:429
  40.3 28.0 %all-to-all-done.p_ref = bf16[16,3,256,128]{3,2,1,0:T(8,128)(2,1)S(1)} async-done(((bf16[16,3,256,128]{3,2,1,0:T(8,128)(2,1)}), bf16[16,3,256,128]{3,2,1,0:T(8,128)(2,1)S(1)}, u32[]{:S(2)}, u32[]{:S(2)}) %all-to-all-start) | async-done | bytes 3145760 | tf_op jit(solution)/shard_map/all_to_all | solution.py:449
  68.3 21.5 %forward.1 = (bf16[4096,4096]{1,0:T(8,128)(2,1)}, bf16[128,4096]{1,0:T(8,128)(2,1)}, bf16[128,4096]{1,0:T(8,128)(2,1)}, f32[8,4096]{1,0:T(8,128)}, bf16[128,4096]{1,0:T(8,128)(2,1)}, /*index=5*/bf16[4096,256]{1,0:T(8,128)(2,1)}) custom-call(s32[1]{0:T(128)S(6)} %copy.41.len_ref, bf16[16,3,256,128]{3,2,1,0:T(8,128)(2,1)S(1)} %all-to-all-done.p_ref), custom_call_target="tpu_custom_call" | custom-call | flops 12884901888 | bytes 33554432 | tf_op jit(solution)/shard_map/forward/pallas_call | solution.py:165
  89.8 2.7 %collective-permute-done.3.refs_4_ = bf16[128,1536]{1,0:T(8,128)(2,1)S(1)} collective-permute-done((bf16[128,1536]{1,0:T(8,128)(2,1)}, bf16[128,1536]{1,0:T(8,128)(2,1)S(1)}, u32[]{:S(2)}, u32[]{:S(2)}) %collective-permute-start.3) | collective-permute-done | bytes 393248 | tf_op jit(solution)/shard_map/ppermute | solution.py:429
  94.0 1.5 collective-permute-start.11
  95.7 1.5 collective-permute-start.12
  99.0 7.3 %project.2 = (bf16[128,4096]{1,0:T(8,128)(2,1)}, f32[8,4096]{1,0:T(8,128)}, f32[128,1536]{1,0:T(8,128)}) custom-call(s32[8]{0:T(128)S(1)} %stack.87.refs_0_, bf16[256,1536]{1,0:T(8,128)(2,1)} %bitcast.43, bf16[256,1536]{1,0:T(8,128)(2,1)} %get-tuple-element.54.refs_2_, bf16[256,1536]{1,0:T(8,128)(2,1)} %get-tuple-element.55.refs_3_, ...), custom_call_target="tpu_custom_call" | custom-call | flops 1610612736 | bytes 6291456 | tf_op jit(solution)/shard_map/project/pallas_call | solution.py:274
  106.8 7.2 %collective-permute-done.12.refs_2_ = bf16[128,1536]{1,0:T(8,128)(2,1)S(1)} collective-permute-done((bf16[128,1536]{1,0:T(8,128)(2,1)}, bf16[128,1536]{1,0:T(8,128)(2,1)S(1)}, u32[]{:S(2)}, u32[]{:S(2)}) %collective-permute-start.12) | collective-permute-done | bytes 393248 | tf_op jit(solution)/shard_map/ppermute | solution.py:429
  118.0 8.1 %project.3 = (bf16[128,4096]{1,0:T(8,128)(2,1)}, f32[8,4096]{1,0:T(8,128)}, f32[128,1536]{1,0:T(8,128)}, bf16[8,128,192]{2,1,0:T(8,128)(2,1)}) custom-call(s32[12]{0:T(128)S(1)} %stack.78.refs_0_, bf16[128,1536]{1,0:T(8,128)(2,1)} %get-tuple-element.50.refs_1_, bf16[128,1536]{1,0:T(8,128)(2,1)} %get-tuple-element.51.refs_2_, ...), custom_call_target="tpu_custom_call" | custom-call | flops 1610612736 | bytes 6291456 | tf_op jit(solution)/shard_map/project/pallas_call | solution.py:274
  126.1 2.0 copy.25
  128.1 6.8 %all-to-all-start.1 = ((bf16[8,128,192]{1,2,0:T(8,128)(2,1)}), bf16[8,128,192]{1,2,0:T(8,128)(2,1)S(1)}, u32[]{:S(2)}, u32[]{:S(2)}) async-start(bf16[8,128,192]{1,2,0:T(8,128)(2,1)} %copy.25), calls=%async_computation.1 | async-start | bytes 786432 | tf_op jit(solution)/shard_map/all_to_all | solution.py:495
  134.9 20.6 %backward.2 = (f32[128,4096]{1,0:T(8,128)}, bf16[16,2,128,128]{3,2,1,0:T(8,128)(2,1)}) custom-call(bf16[4096,4096]{1,0:T(8,128)(2,1)} %get-tuple-element.45.refs_0_, bf16[128,4096]{1,0:T(8,128)(2,1)} %get-tuple-element.63.refs_1_, f32[8,4096]{1,0:T(8,128)} %get-tuple-element.64.refs_2_, bf16[128,4096]{1,0:T(8,128)(2,1)} %get-tuple-element.65.refs_3_, ...), custom_call_target="tpu_custom_call" | custom-call | flops 10737418240 | bytes 16777216 | tf_op jit(solution)/shard_map/backward/pallas_call | solution.py:377
  156.0 3.7 %all-to-all-start.2 = ((bf16[16,2,128,128]{3,2,1,0:T(8,128)(2,1)}), bf16[16,2,128,128]{3,2,1,0:T(8,128)(2,1)S(1)}, u32[]{:S(2)}, u32[]{:S(2)}) async-start(bf16[16,2,128,128]{3,2,1,0:T(8,128)(2,1)} %get-tuple-element.71), calls=%async_computation.2 | async-start | bytes 2097152 | tf_op jit(solution)/shard_map/all_to_all | solution.py:498
  160.4 21.1 %backward.3 = bf16[16,544,128]{2,1,0:T(8,128)(2,1)} custom-call(bf16[4096,4096]{1,0:T(8,128)(2,1)} %get-tuple-element.45.refs_0_, bf16[128,4096]{1,0:T(8,128)(2,1)} %get-tuple-element.63.refs_1_, f32[8,4096]{1,0:T(8,128)} %get-tuple-element.64.refs_2_, bf16[128,4096]{1,0:T(8,128)(2,1)} %get-tuple-element.65.refs_3_, ...), custom_call_target="tpu_custom_call" | custom-call | flops 10737418240 | bytes 16777216 | tf_op jit(solution)/shard_map/backward/pallas_call | solution.py:377
  181.5 5.7 %all-to-all-start.3 = ((bf16[16,544,128]{2,1,0:T(8,128)(2,1)}), bf16[16,544,128]{2,1,0:T(8,128)(2,1)S(1)}, u32[]{:S(2)}, u32[]{:S(2)}) async-start(bf16[16,544,128]{2,1,0:T(8,128)(2,1)} %backward.3), calls=%async_computation.3 | async-start | bytes 4456448 | tf_op jit(solution)/shard_map/all_to_all | solution.py:510
  187.2 3.6 %collective-permute-start.19 = (f32[128]{0:T(128)S(1)}, f32[128]{0:T(128)S(1)}, u32[]{:S(2)}, u32[]{:S(2)}) collective-permute-start(f32[128]{0:T(128)S(1)} %get-tuple-element.88), channel_id=1, source_target_pairs={{0,16},{16,0},{32,48},{48,32},{64,80},{80,64},{96,112},{112,96},{1... | collective-permute-start | bytes 1544 | tf_op jit(solution)/shard_map/ppermute | solution.py:403
  190.8 1.5 collective-permute-start.20
  192.3 25.1 %collective-permute-done.19 = f32[128]{0:T(128)S(1)} collective-permute-done((f32[128]{0:T(128)S(1)}, f32[128]{0:T(128)S(1)}, u32[]{:S(2)}, u32[]{:S(2)}) %collective-permute-start.19) | collective-permute-done | bytes 544 | tf_op jit(solution)/shard_map/ppermute | solution.py:403
  217.5 3.0 %collective-permute-start.22 = (f32[128]{0:T(128)S(1)}, f32[128]{0:T(128)S(1)}, u32[]{:S(2)}, u32[]{:S(2)}) collective-permute-start(f32[128]{0:T(128)S(1)} %add_add_fusion), channel_id=1, source_target_pairs={{0,64},{16,80},{32,96},{48,112},{64,0},{80,16},{96,32},{112,48},{1... | collective-permute-start | bytes 1544 | tf_op jit(solution)/shard_map/ppermute | solution.py:403
  220.5 2.1 collective-permute-done.22
  223.1 2.1 join_columns.1
  (87 shorter events, 12.9 us)
Async XLA Ops:
  0.6 19.5 %collective-permute-start = (bf16[256,1536]{1,0:T(8,128)(2,1)}, bf16[256,1536]{1,0:T(8,128)(2,1)S(1)}, u32[]{:S(2)}, u32[]{:S(2)}) collective-permute-start(bf16[256,1536]{1,0:T(8,128)(2,1)} %bitcast.39), channel_id=1, source_target_pairs={{0,2},{1,3},{2,0},{3,1},{4,6},{5,7},{6,4},{7,5},{8,10},{9,11},{10,... | collective-permute-start | bytes 2359304 | tf_op jit(solution)/shard_map/ppermute | solution.py:429
  2.4 21.5 %collective-permute-start.1 = (bf16[256,1536]{1,0:T(8,128)(2,1)}, bf16[256,1536]{1,0:T(8,128)(2,1)S(1)}, u32[]{:S(2)}, u32[]{:S(2)}) collective-permute-start(bf16[256,1536]{1,0:T(8,128)(2,1)} %bitcast.40), channel_id=1, source_target_pairs={{0,4},{1,5},{2,6},{3,7},{4,8},{5,9},{6,10},{7,11},{8,12},{9,13},{1... | collective-permute-start | bytes 2359304 | tf_op jit(solution)/shard_map/ppermute | solution.py:429
  4.3 19.6 %collective-permute-start.2 = (bf16[256,1536]{1,0:T(8,128)(2,1)}, bf16[256,1536]{1,0:T(8,128)(2,1)S(1)}, u32[]{:S(2)}, u32[]{:S(2)}) collective-permute-start(bf16[256,1536]{1,0:T(8,128)(2,1)} %bitcast.41), channel_id=1, source_target_pairs={{0,12},{1,13},{2,14},{3,15},{4,0},{5,1},{6,2},{7,3},{8,4},{9,5},{1... | collective-permute-start | bytes 2359304 | tf_op jit(solution)/shard_map/ppermute | solution.py:429
  25.0 43.2 %all-to-all-start = ((bf16[16,3,256,128]{3,2,1,0:T(8,128)(2,1)}), bf16[16,3,256,128]{3,2,1,0:T(8,128)(2,1)S(1)}, u32[]{:S(2)}, u32[]{:S(2)}) async-start(bf16[16,3,256,128]{3,2,1,0:T(8,128)(2,1)} %split_columns.1), calls=%async_computation | async-start | bytes 6291456 | tf_op jit(solution)/shard_map/all_to_all | solution.py:449
  29.1 66.4 %collective-permute-start.7 = (bf16[256,1536]{1,0:T(8,128)(2,1)}, bf16[256,1536]{1,0:T(8,128)(2,1)}, u32[]{:S(2)}, u32[]{:S(2)}) collective-permute-start(bf16[256,1536]{1,0:T(8,128)(2,1)} %bitcast.42), channel_id=1, source_target_pairs={{0,1},{1,0},{2,3},{3,2},{4,5},{5,4},{6,7},{7,6},{8,9},{9,8},{10,11... | collective-permute-start | bytes 2359304 | tf_op jit(solution)/shard_map/ppermute | solution.py:429
  30.2 62.3 %collective-permute-start.5 = (bf16[256,1536]{1,0:T(8,128)(2,1)}, bf16[256,1536]{1,0:T(8,128)(2,1)}, u32[]{:S(2)}, u32[]{:S(2)}) collective-permute-start(bf16[256,1536]{1,0:T(8,128)(2,1)} %copy-done.2), channel_id=1, source_target_pairs={{0,4},{1,5},{2,6},{3,7},{4,8},{5,9},{6,10},{7,11},{8,12},{9,13},{1... | collective-permute-start | bytes 2359304 | tf_op jit(solution)/shard_map/ppermute | solution.py:429
  31.9 60.5 %collective-permute-start.6 = (bf16[256,1536]{1,0:T(8,128)(2,1)}, bf16[256,1536]{1,0:T(8,128)(2,1)}, u32[]{:S(2)}, u32[]{:S(2)}) collective-permute-start(bf16[256,1536]{1,0:T(8,128)(2,1)} %copy-done.2), channel_id=1, source_target_pairs={{0,12},{1,13},{2,14},{3,15},{4,0},{5,1},{6,2},{7,3},{8,4},{9,5},{1... | collective-permute-start | bytes 2359304 | tf_op jit(solution)/shard_map/ppermute | solution.py:429
  35.2 57.2 %collective-permute-start.3 = (bf16[128,1536]{1,0:T(8,128)(2,1)}, bf16[128,1536]{1,0:T(8,128)(2,1)S(1)}, u32[]{:S(2)}, u32[]{:S(2)}) collective-permute-start(bf16[128,1536]{1,0:T(8,128)(2,1)} %slice.13), channel_id=1, source_target_pairs={{0,4},{1,5},{2,6},{3,7},{4,8},{5,9},{6,10},{7,11},{8,12},{9,13},{1... | collective-permute-start | bytes 1179656 | tf_op jit(solution)/shard_map/ppermute | solution.py:429
  37.5 55.0 %collective-permute-start.4 = (bf16[128,1536]{1,0:T(8,128)(2,1)}, bf16[128,1536]{1,0:T(8,128)(2,1)}, u32[]{:S(2)}, u32[]{:S(2)}) collective-permute-start(bf16[128,1536]{1,0:T(8,128)(2,1)} %slice.14), channel_id=1, source_target_pairs={{0,12},{1,13},{2,14},{3,15},{4,0},{5,1},{6,2},{7,3},{8,4},{9,5},{1... | collective-permute-start | bytes 1179656 | tf_op jit(solution)/shard_map/ppermute | solution.py:429
  93.2 2.5 %collective-permute-start.10 = (bf16[256,1536]{1,0:T(8,128)(2,1)}, bf16[256,1536]{1,0:T(8,128)(2,1)S(1)}, u32[]{:S(2)}, u32[]{:S(2)}) collective-permute-start(bf16[256,1536]{1,0:T(8,128)(2,1)} %get-tuple-element.56.refs_4_), channel_id=1, source_target_pairs={{0,1},{1,0},{2,3},{3,2},{4,5},{5,4},{6,7},{7,6},{8,9},{9,8},{10,11... | collective-permute-start | bytes 2359304 | tf_op jit(solution)/shard_map/ppermute | solution.py:429
  93.2 4.7 %collective-permute-start.8 = (bf16[256,1536]{1,0:T(8,128)(2,1)}, bf16[256,1536]{1,0:T(8,128)(2,1)S(1)}, u32[]{:S(2)}, u32[]{:S(2)}) collective-permute-start(bf16[256,1536]{1,0:T(8,128)(2,1)} %get-tuple-element.54.refs_2_), channel_id=1, source_target_pairs={{0,1},{1,0},{2,3},{3,2},{4,5},{5,4},{6,7},{7,6},{8,9},{9,8},{10,11... | collective-permute-start | bytes 2359304 | tf_op jit(solution)/shard_map/ppermute | solution.py:429
  93.7 4.4 %collective-permute-start.9 = (bf16[256,1536]{1,0:T(8,128)(2,1)}, bf16[256,1536]{1,0:T(8,128)(2,1)}, u32[]{:S(2)}, u32[]{:S(2)}) collective-permute-start(bf16[256,1536]{1,0:T(8,128)(2,1)} %get-tuple-element.55.refs_3_), channel_id=1, source_target_pairs={{0,1},{1,0},{2,3},{3,2},{4,5},{5,4},{6,7},{7,6},{8,9},{9,8},{10,11... | collective-permute-start | bytes 2359304 | tf_op jit(solution)/shard_map/ppermute | solution.py:429
  94.0 12.3 %collective-permute-start.11 = (bf16[128,1536]{1,0:T(8,128)(2,1)}, bf16[128,1536]{1,0:T(8,128)(2,1)S(1)}, u32[]{:S(2)}, u32[]{:S(2)}) collective-permute-start(bf16[128,1536]{1,0:T(8,128)(2,1)} %get-tuple-element.50.refs_1_), channel_id=1, source_target_pairs={{0,2},{1,3},{2,0},{3,1},{4,6},{5,7},{6,4},{7,5},{8,10},{9,11},{10,... | collective-permute-start | bytes 1179656 | tf_op jit(solution)/shard_map/ppermute | solution.py:429
  95.5 19.3 %collective-permute-start.13 = (bf16[128,1536]{1,0:T(8,128)(2,1)}, bf16[128,1536]{1,0:T(8,128)(2,1)S(1)}, u32[]{:S(2)}, u32[]{:S(2)}) collective-permute-start(bf16[128,1536]{1,0:T(8,128)(2,1)} %get-tuple-element.50.refs_1_), channel_id=1, source_target_pairs={{0,1},{1,0},{2,3},{3,2},{4,5},{5,4},{6,7},{7,6},{8,9},{9,8},{10,11... | collective-permute-start | bytes 1179656 | tf_op jit(solution)/shard_map/ppermute | solution.py:429
  95.7 18.3 %collective-permute-start.12 = (bf16[128,1536]{1,0:T(8,128)(2,1)}, bf16[128,1536]{1,0:T(8,128)(2,1)S(1)}, u32[]{:S(2)}, u32[]{:S(2)}) collective-permute-start(bf16[128,1536]{1,0:T(8,128)(2,1)} %get-tuple-element.51.refs_2_), channel_id=1, source_target_pairs={{0,2},{1,3},{2,0},{3,1},{4,6},{5,7},{6,4},{7,5},{8,10},{9,11},{10,... | collective-permute-start | bytes 1179656 | tf_op jit(solution)/shard_map/ppermute | solution.py:429
  97.9 17.4 %collective-permute-start.15 = (bf16[256,1536]{1,0:T(8,128)(2,1)}, bf16[256,1536]{1,0:T(8,128)(2,1)S(1)}, u32[]{:S(2)}, u32[]{:S(2)}) collective-permute-start(bf16[256,1536]{1,0:T(8,128)(2,1)} %get-tuple-element.52.refs_3_), channel_id=1, source_target_pairs={{0,1},{1,0},{2,3},{3,2},{4,5},{5,4},{6,7},{7,6},{8,9},{9,8},{10,11... | collective-permute-start | bytes 2359304 | tf_op jit(solution)/shard_map/ppermute | solution.py:429
  98.8 16.6 %collective-permute-start.16 = (bf16[256,1536]{1,0:T(8,128)(2,1)}, bf16[256,1536]{1,0:T(8,128)(2,1)S(1)}, u32[]{:S(2)}, u32[]{:S(2)}) collective-permute-start(bf16[256,1536]{1,0:T(8,128)(2,1)} %get-tuple-element.53.refs_4_), channel_id=1, source_target_pairs={{0,1},{1,0},{2,3},{3,2},{4,5},{5,4},{6,7},{7,6},{8,9},{9,8},{10,11... | collective-permute-start | bytes 2359304 | tf_op jit(solution)/shard_map/ppermute | solution.py:429
  106.3 7.7 %copy-start.3 = (bf16[128,1536]{1,0:T(8,128)(2,1)}, bf16[128,1536]{1,0:T(8,128)(2,1)S(1)}, u32[]{:S(2)}) copy-start(bf16[128,1536]{1,0:T(8,128)(2,1)S(1)} %collective-permute-done.11.refs_1_) | copy-start | bytes 1179652
  106.3 9.0 %collective-permute-start.14 = (bf16[128,1536]{1,0:T(8,128)(2,1)}, bf16[128,1536]{1,0:T(8,128)(2,1)}, u32[]{:S(2)}, u32[]{:S(2)}) collective-permute-start(bf16[128,1536]{1,0:T(8,128)(2,1)} %get-tuple-element.51.refs_2_), channel_id=1, source_target_pairs={{0,1},{1,0},{2,3},{3,2},{4,5},{5,4},{6,7},{7,6},{8,9},{9,8},{10,11... | collective-permute-start | bytes 1179656 | tf_op jit(solution)/shard_map/ppermute | solution.py:429
  114.8 1.9 collective-permute-start.17
  114.8 2.5 %collective-permute-start.18 = (bf16[128,1536]{1,0:T(8,128)(2,1)}, bf16[128,1536]{1,0:T(8,128)(2,1)S(1)}, u32[]{:S(2)}, u32[]{:S(2)}) collective-permute-start(bf16[128,1536]{1,0:T(8,128)(2,1)} %get-tuple-element.60.refs_6_), channel_id=1, source_target_pairs={{0,1},{1,0},{2,3},{3,2},{4,5},{5,4},{6,7},{7,6},{8,9},{9,8},{10,11... | collective-permute-start | bytes 1179656 | tf_op jit(solution)/shard_map/ppermute | solution.py:429
  128.1 27.6 %all-to-all-start.1 = ((bf16[8,128,192]{1,2,0:T(8,128)(2,1)}), bf16[8,128,192]{1,2,0:T(8,128)(2,1)S(1)}, u32[]{:S(2)}, u32[]{:S(2)}) async-start(bf16[8,128,192]{1,2,0:T(8,128)(2,1)} %copy.25), calls=%async_computation.1 | async-start | bytes 786432 | tf_op jit(solution)/shard_map/all_to_all | solution.py:495
  134.9 20.6 %copy-start.9 = (f32[128,1536]{1,0:T(8,128)S(1)}, f32[128,1536]{1,0:T(8,128)}, u32[]{:S(2)}) copy-start(f32[128,1536]{1,0:T(8,128)} %get-tuple-element.73) | copy-start | bytes 2359300
  155.8 25.7 %copy-start.15 = (f32[128,192]{0,1:T(8,128)}, f32[128,192]{0,1:T(8,128)S(1)}, u32[]{:S(2)}) copy-start(f32[128,192]{0,1:T(8,128)S(1)} %convert_reduce_fusion) | copy-start | bytes 294916
  156.0 25.5 %all-to-all-start.2 = ((bf16[16,2,128,128]{3,2,1,0:T(8,128)(2,1)}), bf16[16,2,128,128]{3,2,1,0:T(8,128)(2,1)S(1)}, u32[]{:S(2)}, u32[]{:S(2)}) async-start(bf16[16,2,128,128]{3,2,1,0:T(8,128)(2,1)} %get-tuple-element.71), calls=%async_computation.2 | async-start | bytes 2097152 | tf_op jit(solution)/shard_map/all_to_all | solution.py:498
  181.4 41.1 %copy-start.18 = (f32[128]{0:T(128)S(1)}, f32[128]{0:T(128)}, u32[]{:S(2)}) copy-start(f32[128]{0:T(128)} %param.16) | copy-start | bytes 1540
  181.5 41.6 %all-to-all-start.3 = ((bf16[16,544,128]{2,1,0:T(8,128)(2,1)}), bf16[16,544,128]{2,1,0:T(8,128)(2,1)S(1)}, u32[]{:S(2)}, u32[]{:S(2)}) async-start(bf16[16,544,128]{2,1,0:T(8,128)(2,1)} %backward.3), calls=%async_computation.3 | async-start | bytes 4456448 | tf_op jit(solution)/shard_map/all_to_all | solution.py:510
  187.2 38.6 %copy-start.17 = (f32[192]{0:T(256)S(1)}, f32[192]{0:T(256)}, u32[]{:S(2)}) copy-start(f32[192]{0:T(256)} %param.17) | copy-start | bytes 2308
  187.2 30.2 %collective-permute-start.19 = (f32[128]{0:T(128)S(1)}, f32[128]{0:T(128)S(1)}, u32[]{:S(2)}, u32[]{:S(2)}) collective-permute-start(f32[128]{0:T(128)S(1)} %get-tuple-element.88), channel_id=1, source_target_pairs={{0,16},{16,0},{32,48},{48,32},{64,80},{80,64},{96,112},{112,96},{1... | collective-permute-start | bytes 1544 | tf_op jit(solution)/shard_map/ppermute | solution.py:403
  190.8 26.7 %collective-permute-start.20 = (f32[128]{0:T(128)S(1)}, f32[128]{0:T(128)S(1)}, u32[]{:S(2)}, u32[]{:S(2)}) collective-permute-start(f32[128]{0:T(128)S(1)} %get-tuple-element.88), channel_id=1, source_target_pairs={{0,32},{16,48},{32,0},{48,16},{64,96},{80,112},{96,64},{112,80},{1... | collective-permute-start | bytes 1544 | tf_op jit(solution)/shard_map/ppermute | solution.py:403
  192.3 25.2 %collective-permute-start.21 = (f32[128]{0:T(128)S(1)}, f32[128]{0:T(128)S(1)}, u32[]{:S(2)}, u32[]{:S(2)}) collective-permute-start(f32[128]{0:T(128)S(1)} %get-tuple-element.88), channel_id=1, source_target_pairs={{0,48},{16,32},{32,16},{48,0},{64,112},{80,96},{96,80},{112,64},{1... | collective-permute-start | bytes 1544 | tf_op jit(solution)/shard_map/ppermute | solution.py:403
  217.5 5.1 %collective-permute-start.22 = (f32[128]{0:T(128)S(1)}, f32[128]{0:T(128)S(1)}, u32[]{:S(2)}, u32[]{:S(2)}) collective-permute-start(f32[128]{0:T(128)S(1)} %add_add_fusion), channel_id=1, source_target_pairs={{0,64},{16,80},{32,96},{48,112},{64,0},{80,16},{96,32},{112,48},{1... | collective-permute-start | bytes 1544 | tf_op jit(solution)/shard_map/ppermute | solution.py:403
  (14 other events, 24.7 us)

commit v10 on v9

--- a/solution.py
+++ b/solution.py
@@ -260,9 +260,8 @@
             outer = outer + contract(out, rows, 1, 0)
         a_ref[...] = outer
         if gate is not None:
-            partial = (outer * refs[4 + count + len(earlier)][...]).astype(BF16)
-            for i in range(8):
-                outs[3][i] = partial[:, i * eighth : (i + 1) * eighth]
+            partial = (outer * refs[4 + count + len(earlier)][...]).T.astype(BF16)
+            outs[3][...] = partial.reshape(8, eighth, HEAD_DIM)
 
     out_shape = [
         pltpu.HBM((HEAD_DIM, total), BF16),
@@ -270,7 +269,7 @@
         pltpu.HBM((HEAD_DIM, width), F32),
     ]
     if gate is not None:
-        out_shape.append(pltpu.HBM((8, HEAD_DIM, eighth), BF16))
+        out_shape.append(pltpu.HBM((8, eighth, HEAD_DIM), BF16))
     return pl.pallas_call(
         body,
         in_specs=[pl.BlockSpec(memory_space=pltpu.SMEM)]
@@ -456,7 +455,7 @@
     side, below, above, far_low, far_high, side_below, side_above = after(
         inverse, [side, below, above, far_low, far_high, side_below, side_above]
     )
-    side_low, side_high = move(far_low, y_step=1), move(far_high, y_step=1)
+    side_low, side_high = move(side_below[:half], z_step=1), move(side_above[half:], z_step=3)
     found = [
         (own, 0, 0, 0),
         (side, 0, 1, 0),
@@ -496,7 +495,7 @@
     some_q, early = backward(0, low, grad, delta, query, key, value, seq_size, [])
     some_q, early, partial = lax.optimization_barrier((some_q, early, partial))
     early = lax.all_to_all(early, "seq", 0, 0, tiled=True)
-    grad_weight = jnp.sum(partial.astype(F32), axis=0)
+    grad_weight = jnp.sum(partial.astype(F32), axis=0).T
     squares = grad_weight * grad_weight + EPSILON
     gate_part = jnp.sum(weight * outer, axis=0)
     row_total = total_over(jnp.sum(squares, axis=1), "dp")

time: 227 us -> 222 us (0.978)
  waiting for transfers between devices: 81 us -> 75 us
    ppermute x19, waiting for transfers between devices: 25.8 us -> 19.8 us  [move(): return lax.ppermute(values, 'seq', pairs)]
    unnamed x41 -> x36, local copies, waits for them, and re-layouts: 4.93 us -> 4.25 us
  transfers between devices with their start and end apart: 27 -> 27, of which waited for: 11 -> 11; matrix products, arithmetic and copies ran while one was open for 2% -> 3% of each run, Pallas kernels for 33% -> 34%
where the time goes in v10:
time: 222 us; the launch traced here: 221 us
  Pallas kernels  85.1 us (38%)
  waiting for transfers between devices  75 us (34%)
  starting transfers between devices  47.5 us (21%)
  local copies, waits for them, and re-layouts  10.7 us (5%)
    pallas_call x2, Pallas kernels, backward(): pl.pallas_call(body, grid=(steps,), in_specs=[pl.BlockSpec((some, BLOCK),...  41.7 us
    all_to_all x1, waiting for transfers between devices, shards(): packed = lax.all_to_all(packed, 'seq', 0, 0, tiled=True)  28 us
    ppermute x4, waiting for transfers between devices, swap(): return lax.ppermute(values, axis, [(i, i ^ bit) for i in range(size)])  27.2 us
    pallas_call x1, Pallas kernels, forward(): pl.pallas_call(body, grid_spec=pltpu.PrefetchScalarGridSpec(num_scalar_pr...  21.4 us
    ppermute x19, waiting for transfers between devices, move(): return lax.ppermute(values, 'seq', pairs)  19.8 us
    ppermute x19, starting transfers between devices, move(): return lax.ppermute(values, 'seq', pairs)  17.5 us
    pallas_call x2, Pallas kernels, project(): pl.pallas_call(body, in_specs=[pl.BlockSpec(memory_space=pltpu.SMEM)] + [...  15.4 us
    ppermute x4, starting transfers between devices, swap(): return lax.ppermute(values, axis, [(i, i ^ bit) for i in range(size)])  8.85 us
  transfers between devices with their start and end apart: 27, of which 11 were waited for; matrix products, arithmetic and copies ran while one was open for 3% of the time, Pallas kernels for 34%

profile of v10, /device:TPU:0, one launch (start us, length us, event | category | flops | bytes accessed | tf_op | source)
XLA Modules:
  0.0 221.2 jit_solution(10381035004605560163)
XLA Ops:
  0.6 1.7 collective-permute-start
  2.4 1.9 collective-permute-start.1
  4.3 2.1 collective-permute-start.2
  6.4 4.4 %split_columns.1 = bf16[16,3,256,128]{3,2,1,0:T(8,128)(2,1)} custom-call(bf16[256,2048]{1,0:T(8,128)(2,1)} %bitcast.38, bf16[256,2048]{1,0:T(8,128)(2,1)} %bitcast.39, bf16[256,2048]{1,0:T(8,128)(2,1)} %bitcast.40), custom_call_target="tpu_custom_call" | custom-call | tf_op jit(solution)/shard_map/split_columns/pallas_call | solution.py:36
  10.8 9.3 %collective-permute-done.refs_1_ = bf16[256,1536]{1,0:T(8,128)(2,1)S(1)} collective-permute-done((bf16[256,1536]{1,0:T(8,128)(2,1)}, bf16[256,1536]{1,0:T(8,128)(2,1)S(1)}, u32[]{:S(2)}, u32[]{:S(2)}) %collective-permute-start) | collective-permute-done | bytes 786464 | tf_op jit(solution)/shard_map/ppermute | solution.py:428
  20.1 3.8 %collective-permute-done.1.refs_2_ = bf16[256,1536]{1,0:T(8,128)(2,1)S(1)} collective-permute-done((bf16[256,1536]{1,0:T(8,128)(2,1)}, bf16[256,1536]{1,0:T(8,128)(2,1)S(1)}, u32[]{:S(2)}, u32[]{:S(2)}) %collective-permute-start.1) | collective-permute-done | bytes 786464 | tf_op jit(solution)/shard_map/ppermute | solution.py:428
  25.1 4.0 %all-to-all-start = ((bf16[16,3,256,128]{3,2,1,0:T(8,128)(2,1)}), bf16[16,3,256,128]{3,2,1,0:T(8,128)(2,1)S(1)}, u32[]{:S(2)}, u32[]{:S(2)}) async-start(bf16[16,3,256,128]{3,2,1,0:T(8,128)(2,1)} %split_columns.1), calls=%async_computation | async-start | bytes 6291456 | tf_op jit(solution)/shard_map/all_to_all | solution.py:448
  30.2 1.7 collective-permute-start.5
  31.9 1.6 collective-permute-start.6
  33.5 1.8 slice.19
  35.7 1.8 slice.20
  37.5 2.8 %collective-permute-start.4 = (bf16[128,1536]{1,0:T(8,128)(2,1)}, bf16[128,1536]{1,0:T(8,128)(2,1)}, u32[]{:S(2)}, u32[]{:S(2)}) collective-permute-start(bf16[128,1536]{1,0:T(8,128)(2,1)} %slice.20), channel_id=1, source_target_pairs={{0,12},{1,13},{2,14},{3,15},{4,0},{5,1},{6,2},{7,3},{8,4},{9,5},{1... | collective-permute-start | bytes 1179656 | tf_op jit(solution)/shard_map/ppermute | solution.py:428
  40.3 28.0 %all-to-all-done.p_ref = bf16[16,3,256,128]{3,2,1,0:T(8,128)(2,1)S(1)} async-done(((bf16[16,3,256,128]{3,2,1,0:T(8,128)(2,1)}), bf16[16,3,256,128]{3,2,1,0:T(8,128)(2,1)S(1)}, u32[]{:S(2)}, u32[]{:S(2)}) %all-to-all-start) | async-done | bytes 3145760 | tf_op jit(solution)/shard_map/all_to_all | solution.py:448
  68.3 21.4 %forward.1 = (bf16[4096,4096]{1,0:T(8,128)(2,1)}, bf16[128,4096]{1,0:T(8,128)(2,1)}, bf16[128,4096]{1,0:T(8,128)(2,1)}, f32[8,4096]{1,0:T(8,128)}, bf16[128,4096]{1,0:T(8,128)(2,1)}, /*index=5*/bf16[4096,256]{1,0:T(8,128)(2,1)}) custom-call(s32[1]{0:T(128)S(6)} %copy.37.len_ref, bf16[16,3,256,128]{3,2,1,0:T(8,128)(2,1)S(1)} %all-to-all-done.p_ref), custom_call_target="tpu_custom_call" | custom-call | flops 12884901888 | bytes 33554432 | tf_op jit(solution)/shard_map/forward/pallas_call | solution.py:165
  89.7 2.7 %collective-permute-done.3.refs_4_ = bf16[128,1536]{1,0:T(8,128)(2,1)S(1)} collective-permute-done((bf16[128,1536]{1,0:T(8,128)(2,1)}, bf16[128,1536]{1,0:T(8,128)(2,1)S(1)}, u32[]{:S(2)}, u32[]{:S(2)}) %collective-permute-start.3) | collective-permute-done | bytes 393248 | tf_op jit(solution)/shard_map/ppermute | solution.py:428
  94.0 1.0 slice.21
  95.5 1.0 slice.22
  97.0 3.0 %collective-permute-start.12 = (bf16[128,1536]{1,0:T(8,128)(2,1)S(1)}, bf16[128,1536]{1,0:T(8,128)(2,1)S(1)}, u32[]{:S(2)}, u32[]{:S(2)}) collective-permute-start(bf16[128,1536]{1,0:T(8,128)(2,1)S(1)} %slice.22), channel_id=1, source_target_pairs={{0,12},{1,13},{2,14},{3,15},{4,0},{5,1},{6,2},{7,3},{8,4},{9,5},{1... | collective-permute-start | bytes 1179656 | tf_op jit(solution)/shard_map/ppermute | solution.py:428
  100.1 7.3 %project.2 = (bf16[128,4096]{1,0:T(8,128)(2,1)}, f32[8,4096]{1,0:T(8,128)}, f32[128,1536]{1,0:T(8,128)}) custom-call(s32[8]{0:T(128)S(1)} %stack.87.refs_0_, bf16[256,1536]{1,0:T(8,128)(2,1)} %bitcast.45, bf16[256,1536]{1,0:T(8,128)(2,1)} %get-tuple-element.54.refs_2_, bf16[256,1536]{1,0:T(8,128)(2,1)} %get-tuple-element.55.refs_3_, ...), custom_call_target="tpu_custom_call" | custom-call | flops 1610612736 | bytes 6291456 | tf_op jit(solution)/shard_map/project/pallas_call | solution.py:273
  107.4 1.9 collective-permute-done.11.refs_1_
  113.5 8.0 %project.3 = (bf16[128,4096]{1,0:T(8,128)(2,1)}, f32[8,4096]{1,0:T(8,128)}, f32[128,1536]{1,0:T(8,128)}, bf16[8,192,128]{2,1,0:T(8,128)(2,1)}) custom-call(s32[12]{0:T(128)S(1)} %stack.78.refs_0_, bf16[128,1536]{1,0:T(8,128)(2,1)} %get-tuple-element.50.refs_1_, bf16[128,1536]{1,0:T(8,128)(2,1)} %get-tuple-element.51.refs_2_, ...), custom_call_target="tpu_custom_call" | custom-call | flops 1610612736 | bytes 6291456 | tf_op jit(solution)/shard_map/project/pallas_call | solution.py:273
  121.5 6.8 %all-to-all-start.1 = ((bf16[8,192,128]{2,1,0:T(8,128)(2,1)}), bf16[8,192,128]{2,1,0:T(8,128)(2,1)S(1)}, u32[]{:S(2)}, u32[]{:S(2)}) async-start(bf16[8,192,128]{2,1,0:T(8,128)(2,1)} %get-tuple-element.70), calls=%async_computation.1 | async-start | bytes 786432 | tf_op jit(solution)/shard_map/all_to_all | solution.py:494
  128.4 20.6 %backward.2 = (f32[128,4096]{1,0:T(8,128)}, bf16[16,2,128,128]{3,2,1,0:T(8,128)(2,1)}) custom-call(bf16[4096,4096]{1,0:T(8,128)(2,1)} %get-tuple-element.45.refs_0_, bf16[128,4096]{1,0:T(8,128)(2,1)} %get-tuple-element.63.refs_1_, f32[8,4096]{1,0:T(8,128)} %get-tuple-element.64.refs_2_, bf16[128,4096]{1,0:T(8,128)(2,1)} %get-tuple-element.65.refs_3_, ...), custom_call_target="tpu_custom_call" | custom-call | flops 10737418240 | bytes 16777216 | tf_op jit(solution)/shard_map/backward/pallas_call | solution.py:376
  149.3 4.5 %all-to-all-start.2 = ((bf16[16,2,128,128]{3,2,1,0:T(8,128)(2,1)}), bf16[16,2,128,128]{3,2,1,0:T(8,128)(2,1)S(1)}, u32[]{:S(2)}, u32[]{:S(2)}) async-start(bf16[16,2,128,128]{3,2,1,0:T(8,128)(2,1)} %get-tuple-element.71), calls=%async_computation.2 | async-start | bytes 2097152 | tf_op jit(solution)/shard_map/all_to_all | solution.py:497
  154.5 21.1 %backward.3 = bf16[16,544,128]{2,1,0:T(8,128)(2,1)} custom-call(bf16[4096,4096]{1,0:T(8,128)(2,1)} %get-tuple-element.45.refs_0_, bf16[128,4096]{1,0:T(8,128)(2,1)} %get-tuple-element.63.refs_1_, f32[8,4096]{1,0:T(8,128)} %get-tuple-element.64.refs_2_, bf16[128,4096]{1,0:T(8,128)(2,1)} %get-tuple-element.65.refs_3_, ...), custom_call_target="tpu_custom_call" | custom-call | flops 10737418240 | bytes 16777216 | tf_op jit(solution)/shard_map/backward/pallas_call | solution.py:376
  175.6 5.7 %all-to-all-start.3 = ((bf16[16,544,128]{2,1,0:T(8,128)(2,1)}), bf16[16,544,128]{2,1,0:T(8,128)(2,1)S(1)}, u32[]{:S(2)}, u32[]{:S(2)}) async-start(bf16[16,544,128]{2,1,0:T(8,128)(2,1)} %backward.3), calls=%async_computation.3 | async-start | bytes 4456448 | tf_op jit(solution)/shard_map/all_to_all | solution.py:509
  181.3 4.3 %collective-permute-start.19 = (f32[128]{0:T(128)S(1)}, f32[128]{0:T(128)S(1)}, u32[]{:S(2)}, u32[]{:S(2)}) collective-permute-start(f32[128]{0:T(128)S(1)} %get-tuple-element.81), channel_id=1, source_target_pairs={{0,16},{16,0},{32,48},{48,32},{64,80},{80,64},{96,112},{112,96},{1... | collective-permute-start | bytes 1544 | tf_op jit(solution)/shard_map/ppermute | solution.py:402
  185.6 1.5 collective-permute-start.20
  187.2 25.1 %collective-permute-done.19 = f32[128]{0:T(128)S(1)} collective-permute-done((f32[128]{0:T(128)S(1)}, f32[128]{0:T(128)S(1)}, u32[]{:S(2)}, u32[]{:S(2)}) %collective-permute-start.19) | collective-permute-done | bytes 544 | tf_op jit(solution)/shard_map/ppermute | solution.py:402
  212.3 3.0 %collective-permute-start.22 = (f32[128]{0:T(128)S(1)}, f32[128]{0:T(128)S(1)}, u32[]{:S(2)}, u32[]{:S(2)}) collective-permute-start(f32[128]{0:T(128)S(1)} %add_add_fusion), channel_id=1, source_target_pairs={{0,64},{16,80},{32,96},{48,112},{64,0},{80,16},{96,32},{112,48},{1... | collective-permute-start | bytes 1544 | tf_op jit(solution)/shard_map/ppermute | solution.py:402
  215.3 2.1 collective-permute-done.22
  217.9 2.1 join_columns.1
  (83 shorter events, 11.5 us)
Async XLA Ops:
  0.6 19.5 %collective-permute-start = (bf16[256,1536]{1,0:T(8,128)(2,1)}, bf16[256,1536]{1,0:T(8,128)(2,1)S(1)}, u32[]{:S(2)}, u32[]{:S(2)}) collective-permute-start(bf16[256,1536]{1,0:T(8,128)(2,1)} %bitcast.41), channel_id=1, source_target_pairs={{0,2},{1,3},{2,0},{3,1},{4,6},{5,7},{6,4},{7,5},{8,10},{9,11},{10,... | collective-permute-start | bytes 2359304 | tf_op jit(solution)/shard_map/ppermute | solution.py:428
  2.4 21.5 %collective-permute-start.1 = (bf16[256,1536]{1,0:T(8,128)(2,1)}, bf16[256,1536]{1,0:T(8,128)(2,1)S(1)}, u32[]{:S(2)}, u32[]{:S(2)}) collective-permute-start(bf16[256,1536]{1,0:T(8,128)(2,1)} %bitcast.42), channel_id=1, source_target_pairs={{0,4},{1,5},{2,6},{3,7},{4,8},{5,9},{6,10},{7,11},{8,12},{9,13},{1... | collective-permute-start | bytes 2359304 | tf_op jit(solution)/shard_map/ppermute | solution.py:428
  4.3 19.6 %collective-permute-start.2 = (bf16[256,1536]{1,0:T(8,128)(2,1)}, bf16[256,1536]{1,0:T(8,128)(2,1)S(1)}, u32[]{:S(2)}, u32[]{:S(2)}) collective-permute-start(bf16[256,1536]{1,0:T(8,128)(2,1)} %bitcast.43), channel_id=1, source_target_pairs={{0,12},{1,13},{2,14},{3,15},{4,0},{5,1},{6,2},{7,3},{8,4},{9,5},{1... | collective-permute-start | bytes 2359304 | tf_op jit(solution)/shard_map/ppermute | solution.py:428
  25.1 43.2 %all-to-all-start = ((bf16[16,3,256,128]{3,2,1,0:T(8,128)(2,1)}), bf16[16,3,256,128]{3,2,1,0:T(8,128)(2,1)S(1)}, u32[]{:S(2)}, u32[]{:S(2)}) async-start(bf16[16,3,256,128]{3,2,1,0:T(8,128)(2,1)} %split_columns.1), calls=%async_computation | async-start | bytes 6291456 | tf_op jit(solution)/shard_map/all_to_all | solution.py:448
  29.1 67.4 %collective-permute-start.7 = (bf16[256,1536]{1,0:T(8,128)(2,1)}, bf16[256,1536]{1,0:T(8,128)(2,1)}, u32[]{:S(2)}, u32[]{:S(2)}) collective-permute-start(bf16[256,1536]{1,0:T(8,128)(2,1)} %bitcast.44), channel_id=1, source_target_pairs={{0,1},{1,0},{2,3},{3,2},{4,5},{5,4},{6,7},{7,6},{8,9},{9,8},{10,11... | collective-permute-start | bytes 2359304 | tf_op jit(solution)/shard_map/ppermute | solution.py:428
  30.2 62.3 %collective-permute-start.5 = (bf16[256,1536]{1,0:T(8,128)(2,1)}, bf16[256,1536]{1,0:T(8,128)(2,1)}, u32[]{:S(2)}, u32[]{:S(2)}) collective-permute-start(bf16[256,1536]{1,0:T(8,128)(2,1)} %copy-done.2), channel_id=1, source_target_pairs={{0,4},{1,5},{2,6},{3,7},{4,8},{5,9},{6,10},{7,11},{8,12},{9,13},{1... | collective-permute-start | bytes 2359304 | tf_op jit(solution)/shard_map/ppermute | solution.py:428
  31.9 60.5 %collective-permute-start.6 = (bf16[256,1536]{1,0:T(8,128)(2,1)}, bf16[256,1536]{1,0:T(8,128)(2,1)}, u32[]{:S(2)}, u32[]{:S(2)}) collective-permute-start(bf16[256,1536]{1,0:T(8,128)(2,1)} %copy-done.2), channel_id=1, source_target_pairs={{0,12},{1,13},{2,14},{3,15},{4,0},{5,1},{6,2},{7,3},{8,4},{9,5},{1... | collective-permute-start | bytes 2359304 | tf_op jit(solution)/shard_map/ppermute | solution.py:428
  35.3 57.2 %collective-permute-start.3 = (bf16[128,1536]{1,0:T(8,128)(2,1)}, bf16[128,1536]{1,0:T(8,128)(2,1)S(1)}, u32[]{:S(2)}, u32[]{:S(2)}) collective-permute-start(bf16[128,1536]{1,0:T(8,128)(2,1)} %slice.19), channel_id=1, source_target_pairs={{0,4},{1,5},{2,6},{3,7},{4,8},{5,9},{6,10},{7,11},{8,12},{9,13},{1... | collective-permute-start | bytes 1179656 | tf_op jit(solution)/shard_map/ppermute | solution.py:428
  37.5 54.9 %collective-permute-start.4 = (bf16[128,1536]{1,0:T(8,128)(2,1)}, bf16[128,1536]{1,0:T(8,128)(2,1)}, u32[]{:S(2)}, u32[]{:S(2)}) collective-permute-start(bf16[128,1536]{1,0:T(8,128)(2,1)} %slice.20), channel_id=1, source_target_pairs={{0,12},{1,13},{2,14},{3,15},{4,0},{5,1},{6,2},{7,3},{8,4},{9,5},{1... | collective-permute-start | bytes 1179656 | tf_op jit(solution)/shard_map/ppermute | solution.py:428
  93.2 6.8 %copy-start.6 = (bf16[128,1536]{1,0:T(8,128)(2,1)S(1)}, bf16[128,1536]{1,0:T(8,128)(2,1)}, u32[]{:S(2)}) copy-start(bf16[128,1536]{1,0:T(8,128)(2,1)} %param.15) | copy-start | bytes 1179652
  93.2 3.5 %collective-permute-start.10 = (bf16[256,1536]{1,0:T(8,128)(2,1)}, bf16[256,1536]{1,0:T(8,128)(2,1)}, u32[]{:S(2)}, u32[]{:S(2)}) collective-permute-start(bf16[256,1536]{1,0:T(8,128)(2,1)} %get-tuple-element.56.refs_4_), channel_id=1, source_target_pairs={{0,1},{1,0},{2,3},{3,2},{4,5},{5,4},{6,7},{7,6},{8,9},{9,8},{10,11... | collective-permute-start | bytes 2359304 | tf_op jit(solution)/shard_map/ppermute | solution.py:428
  93.2 3.7 %collective-permute-start.8 = (bf16[256,1536]{1,0:T(8,128)(2,1)}, bf16[256,1536]{1,0:T(8,128)(2,1)}, u32[]{:S(2)}, u32[]{:S(2)}) collective-permute-start(bf16[256,1536]{1,0:T(8,128)(2,1)} %get-tuple-element.54.refs_2_), channel_id=1, source_target_pairs={{0,1},{1,0},{2,3},{3,2},{4,5},{5,4},{6,7},{7,6},{8,9},{9,8},{10,11... | collective-permute-start | bytes 2359304 | tf_op jit(solution)/shard_map/ppermute | solution.py:428
  93.7 6.3 %collective-permute-start.9 = (bf16[256,1536]{1,0:T(8,128)(2,1)}, bf16[256,1536]{1,0:T(8,128)(2,1)}, u32[]{:S(2)}, u32[]{:S(2)}) collective-permute-start(bf16[256,1536]{1,0:T(8,128)(2,1)} %get-tuple-element.55.refs_3_), channel_id=1, source_target_pairs={{0,1},{1,0},{2,3},{3,2},{4,5},{5,4},{6,7},{7,6},{8,9},{9,8},{10,11... | collective-permute-start | bytes 2359304 | tf_op jit(solution)/shard_map/ppermute | solution.py:428
  95.1 16.3 %collective-permute-start.15 = (bf16[256,1536]{1,0:T(8,128)(2,1)}, bf16[256,1536]{1,0:T(8,128)(2,1)S(1)}, u32[]{:S(2)}, u32[]{:S(2)}) collective-permute-start(bf16[256,1536]{1,0:T(8,128)(2,1)} %get-tuple-element.52.refs_3_), channel_id=1, source_target_pairs={{0,1},{1,0},{2,3},{3,2},{4,5},{5,4},{6,7},{7,6},{8,9},{9,8},{10,11... | collective-permute-start | bytes 2359304 | tf_op jit(solution)/shard_map/ppermute | solution.py:428
  96.5 14.9 %collective-permute-start.16 = (bf16[256,1536]{1,0:T(8,128)(2,1)}, bf16[256,1536]{1,0:T(8,128)(2,1)S(1)}, u32[]{:S(2)}, u32[]{:S(2)}) collective-permute-start(bf16[256,1536]{1,0:T(8,128)(2,1)} %get-tuple-element.53.refs_4_), channel_id=1, source_target_pairs={{0,1},{1,0},{2,3},{3,2},{4,5},{5,4},{6,7},{7,6},{8,9},{9,8},{10,11... | collective-permute-start | bytes 2359304 | tf_op jit(solution)/shard_map/ppermute | solution.py:428
  96.8 12.6 %collective-permute-start.11 = (bf16[128,1536]{1,0:T(8,128)(2,1)S(1)}, bf16[128,1536]{1,0:T(8,128)(2,1)S(1)}, u32[]{:S(2)}, u32[]{:S(2)}) collective-permute-start(bf16[128,1536]{1,0:T(8,128)(2,1)S(1)} %slice.21), channel_id=1, source_target_pairs={{0,4},{1,5},{2,6},{3,7},{4,8},{5,9},{6,10},{7,11},{8,12},{9,13},{1... | collective-permute-start | bytes 1179656 | tf_op jit(solution)/shard_map/ppermute | solution.py:428
  97.0 12.4 %collective-permute-start.12 = (bf16[128,1536]{1,0:T(8,128)(2,1)S(1)}, bf16[128,1536]{1,0:T(8,128)(2,1)S(1)}, u32[]{:S(2)}, u32[]{:S(2)}) collective-permute-start(bf16[128,1536]{1,0:T(8,128)(2,1)S(1)} %slice.22), channel_id=1, source_target_pairs={{0,12},{1,13},{2,14},{3,15},{4,0},{5,1},{6,2},{7,3},{8,4},{9,5},{1... | collective-permute-start | bytes 1179656 | tf_op jit(solution)/shard_map/ppermute | solution.py:428
  100.0 10.6 %collective-permute-start.13 = (bf16[128,1536]{1,0:T(8,128)(2,1)}, bf16[128,1536]{1,0:T(8,128)(2,1)S(1)}, u32[]{:S(2)}, u32[]{:S(2)}) collective-permute-start(bf16[128,1536]{1,0:T(8,128)(2,1)} %get-tuple-element.50.refs_1_), channel_id=1, source_target_pairs={{0,1},{1,0},{2,3},{3,2},{4,5},{5,4},{6,7},{7,6},{8,9},{9,8},{10,11... | collective-permute-start | bytes 1179656 | tf_op jit(solution)/shard_map/ppermute | solution.py:428
  109.3 2.1 collective-permute-start.14
  110.2 2.0 collective-permute-start.17
  110.6 2.1 collective-permute-start.18
  121.5 27.6 %all-to-all-start.1 = ((bf16[8,192,128]{2,1,0:T(8,128)(2,1)}), bf16[8,192,128]{2,1,0:T(8,128)(2,1)S(1)}, u32[]{:S(2)}, u32[]{:S(2)}) async-start(bf16[8,192,128]{2,1,0:T(8,128)(2,1)} %get-tuple-element.70), calls=%async_computation.1 | async-start | bytes 786432 | tf_op jit(solution)/shard_map/all_to_all | solution.py:494
  128.3 20.6 %copy-start.9 = (f32[128,1536]{1,0:T(8,128)S(1)}, f32[128,1536]{1,0:T(8,128)}, u32[]{:S(2)}) copy-start(f32[128,1536]{1,0:T(8,128)} %get-tuple-element.73) | copy-start | bytes 2359300
  149.2 26.4 %copy-start.13 = (f32[192,128]{1,0:T(8,128)}, f32[192,128]{1,0:T(8,128)S(1)}, u32[]{:S(2)}) copy-start(f32[192,128]{1,0:T(8,128)S(1)} %convert_reduce_fusion) | copy-start | bytes 294916
  149.3 26.3 %all-to-all-start.2 = ((bf16[16,2,128,128]{3,2,1,0:T(8,128)(2,1)}), bf16[16,2,128,128]{3,2,1,0:T(8,128)(2,1)S(1)}, u32[]{:S(2)}, u32[]{:S(2)}) async-start(bf16[16,2,128,128]{3,2,1,0:T(8,128)(2,1)} %get-tuple-element.71), calls=%async_computation.2 | async-start | bytes 2097152 | tf_op jit(solution)/shard_map/all_to_all | solution.py:497
  175.6 41.8 %copy-start.16 = (f32[128]{0:T(128)S(1)}, f32[128]{0:T(128)}, u32[]{:S(2)}) copy-start(f32[128]{0:T(128)} %param.16) | copy-start | bytes 1540
  175.6 42.3 %all-to-all-start.3 = ((bf16[16,544,128]{2,1,0:T(8,128)(2,1)}), bf16[16,544,128]{2,1,0:T(8,128)(2,1)S(1)}, u32[]{:S(2)}, u32[]{:S(2)}) async-start(bf16[16,544,128]{2,1,0:T(8,128)(2,1)} %backward.3), calls=%async_computation.3 | async-start | bytes 4456448 | tf_op jit(solution)/shard_map/all_to_all | solution.py:509
  181.3 39.3 %copy-start.15 = (f32[192]{0:T(256)S(1)}, f32[192]{0:T(256)}, u32[]{:S(2)}) copy-start(f32[192]{0:T(256)} %param.17) | copy-start | bytes 2308
  181.3 30.9 %collective-permute-start.19 = (f32[128]{0:T(128)S(1)}, f32[128]{0:T(128)S(1)}, u32[]{:S(2)}, u32[]{:S(2)}) collective-permute-start(f32[128]{0:T(128)S(1)} %get-tuple-element.81), channel_id=1, source_target_pairs={{0,16},{16,0},{32,48},{48,32},{64,80},{80,64},{96,112},{112,96},{1... | collective-permute-start | bytes 1544 | tf_op jit(solution)/shard_map/ppermute | solution.py:402
  185.6 26.7 %collective-permute-start.20 = (f32[128]{0:T(128)S(1)}, f32[128]{0:T(128)S(1)}, u32[]{:S(2)}, u32[]{:S(2)}) collective-permute-start(f32[128]{0:T(128)S(1)} %get-tuple-element.81), channel_id=1, source_target_pairs={{0,32},{16,48},{32,0},{48,16},{64,96},{80,112},{96,64},{112,80},{1... | collective-permute-start | bytes 1544 | tf_op jit(solution)/shard_map/ppermute | solution.py:402
  187.1 25.2 %collective-permute-start.21 = (f32[128]{0:T(128)S(1)}, f32[128]{0:T(128)S(1)}, u32[]{:S(2)}, u32[]{:S(2)}) collective-permute-start(f32[128]{0:T(128)S(1)} %get-tuple-element.81), channel_id=1, source_target_pairs={{0,48},{16,32},{32,16},{48,0},{64,112},{80,96},{96,80},{112,64},{1... | collective-permute-start | bytes 1544 | tf_op jit(solution)/shard_map/ppermute | solution.py:402
  212.3 5.1 %collective-permute-start.22 = (f32[128]{0:T(128)S(1)}, f32[128]{0:T(128)S(1)}, u32[]{:S(2)}, u32[]{:S(2)}) collective-permute-start(f32[128]{0:T(128)S(1)} %add_add_fusion), channel_id=1, source_target_pairs={{0,64},{16,80},{32,96},{48,112},{64,0},{80,16},{96,32},{112,48},{1... | collective-permute-start | bytes 1544 | tf_op jit(solution)/shard_map/ppermute | solution.py:402
  (12 other events, 15.2 us)
